TPU v7x, 32 devices: a whole 2x2x4 slice. The times are simulated.
32 devices in a mesh: case: 2 (over x), slab: 16 (over z, y, core).
Axes of the slice: x: 2, y: 2, z: 4, core: 2. Of those that a mesh axis runs over, the one named last changes fastest.
Arguments:
- density: float32 [64, 256, 256], P('slab', 'case'), may hold values from 0.2 to 1
- support: int32 [64, 256, 256], P('slab'), may hold values 0 or 1
- loads: int32 [4, 64, 256, 256], P('case', 'slab'), may hold values from 0 to 7
- load_table: float32 [8, 3], replicated, may hold values from -4 to 4
Outputs:
- displacement: float32 [4, 3, 64, 256, 256], P('case', None, 'slab')
- filtered: float32 [64, 256, 256], P('slab', 'case')
All inputs are finite; a program needn't handle non-finite values. No bound on the sum of `support` on one device may be relied on, other than what follows from the above.
Results may differ from a plain program's by a relative error of at most 0.0001.
Values sent between devices are 32-bit elements; how exact they have to be, the bound alone decides.
No kernel may reach another device: no remote copies, remote signals or barrier semaphores. Data moves between devices by JAX's collectives and lax.ppermute only.
A program may use at most 128 MiB of HBM per device.

v0:
```python
import jax
import jax.numpy as jnp
from jax import lax
from jax.sharding import PartitionSpec as P

ITERS = 3
FSWEEPS = 4


E_MIN = 0.001
PENALTY = 3.0
SPRING = 4.0
LOWER = 0.05
UPPER = 2.0
RADIUS_SQ = 2.0


def with_halo(cells, sides, width):
    for axis, dim in sides:
        count = lax.axis_size(axis)
        ends = count - 1
        head = lax.slice_in_dim(cells, 0, width, axis=dim)
        tail = lax.slice_in_dim(cells, cells.shape[dim] - width, cells.shape[dim], axis=dim)
        cells = jnp.concatenate(
            [
                lax.ppermute(tail, axis, [(i, (i + 1) % count) for i in range(ends)]),
                cells,
                lax.ppermute(head, axis, [((i + 1) % count, i) for i in range(ends)]),
            ],
            axis=dim,
        )
    return cells


def beside_cells(extended):
    middle = extended[..., 1:-1, :, :]
    widths = [(0, 0)] * (middle.ndim - 2) + [(1, 1), (1, 1)]
    padded = jnp.pad(middle, widths)
    return (
        middle,
        [
            extended[..., 2:, :, :],
            extended[..., :-2, :, :],
            padded[..., 2:, 1:-1],
            padded[..., :-2, 1:-1],
            padded[..., 1:-1, 2:],
            padded[..., 1:-1, :-2],
        ],
    )


def forces(index, table):
    parts = []
    for component in range(3):
        total = jnp.zeros(index.shape, jnp.float32)
        for entry in range(table.shape[0]):
            total = total + jnp.where(index == entry, table[entry, component], jnp.float32(0.0))
        parts.append(total)
    return jnp.stack(parts, axis=-4)


def face_stiffness(modulus_ext):
    middle, beside = beside_cells(modulus_ext)
    return [(middle + other) * 0.5 for other in beside]


def operate(stiffness, diagonal, extended):
    middle, beside = beside_cells(extended)
    total = diagonal * middle
    for weight, other in zip(stiffness, beside):
        total = total - weight * other
    return total


def plane_rim(field):
    shape = field.shape
    flat = field.reshape((-1,) + shape[-3:])
    grown = with_halo(flat, (("slab", 1),), 1)
    return grown.reshape(shape[:-3] + (shape[-3] + 2,) + shape[-2:])


def local(density, support, loads, load_table):
    planes = density.shape[0]
    whole = lax.all_gather(density, "case", axis=1, tiled=True)
    modulus = E_MIN + whole**3 * (1.0 - E_MIN)
    spring = SPRING * support.astype(jnp.float32)
    rows_y = whole.shape[1]
    rows_z = whole.shape[2]
    centre = (UPPER + LOWER) / 2.0
    half = (UPPER - LOWER) / 2.0
    sigma = centre / half
    force = forces(loads, load_table)
    stiffness = face_stiffness(plane_rim(modulus[None])[0])
    diagonal = sum(stiffness) + spring
    residual = force
    search = residual / diagonal / centre
    iterate = search
    factor_old = 1.0 / sigma
    for sweep in range(1, ITERS):
        residual = residual - operate(stiffness, diagonal, plane_rim(search))
        factor_new = 1.0 / (2.0 * sigma - factor_old)
        search = factor_new * factor_old * search + 2.0 * factor_new / half * residual / diagonal
        iterate = iterate + search
        factor_old = factor_new
    framed = plane_rim(iterate)
    middle, beside = beside_cells(framed)
    energy = jnp.zeros((planes, rows_y, rows_z), jnp.float32)
    for other in beside:
        energy = energy + 0.5 * jnp.sum((middle - other) ** 2, axis=(0, 1))
    owned = lax.psum_scatter(energy, "case", scatter_dimension=1, tiled=True)
    sensitivity = -PENALTY * density**2 * (1.0 - E_MIN) * owned
    right = density * sensitivity
    smooth = right
    for sweep in range(FSWEEPS):
        grown_field = with_halo(smooth, (("case", 1), ("slab", 0)), 1)
        core = grown_field[1:-1, 1:-1]
        padded = jnp.pad(core, ((0, 0), (0, 0), (1, 1)))
        total = (
            grown_field[2:, 1:-1]
            + grown_field[:-2, 1:-1]
            + grown_field[1:-1, 2:]
            + grown_field[1:-1, :-2]
            + padded[..., 2:]
            + padded[..., :-2]
        )
        smooth = (right + RADIUS_SQ * total) / (1.0 + 6.0 * RADIUS_SQ)
    return (iterate, smooth / density)


def solution(mesh):
    return jax.shard_map(
        local,
        mesh=mesh,
        in_specs=(
            P("slab", "case", None),
            P("slab", None, None),
            P("case", "slab", None, None),
            P(),
        ),
        out_specs=(P("case", None, "slab", None, None), P("slab", "case", None)),
        check_vma=False,
    )
```

profile of v0, /device:TPU:9, one launch (start us, length us, event | category | flops | bytes accessed | tf_op | source)
XLA Modules:
  0.0 348.0 jit_solution(16939315175215335587)
XLA Ops:
  7.2 0.7 all-gather.2.cloned.1.call-update
  7.9 1.5 fusion.113
  9.5 2.1 fusion.112
  11.5 9.7 %add_bitcast_fusion.2 = (f32[2,1,4,256,256]{4,3,2,1,0:T(8,128)S(1)}, pred[2,4,256,256]{3,2,1,0:T(8,128)(4,1)S(1)}, pred[2,4,256,256]{3,2,1,0:T(8,128)(4,1)S(1)},...) fusion(f32[]{:T(128)} %bitcast.7, f32[]{:T(128)} %bitcast.6, ...), kind=kLoop, calls=%fused_computation.78 | loop fusion | flops 12058624 | bytes 8388640 | tf_op jit(solution)/shard_map/stack | solution.py:59
  21.3 0.7 copy-done.6
  22.9 8.4 %add_bitcast_fusion.1 = f32[2,1,4,256,256]{4,3,2,1,0:T(8,128)} fusion(pred[2,4,256,256]{3,2,1,0:T(8,128)(4,1)S(1)} %get-tuple-element.26, pred[2,4,256,256]{3,2,1,0:T(8,128)(4,1)S(1)} %get-tuple-element.25, pred[2,4,256,256]{3,2,1,0:T(8,128)(4,1)S(1)} %get-tuple-element.24, pred[2,4,256,256]{3,2,1,0:T(8,128)(4,1)S(1)} %get-tuple-element.23, ...), kind=kLoop, calls=%fused_computation.77 | loop fusion | flops 7864320 | bytes 6291488 | tf_op jit(solution)/shard_map/stack | solution.py:59
  31.3 0.7 all-gather.2.cloned.1.call-done
  32.0 1.6 fusion.50
  33.6 2.6 collective-permute-start
  36.2 3.0 collective-permute-start.1
  39.2 8.9 %add_bitcast_fusion = f32[2,1,4,256,256]{4,3,2,1,0:T(8,128)S(1)} fusion(pred[2,4,256,256]{3,2,1,0:T(8,128)(4,1)} %copy-done.11, pred[2,4,256,256]{3,2,1,0:T(8,128)(4,1)} %copy-done.10, pred[2,4,256,256]{3,2,1,0:T(8,128)(4,1)} %copy-done.9, pred[2,4,256,256]{3,2,1,0:T(8,128)(4,1)} %copy-done.8, pred[2,4,256,256]{3,2,1,0:T(8,128)(4,1)} %copy-done.7, ...), kind=kLoop, calls=%fused_computation.76 | loop fusion | flops 7864320 | bytes 6291488 | tf_op jit(solution)/shard_map/stack | solution.py:59
  48.2 4.0 %broadcast_multiply_fusion.1 = (f32[4,256,256]{2,1,0:T(8,128)}, f32[4,256,256]{2,1,0:T(8,128)S(1)}, f32[4,256,256]{2,1,0:T(8,128)}, f32[4,256,256]{2,1,0:T(8,128...) fusion(s32[4,256,256]{2,1,0:T(8,128)S(1)} %copy-done.17, ...), kind=kLoop, calls=%fused_computation.186 | loop fusion | flops 7077888 | bytes 13107200 | tf_op jit(solution)/shard_map/mul | solution.py:69
  52.2 3.3 pad_maximum_fusion.6
  55.5 1.2 fusion.48
  57.0 1.9 collective-permute-start.2
  58.9 3.8 %collective-permute-start.3 = (f32[6,1,256,256]{3,2,1,0:T(8,128)S(1)}, f32[6,1,256,256]{3,2,1,0:T(8,128)S(1)}, u32[]{:S(2)}, u32[]{:S(2)}) collective-permute-start(f32[6,1,256,256]{3,2,1,0:T(8,128)S(1)} %get-tuple-element.32), channel_id=1, source_target_pairs={{0,1},{1,2},{2,3},{3,4},{4,5},{5,6},{6,7},{7,8},{8,9},{9,10},{10,1... | collective-permute-start | bytes 4718600 | tf_op jit(solution)/shard_map/ppermute | solution.py:26
  62.7 32.8 %collective-permute-done.2 = f32[6,1,256,256]{3,2,1,0:T(8,128)S(1)} collective-permute-done((f32[6,1,256,256]{3,2,1,0:T(8,128)S(1)}, f32[6,1,256,256]{3,2,1,0:T(8,128)S(1)}, u32[]{:S(2)}, u32[]{:S(2)}) %collective-permute-start.2) | collective-permute-done | bytes 1572896 | tf_op jit(solution)/shard_map/ppermute | solution.py:28
  95.6 1.1 collective-permute-done.3
  96.8 1.0 copy-done.14
  97.8 24.2 %divide_add_fusion = (f32[2,3,4,256,256]{4,3,2,1,0:T(8,128)S(1)}, f32[2,3,4,256,256]{4,3,2,1,0:T(8,128)}) fusion(f32[4,256,256]{2,1,0:T(8,128)} %copy-done.4, f32[2,1,4,256,256]{4,3,2,1,0:T(8,128)} %copy-done.3, f32[2,1,4,256,256]{4,3,2,1,0:T(8,128)} %add_bitcast_fusion.1, f32[2,1,4,256,256]{4,3,2,1,0:T(8,128)} %copy-done.1, ...), kind=kLoop, calls=%fused_computation.69 | loop fusion | flops 36175872 | bytes 36700160 | tf_op jit(solution)/shard_map/add | solution.py:102
  122.0 2.7 copy-done
  125.0 1.9 collective-permute-start.4
  127.0 4.4 %collective-permute-start.5 = (f32[6,1,256,256]{3,2,0,1:T(8,128)S(1)}, f32[6,1,256,256]{3,2,0,1:T(8,128)S(1)}, u32[]{:S(2)}, u32[]{:S(2)}) collective-permute-start(f32[6,1,256,256]{3,2,0,1:T(8,128)S(1)} %get-tuple-element.30), channel_id=1, source_target_pairs={{0,1},{1,2},{2,3},{3,4},{4,5},{5,6},{6,7},{7,8},{8,9},{9,10},{10,1... | collective-permute-start | bytes 4718600 | tf_op jit(solution)/shard_map/ppermute | solution.py:26
  131.4 33.0 %collective-permute-done.4 = f32[6,1,256,256]{3,2,0,1:T(8,128)S(1)} collective-permute-done((f32[6,1,256,256]{3,2,0,1:T(8,128)S(1)}, f32[6,1,256,256]{3,2,0,1:T(8,128)S(1)}, u32[]{:S(2)}, u32[]{:S(2)}) %collective-permute-start.4) | collective-permute-done | bytes 1572896 | tf_op jit(solution)/shard_map/ppermute | solution.py:28
  164.4 25.5 %fusion.18 = f32[2,3,4,256,256]{4,3,2,1,0:T(8,128)} fusion(f32[2,3,4,256,256]{4,3,2,1,0:T(8,128)} %get-tuple-element.9, f32[2,3,4,256,256]{4,3,2,1,0:T(8,128)} %copy-done, f32[2,3,1,256,256]{4,3,2,1,0:T(8,128)S(1)} %bitcast.73, f32[2,3,1,256,256]{4,3,2,1,0:T(8,128)S(1)} %bitcast.72, f32[4,256,256]{2,1,0:T(8,128)} %get-tuple-element.17, ...), kind=kLoop, calls=%fused_computation.30 | loop fusion | flops 40894464 | bytes 35651584 | tf_op jit(solution)/shard_map/add | solution.py:103
  189.9 2.3 slice_bitcast_fusion.1
  192.1 1.9 collective-permute-start.6
  194.1 3.6 %collective-permute-start.7 = (f32[6,1,256,256]{3,2,0,1:T(8,128)S(1)}, f32[6,1,256,256]{3,2,0,1:T(8,128)S(1)}, u32[]{:S(2)}, u32[]{:S(2)}) collective-permute-start(f32[6,1,256,256]{3,2,0,1:T(8,128)S(1)} %get-tuple-element.28), channel_id=1, source_target_pairs={{0,1},{1,2},{2,3},{3,4},{4,5},{5,6},{6,7},{7,8},{8,9},{9,10},{10,1... | collective-permute-start | bytes 4718600 | tf_op jit(solution)/shard_map/ppermute | solution.py:26
  197.7 20.8 %collective-permute-done.6 = f32[6,1,256,256]{3,2,0,1:T(8,128)S(1)} collective-permute-done((f32[6,1,256,256]{3,2,0,1:T(8,128)S(1)}, f32[6,1,256,256]{3,2,0,1:T(8,128)S(1)}, u32[]{:S(2)}, u32[]{:S(2)}) %collective-permute-start.6) | collective-permute-done | bytes 1572896 | tf_op jit(solution)/shard_map/ppermute | solution.py:28
  218.5 1.2 copy-done.15
  219.7 0.5 copy-done.16
  220.2 19.9 %fusion.36 = (f32[4,256,256]{2,1,0:T(8,128)S(1)}, f32[4,256,256]{2,1,0:T(8,128)S(1)}, f32[4,256,256]{2,1,0:T(8,128)}, f32[4,256,256]{2,1,0:T(8,128)}, f32[4,256,256]{2,1,0:T(8,128)}, /*index=5*/f32[4,256,256]{2,1,0:T(8,128)}) fusion(f32[2,3,4,256,256]{4,3,2,1,0:T(8,128)} %fusion.18, f32[2,3,1,256,256]{4,3,2,1,0:T(8,128)} %bitcast.77, ...), kind=kLoop, calls=%fused_computation.49 | loop fusion | flops 29884416 | bytes 15728640 | tf_op jit(solution)/shard_map/reduce_sum | solution.py:109
  240.0 3.6 %add_multiply_fusion = f32[4,256,256]{2,1,0:T(8,128)} fusion(f32[4,256,256]{2,1,0:T(8,128)} %get-tuple-element.7, f32[4,256,256]{2,1,0:T(8,128)} %get-tuple-element.5, f32[4,256,256]{2,1,0:T(8,128)S(1)} %get-tuple-element.3, f32[4,256,256]{2,1,0:T(8,128)} %get-tuple-element.4, f32[4,256,256]{2,1,0:T(8,128)} %get-tuple-element.6, ...), kind=kLoop, calls=%fused_computation.102 | loop fusion | flops 1572864 | bytes 7340032 | tf_op jit(solution)/shard_map/add | solution.py:109
  243.7 30.4 %reduce-scatter.2.cloned.1.call-done = f32[4,128,256]{2,1,0:T(8,128)} async-done(((f32[4,256,256]{2,1,0:T(8,128)}), f32[4,128,256]{2,1,0:T(8,128)}) %reduce-scatter.2.cloned.1.call-update) | async-done | bytes 524304 | tf_op jit(solution)/shard_map/reduce_scatter | solution.py:110
  274.1 1.1 multiply_multiply_fusion.1
  275.3 1.3 collective-permute-start.9
  276.6 4.0 %collective-permute-start.8 = (f32[4,1,256]{2,1,0:T(1,128)S(1)}, f32[4,1,256]{2,1,0:T(1,128)S(1)}, u32[]{:S(2)}, u32[]{:S(2)}) collective-permute-start(f32[4,1,256]{2,1,0:T(1,128)S(1)} %get-tuple-element.54), channel_id=1, source_target_pairs={{0,16},{1,17},{2,18},{3,19},{4,20},{5,21},{6,22},{7,23},{8,24},{9,... | collective-permute-start | bytes 12296 | tf_op jit(solution)/shard_map/ppermute | solution.py:26
  280.6 0.7 collective-permute-done.8
  281.3 3.7 %collective-permute-start.10 = (f32[1,130,256]{2,1,0:T(8,128)S(1)}, f32[1,130,256]{2,1,0:T(8,128)S(1)}, u32[]{:S(2)}, u32[]{:S(2)}) collective-permute-start(f32[1,130,256]{2,1,0:T(8,128)S(1)} %get-tuple-element.45), channel_id=1, source_target_pairs={{1,0},{2,1},{3,2},{4,3},{5,4},{6,5},{7,6},{8,7},{9,8},{10,9},{11,1... | collective-permute-start | bytes 399368 | tf_op jit(solution)/shard_map/ppermute | solution.py:28
  285.0 3.0 collective-permute-start.11
  288.0 0.8 collective-permute-done.10
  288.8 1.2 collective-permute-done.11
  290.4 1.3 collective-permute-start.13
  291.7 4.0 %collective-permute-start.12 = (f32[4,1,256]{2,1,0:T(1,128)S(1)}, f32[4,1,256]{2,1,0:T(1,128)S(1)}, u32[]{:S(2)}, u32[]{:S(2)}) collective-permute-start(f32[4,1,256]{2,1,0:T(1,128)S(1)} %get-tuple-element.52), channel_id=1, source_target_pairs={{0,16},{1,17},{2,18},{3,19},{4,20},{5,21},{6,22},{7,23},{8,24},{9,... | collective-permute-start | bytes 12296 | tf_op jit(solution)/shard_map/ppermute | solution.py:26
  295.7 0.7 collective-permute-done.12
  296.5 5.3 %collective-permute-start.14 = (f32[1,130,256]{2,1,0:T(8,128)S(1)}, f32[1,130,256]{2,1,0:T(8,128)S(1)}, u32[]{:S(2)}, u32[]{:S(2)}) collective-permute-start(f32[1,130,256]{2,1,0:T(8,128)S(1)} %get-tuple-element.43), channel_id=1, source_target_pairs={{1,0},{2,1},{3,2},{4,3},{5,4},{6,5},{7,6},{8,7},{9,8},{10,9},{11,1... | collective-permute-start | bytes 399368 | tf_op jit(solution)/shard_map/ppermute | solution.py:28
  301.8 2.1 collective-permute-start.15
  303.9 0.8 collective-permute-done.14
  304.7 1.7 collective-permute-done.15
  306.8 1.3 collective-permute-start.17
  308.1 4.0 %collective-permute-start.16 = (f32[4,1,256]{2,1,0:T(1,128)S(1)}, f32[4,1,256]{2,1,0:T(1,128)S(1)}, u32[]{:S(2)}, u32[]{:S(2)}) collective-permute-start(f32[4,1,256]{2,1,0:T(1,128)S(1)} %get-tuple-element.50), channel_id=1, source_target_pairs={{0,16},{1,17},{2,18},{3,19},{4,20},{5,21},{6,22},{7,23},{8,24},{9,... | collective-permute-start | bytes 12296 | tf_op jit(solution)/shard_map/ppermute | solution.py:26
  312.1 0.7 collective-permute-done.16
  312.8 5.7 %collective-permute-start.18 = (f32[1,130,256]{2,1,0:T(8,128)S(1)}, f32[1,130,256]{2,1,0:T(8,128)S(1)}, u32[]{:S(2)}, u32[]{:S(2)}) collective-permute-start(f32[1,130,256]{2,1,0:T(8,128)S(1)} %get-tuple-element.41), channel_id=1, source_target_pairs={{1,0},{2,1},{3,2},{4,3},{5,4},{6,5},{7,6},{8,7},{9,8},{10,9},{11,1... | collective-permute-start | bytes 399368 | tf_op jit(solution)/shard_map/ppermute | solution.py:28
  318.6 1.9 collective-permute-start.19
  320.5 0.6 collective-permute-done.18
  321.1 2.1 collective-permute-done.19
  323.5 1.3 collective-permute-start.21
  324.8 4.0 %collective-permute-start.20 = (f32[4,1,256]{2,1,0:T(1,128)S(1)}, f32[4,1,256]{2,1,0:T(1,128)S(1)}, u32[]{:S(2)}, u32[]{:S(2)}) collective-permute-start(f32[4,1,256]{2,1,0:T(1,128)S(1)} %get-tuple-element.48), channel_id=1, source_target_pairs={{0,16},{1,17},{2,18},{3,19},{4,20},{5,21},{6,22},{7,23},{8,24},{9,... | collective-permute-start | bytes 12296 | tf_op jit(solution)/shard_map/ppermute | solution.py:26
  328.8 0.7 collective-permute-done.20
  329.6 5.7 %collective-permute-start.22 = (f32[1,130,256]{2,1,0:T(8,128)S(1)}, f32[1,130,256]{2,1,0:T(8,128)S(1)}, u32[]{:S(2)}, u32[]{:S(2)}) collective-permute-start(f32[1,130,256]{2,1,0:T(8,128)S(1)} %get-tuple-element.39), channel_id=1, source_target_pairs={{1,0},{2,1},{3,2},{4,3},{5,4},{6,5},{7,6},{8,7},{9,8},{10,9},{11,1... | collective-permute-start | bytes 399368 | tf_op jit(solution)/shard_map/ppermute | solution.py:28
  335.3 1.9 collective-permute-start.23
  337.3 0.6 collective-permute-done.22
  337.9 2.1 collective-permute-done.23
  339.9 1.2 fusion.85
  (56 shorter events, 3.0 us)
Async XLA Ops:
  7.2 24.9 %all-gather.2.cloned.1.call-start = ((), (), s32[]{:S(2)}) async-start(), calls=%async_computation.1 | async-start | bytes 1572864 | tf_op jit(solution)/shard_map/all_gather | solution.py:84
  7.9 266.2 %reduce-scatter.2.cloned.1.call-start = ((), (), s32[]{:S(2)}) async-start(), calls=%async_computation.2 | async-start | bytes 1572864 | tf_op jit(solution)/shard_map/reduce_scatter | solution.py:110
  21.3 0.8 copy-start.6
  21.3 1.0 copy-start.7
  21.3 1.1 copy-start.8
  21.3 1.3 copy-start.9
  21.3 1.4 copy-start.10
  21.3 1.6 copy-start.11
  21.3 30.9 %copy-start.1 = (f32[2,1,4,256,256]{4,3,2,1,0:T(8,128)}, f32[2,1,4,256,256]{4,3,2,1,0:T(8,128)S(1)}, u32[]{:S(2)}) copy-start(f32[2,1,4,256,256]{4,3,2,1,0:T(8,128)S(1)} %get-tuple-element.18) | copy-start | bytes 6291460
  32.0 16.1 %copy-start.12 = (f32[4,256,256]{2,1,0:T(8,128)S(1)}, f32[4,256,256]{2,1,0:T(8,128)}, u32[]{:S(2)}) copy-start(f32[4,256,256]{2,1,0:T(8,128)} %all-gather.2.cloned.1.call-done) | copy-start | bytes 3145732
  32.0 16.1 %copy-start.17 = (s32[4,256,256]{2,1,0:T(8,128)S(1)}, s32[4,256,256]{2,1,0:T(8,128)}, u32[]{:S(2)}) copy-start(s32[4,256,256]{2,1,0:T(8,128)} %param.5) | copy-start | bytes 3145732
  33.6 14.5 %collective-permute-start = (f32[1,1,256,256]{3,2,1,0:T(8,128)S(1)}, f32[1,1,256,256]{3,2,1,0:T(8,128)S(1)}, u32[]{:S(2)}, u32[]{:S(2)}) collective-permute-start(f32[1,1,256,256]{3,2,1,0:T(8,128)S(1)} %get-tuple-element.37), channel_id=1, source_target_pairs={{1,0},{2,1},{3,2},{4,3},{5,4},{6,5},{7,6},{8,7},{9,8},{10,9},{11,1... | collective-permute-start | bytes 786440 | tf_op jit(solution)/shard_map/ppermute | solution.py:28
  36.2 11.9 %collective-permute-start.1 = (f32[1,1,256,256]{3,2,1,0:T(8,128)S(1)}, f32[1,1,256,256]{3,2,1,0:T(8,128)S(1)}, u32[]{:S(2)}, u32[]{:S(2)}) collective-permute-start(f32[1,1,256,256]{3,2,1,0:T(8,128)S(1)} %get-tuple-element.38), channel_id=1, source_target_pairs={{0,1},{1,2},{2,3},{3,4},{4,5},{5,6},{6,7},{7,8},{8,9},{9,10},{10,1... | collective-permute-start | bytes 786440 | tf_op jit(solution)/shard_map/ppermute | solution.py:26
  48.1 4.1 %copy-start.3 = (f32[2,1,4,256,256]{4,3,2,1,0:T(8,128)}, f32[2,1,4,256,256]{4,3,2,1,0:T(8,128)S(1)}, u32[]{:S(2)}) copy-start(f32[2,1,4,256,256]{4,3,2,1,0:T(8,128)S(1)} %add_bitcast_fusion) | copy-start | bytes 6291460
  48.2 4.1 %copy-start.2 = (f32[2,1,4,256,256]{4,3,2,1,0:T(8,128)S(1)}, f32[2,1,4,256,256]{4,3,2,1,0:T(8,128)}, u32[]{:S(2)}) copy-start(f32[2,1,4,256,256]{4,3,2,1,0:T(8,128)} %add_bitcast_fusion.1) | copy-start | bytes 6291460
  52.2 3.3 copy-start.4
  57.0 38.6 %collective-permute-start.2 = (f32[6,1,256,256]{3,2,1,0:T(8,128)S(1)}, f32[6,1,256,256]{3,2,1,0:T(8,128)S(1)}, u32[]{:S(2)}, u32[]{:S(2)}) collective-permute-start(f32[6,1,256,256]{3,2,1,0:T(8,128)S(1)} %get-tuple-element.31), channel_id=1, source_target_pairs={{1,0},{2,1},{3,2},{4,3},{5,4},{6,5},{7,6},{8,7},{9,8},{10,9},{11,1... | collective-permute-start | bytes 4718600 | tf_op jit(solution)/shard_map/ppermute | solution.py:28
  58.9 37.7 %collective-permute-start.3 = (f32[6,1,256,256]{3,2,1,0:T(8,128)S(1)}, f32[6,1,256,256]{3,2,1,0:T(8,128)S(1)}, u32[]{:S(2)}, u32[]{:S(2)}) collective-permute-start(f32[6,1,256,256]{3,2,1,0:T(8,128)S(1)} %get-tuple-element.32), channel_id=1, source_target_pairs={{0,1},{1,2},{2,3},{3,4},{4,5},{5,6},{6,7},{7,8},{8,9},{9,10},{10,1... | collective-permute-start | bytes 4718600 | tf_op jit(solution)/shard_map/ppermute | solution.py:26
  95.5 1.2 copy-start.13
  96.6 1.2 copy-start.14
  122.0 2.7 copy-start
  125.0 39.3 %collective-permute-start.4 = (f32[6,1,256,256]{3,2,0,1:T(8,128)S(1)}, f32[6,1,256,256]{3,2,0,1:T(8,128)S(1)}, u32[]{:S(2)}, u32[]{:S(2)}) collective-permute-start(f32[6,1,256,256]{3,2,0,1:T(8,128)S(1)} %get-tuple-element.29), channel_id=1, source_target_pairs={{1,0},{2,1},{3,2},{4,3},{5,4},{6,5},{7,6},{8,7},{9,8},{10,9},{11,1... | collective-permute-start | bytes 4718600 | tf_op jit(solution)/shard_map/ppermute | solution.py:28
  127.0 37.4 %collective-permute-start.5 = (f32[6,1,256,256]{3,2,0,1:T(8,128)S(1)}, f32[6,1,256,256]{3,2,0,1:T(8,128)S(1)}, u32[]{:S(2)}, u32[]{:S(2)}) collective-permute-start(f32[6,1,256,256]{3,2,0,1:T(8,128)S(1)} %get-tuple-element.30), channel_id=1, source_target_pairs={{0,1},{1,2},{2,3},{3,4},{4,5},{5,6},{6,7},{7,8},{8,9},{9,10},{10,1... | collective-permute-start | bytes 4718600 | tf_op jit(solution)/shard_map/ppermute | solution.py:26
  192.1 26.4 %collective-permute-start.6 = (f32[6,1,256,256]{3,2,0,1:T(8,128)S(1)}, f32[6,1,256,256]{3,2,0,1:T(8,128)S(1)}, u32[]{:S(2)}, u32[]{:S(2)}) collective-permute-start(f32[6,1,256,256]{3,2,0,1:T(8,128)S(1)} %get-tuple-element.27), channel_id=1, source_target_pairs={{1,0},{2,1},{3,2},{4,3},{5,4},{6,5},{7,6},{8,7},{9,8},{10,9},{11,1... | collective-permute-start | bytes 4718600 | tf_op jit(solution)/shard_map/ppermute | solution.py:28
  194.1 24.5 %collective-permute-start.7 = (f32[6,1,256,256]{3,2,0,1:T(8,128)S(1)}, f32[6,1,256,256]{3,2,0,1:T(8,128)S(1)}, u32[]{:S(2)}, u32[]{:S(2)}) collective-permute-start(f32[6,1,256,256]{3,2,0,1:T(8,128)S(1)} %get-tuple-element.28), channel_id=1, source_target_pairs={{0,1},{1,2},{2,3},{3,4},{4,5},{5,6},{6,7},{7,8},{8,9},{9,10},{10,1... | collective-permute-start | bytes 4718600 | tf_op jit(solution)/shard_map/ppermute | solution.py:26
  218.5 1.2 copy-start.15
  218.5 1.6 copy-start.16
  240.0 34.1 %copy-start.5 = (f32[4,128,256]{2,1,0:T(8,128)S(1)}, f32[4,128,256]{2,1,0:T(8,128)}, u32[]{:S(2)}) copy-start(f32[4,128,256]{2,1,0:T(8,128)} %param.4) | copy-start | bytes 1572868
  275.3 5.3 %collective-permute-start.9 = (f32[4,1,256]{2,1,0:T(1,128)S(1)}, f32[4,1,256]{2,1,0:T(1,128)S(1)}, u32[]{:S(2)}, u32[]{:S(2)}) collective-permute-start(f32[4,1,256]{2,1,0:T(1,128)S(1)} %get-tuple-element.53), channel_id=1, source_target_pairs={{16,0},{17,1},{18,2},{19,3},{20,4},{21,5},{22,6},{23,7},{24,8},{25... | collective-permute-start | bytes 12296 | tf_op jit(solution)/shard_map/ppermute | solution.py:28
  276.6 4.7 %collective-permute-start.8 = (f32[4,1,256]{2,1,0:T(1,128)S(1)}, f32[4,1,256]{2,1,0:T(1,128)S(1)}, u32[]{:S(2)}, u32[]{:S(2)}) collective-permute-start(f32[4,1,256]{2,1,0:T(1,128)S(1)} %get-tuple-element.54), channel_id=1, source_target_pairs={{0,16},{1,17},{2,18},{3,19},{4,20},{5,21},{6,22},{7,23},{8,24},{9,... | collective-permute-start | bytes 12296 | tf_op jit(solution)/shard_map/ppermute | solution.py:26
  281.3 7.5 %collective-permute-start.10 = (f32[1,130,256]{2,1,0:T(8,128)S(1)}, f32[1,130,256]{2,1,0:T(8,128)S(1)}, u32[]{:S(2)}, u32[]{:S(2)}) collective-permute-start(f32[1,130,256]{2,1,0:T(8,128)S(1)} %get-tuple-element.45), channel_id=1, source_target_pairs={{1,0},{2,1},{3,2},{4,3},{5,4},{6,5},{7,6},{8,7},{9,8},{10,9},{11,1... | collective-permute-start | bytes 399368 | tf_op jit(solution)/shard_map/ppermute | solution.py:28
  285.0 5.0 %collective-permute-start.11 = (f32[1,130,256]{2,1,0:T(8,128)S(1)}, f32[1,130,256]{2,1,0:T(8,128)S(1)}, u32[]{:S(2)}, u32[]{:S(2)}) collective-permute-start(f32[1,130,256]{2,1,0:T(8,128)S(1)} %get-tuple-element.46), channel_id=1, source_target_pairs={{0,1},{1,2},{2,3},{3,4},{4,5},{5,6},{6,7},{7,8},{8,9},{9,10},{10,1... | collective-permute-start | bytes 399368 | tf_op jit(solution)/shard_map/ppermute | solution.py:26
  290.4 5.3 %collective-permute-start.13 = (f32[4,1,256]{2,1,0:T(1,128)S(1)}, f32[4,1,256]{2,1,0:T(1,128)S(1)}, u32[]{:S(2)}, u32[]{:S(2)}) collective-permute-start(f32[4,1,256]{2,1,0:T(1,128)S(1)} %get-tuple-element.51), channel_id=1, source_target_pairs={{16,0},{17,1},{18,2},{19,3},{20,4},{21,5},{22,6},{23,7},{24,8},{25... | collective-permute-start | bytes 12296 | tf_op jit(solution)/shard_map/ppermute | solution.py:28
  291.7 4.7 %collective-permute-start.12 = (f32[4,1,256]{2,1,0:T(1,128)S(1)}, f32[4,1,256]{2,1,0:T(1,128)S(1)}, u32[]{:S(2)}, u32[]{:S(2)}) collective-permute-start(f32[4,1,256]{2,1,0:T(1,128)S(1)} %get-tuple-element.52), channel_id=1, source_target_pairs={{0,16},{1,17},{2,18},{3,19},{4,20},{5,21},{6,22},{7,23},{8,24},{9,... | collective-permute-start | bytes 12296 | tf_op jit(solution)/shard_map/ppermute | solution.py:26
  296.5 8.2 %collective-permute-start.14 = (f32[1,130,256]{2,1,0:T(8,128)S(1)}, f32[1,130,256]{2,1,0:T(8,128)S(1)}, u32[]{:S(2)}, u32[]{:S(2)}) collective-permute-start(f32[1,130,256]{2,1,0:T(8,128)S(1)} %get-tuple-element.43), channel_id=1, source_target_pairs={{1,0},{2,1},{3,2},{4,3},{5,4},{6,5},{7,6},{8,7},{9,8},{10,9},{11,1... | collective-permute-start | bytes 399368 | tf_op jit(solution)/shard_map/ppermute | solution.py:28
  301.8 4.6 %collective-permute-start.15 = (f32[1,130,256]{2,1,0:T(8,128)S(1)}, f32[1,130,256]{2,1,0:T(8,128)S(1)}, u32[]{:S(2)}, u32[]{:S(2)}) collective-permute-start(f32[1,130,256]{2,1,0:T(8,128)S(1)} %get-tuple-element.44), channel_id=1, source_target_pairs={{0,1},{1,2},{2,3},{3,4},{4,5},{5,6},{6,7},{7,8},{8,9},{9,10},{10,1... | collective-permute-start | bytes 399368 | tf_op jit(solution)/shard_map/ppermute | solution.py:26
  306.8 5.3 %collective-permute-start.17 = (f32[4,1,256]{2,1,0:T(1,128)S(1)}, f32[4,1,256]{2,1,0:T(1,128)S(1)}, u32[]{:S(2)}, u32[]{:S(2)}) collective-permute-start(f32[4,1,256]{2,1,0:T(1,128)S(1)} %get-tuple-element.49), channel_id=1, source_target_pairs={{16,0},{17,1},{18,2},{19,3},{20,4},{21,5},{22,6},{23,7},{24,8},{25... | collective-permute-start | bytes 12296 | tf_op jit(solution)/shard_map/ppermute | solution.py:28
  308.1 4.7 %collective-permute-start.16 = (f32[4,1,256]{2,1,0:T(1,128)S(1)}, f32[4,1,256]{2,1,0:T(1,128)S(1)}, u32[]{:S(2)}, u32[]{:S(2)}) collective-permute-start(f32[4,1,256]{2,1,0:T(1,128)S(1)} %get-tuple-element.50), channel_id=1, source_target_pairs={{0,16},{1,17},{2,18},{3,19},{4,20},{5,21},{6,22},{7,23},{8,24},{9,... | collective-permute-start | bytes 12296 | tf_op jit(solution)/shard_map/ppermute | solution.py:26
  312.8 8.3 %collective-permute-start.18 = (f32[1,130,256]{2,1,0:T(8,128)S(1)}, f32[1,130,256]{2,1,0:T(8,128)S(1)}, u32[]{:S(2)}, u32[]{:S(2)}) collective-permute-start(f32[1,130,256]{2,1,0:T(8,128)S(1)} %get-tuple-element.41), channel_id=1, source_target_pairs={{1,0},{2,1},{3,2},{4,3},{5,4},{6,5},{7,6},{8,7},{9,8},{10,9},{11,1... | collective-permute-start | bytes 399368 | tf_op jit(solution)/shard_map/ppermute | solution.py:28
  318.6 4.6 %collective-permute-start.19 = (f32[1,130,256]{2,1,0:T(8,128)S(1)}, f32[1,130,256]{2,1,0:T(8,128)S(1)}, u32[]{:S(2)}, u32[]{:S(2)}) collective-permute-start(f32[1,130,256]{2,1,0:T(8,128)S(1)} %get-tuple-element.42), channel_id=1, source_target_pairs={{0,1},{1,2},{2,3},{3,4},{4,5},{5,6},{6,7},{7,8},{8,9},{9,10},{10,1... | collective-permute-start | bytes 399368 | tf_op jit(solution)/shard_map/ppermute | solution.py:26
  323.5 5.3 %collective-permute-start.21 = (f32[4,1,256]{2,1,0:T(1,128)S(1)}, f32[4,1,256]{2,1,0:T(1,128)S(1)}, u32[]{:S(2)}, u32[]{:S(2)}) collective-permute-start(f32[4,1,256]{2,1,0:T(1,128)S(1)} %get-tuple-element.47), channel_id=1, source_target_pairs={{16,0},{17,1},{18,2},{19,3},{20,4},{21,5},{22,6},{23,7},{24,8},{25... | collective-permute-start | bytes 12296 | tf_op jit(solution)/shard_map/ppermute | solution.py:28
  324.8 4.7 %collective-permute-start.20 = (f32[4,1,256]{2,1,0:T(1,128)S(1)}, f32[4,1,256]{2,1,0:T(1,128)S(1)}, u32[]{:S(2)}, u32[]{:S(2)}) collective-permute-start(f32[4,1,256]{2,1,0:T(1,128)S(1)} %get-tuple-element.48), channel_id=1, source_target_pairs={{0,16},{1,17},{2,18},{3,19},{4,20},{5,21},{6,22},{7,23},{8,24},{9,... | collective-permute-start | bytes 12296 | tf_op jit(solution)/shard_map/ppermute | solution.py:26
  329.6 8.3 %collective-permute-start.22 = (f32[1,130,256]{2,1,0:T(8,128)S(1)}, f32[1,130,256]{2,1,0:T(8,128)S(1)}, u32[]{:S(2)}, u32[]{:S(2)}) collective-permute-start(f32[1,130,256]{2,1,0:T(8,128)S(1)} %get-tuple-element.39), channel_id=1, source_target_pairs={{1,0},{2,1},{3,2},{4,3},{5,4},{6,5},{7,6},{8,7},{9,8},{10,9},{11,1... | collective-permute-start | bytes 399368 | tf_op jit(solution)/shard_map/ppermute | solution.py:28
  335.3 4.6 %collective-permute-start.23 = (f32[1,130,256]{2,1,0:T(8,128)S(1)}, f32[1,130,256]{2,1,0:T(8,128)S(1)}, u32[]{:S(2)}, u32[]{:S(2)}) collective-permute-start(f32[1,130,256]{2,1,0:T(8,128)S(1)} %get-tuple-element.40), channel_id=1, source_target_pairs={{0,1},{1,2},{2,3},{3,4},{4,5},{5,6},{6,7},{7,8},{8,9},{9,10},{10,1... | collective-permute-start | bytes 399368 | tf_op jit(solution)/shard_map/ppermute | solution.py:26
Sparse Core Ops, SparseCore 0:
  9.5 22.4 all-gather.1
  243.8 30.2 reduce-scatter.1
where the time goes:
time: 352 us; the launch traced here: 348 us
  waiting for transfers between devices  132 us (38%)
  other arithmetic  114 us (32%)
  starting transfers between devices  73.8 us (21%)
  between operations  14.5 us (4%)
  local copies, waits for them, and re-layouts  13.6 us (4%)
    ppermute x12, waiting for transfers between devices, with_halo(): lax.ppermute(head, axis, [((i + 1) % count, i) for i in range(ends)])  89.4 us
    ppermute x12, starting transfers between devices, with_halo(): lax.ppermute(tail, axis, [(i, (i + 1) % count) for i in range(ends)])  39.7 us
    ppermute x12, starting transfers between devices, with_halo(): lax.ppermute(head, axis, [((i + 1) % count, i) for i in range(ends)])  34 us
    reduce_scatter x1, waiting for transfers between devices, local(): owned = lax.psum_scatter(energy, 'case', scatter_dimension=1, tiled=True)  30.4 us
    another operation x4, other arithmetic, forces(): return jnp.stack(parts, axis=-4)  30.3 us
    add x1, other arithmetic, local(): iterate = iterate + search  25.5 us
    add x1, other arithmetic, local(): factor_new * factor_old * search  24.2 us
    reduce_sum x1, other arithmetic, local(): energy = energy + 0.5 * jnp.sum((middle - other) ** 2, axis=(0, 1))  19.9 us
  transfers between devices with their start and end apart: 26, of which 18 were waited for; matrix products, arithmetic and copies ran while one was open for 9% of the time, Pallas kernels for 0%

commit v1 on v0

v1 whole, which is shorter than its diff:
```python
import jax
import jax.numpy as jnp
from jax import lax
from jax.experimental import pallas as pl
from jax.experimental.pallas import tpu as pltpu
from jax.sharding import PartitionSpec as P

ITERS = 3
FSWEEPS = 4

E_MIN = 0.001
PENALTY = 3.0
SPRING = 4.0
LOWER = 0.05
UPPER = 2.0
RADIUS_SQ = 2.0

CENTRE = (UPPER + LOWER) / 2.0
HALF = (UPPER - LOWER) / 2.0
SIGMA = CENTRE / HALF
RHO0 = 1.0 / SIGMA
RHO1 = 1.0 / (2.0 * SIGMA - RHO0)
RHO2 = 1.0 / (2.0 * SIGMA - RHO1)
ALPHA1, B1 = RHO1 * RHO0, 2.0 * RHO1 / HALF
ALPHA2, B2 = RHO2 * RHO1, 2.0 * RHO2 / HALF
G0 = ALPHA1 + B1 * (CENTRE - 1.0)
A0 = 1.0 - B2 * ALPHA1 / B1
A1 = 1.0 + ALPHA2 + B2 / B1 - B2
RATIO = B2 / B1

HALO = 4
EXTRA = 8
PAD = 8


def step_kernel(planes, rows, info, table, valid, loads, support, mid, lo_d, hi_d, lo_i, hi_i, *rest):
    (u_out, e_out, idx_v, sup_v, m_v, k_v, s0_v, s1_v, u_v, in_sem, out_sem) = rest[-11:]
    tiles = rows // 8
    h = info[0]
    vlo, vhi = valid[0], valid[1]
    start = pl.multiple_of(h * info[1], 8)
    wide = planes + 6
    copies = []
    for case in range(2):
        copies.append(pltpu.make_async_copy(
            loads.at[case, :, pl.ds(start, rows), :], idx_v.at[case, pl.ds(3, planes)], in_sem.at[case]))
        copies.append(pltpu.make_async_copy(lo_i.at[pl.ds(3 * case, 3)], idx_v.at[case, pl.ds(0, 3)], in_sem.at[2 + case]))
        copies.append(pltpu.make_async_copy(hi_i.at[pl.ds(3 * case, 3)], idx_v.at[case, pl.ds(planes + 3, 3)], in_sem.at[4 + case]))
    copies.append(pltpu.make_async_copy(support.at[:, pl.ds(start, rows), :], sup_v.at[pl.ds(3, planes)], in_sem.at[6]))
    copies.append(pltpu.make_async_copy(lo_i.at[pl.ds(6, 3)], sup_v.at[pl.ds(0, 3)], in_sem.at[7]))
    copies.append(pltpu.make_async_copy(hi_i.at[pl.ds(6, 3)], sup_v.at[pl.ds(planes + 3, 3)], in_sem.at[8]))
    for copy in copies:
        copy.start()

    zero = jnp.zeros((PAD, 128), jnp.float32)
    for z in range(2):
        def clear(count, ref):
            def body(i, carry):
                ref[i, z, pl.ds(0, PAD), :] = zero
                ref[i, z, pl.ds(PAD + rows, PAD), :] = zero
                return carry
            lax.fori_loop(0, count, body, 0)
        clear(planes + 8, m_v)
        clear(6 * (planes + 6), s0_v)
        clear(6 * (planes + 4), s1_v)
        clear(6 * (planes + 2), u_v)

    def modulus(source, first, count, scale):
        def body(i, carry):
            p, r = i // tiles, pl.multiple_of(i % tiles * 8, 8)
            for z in range(2):
                d = source[p, pl.ds(r, 8), pl.ds(128 * z, 128)]
                m = E_MIN + d * d * d * (1.0 - E_MIN)
                if scale is not None:
                    m = m * scale
                m_v[first + p, z, pl.ds(PAD + r, 8), :] = m
            return carry
        lax.fori_loop(0, count * tiles, body, 0)

    modulus(lo_d, 0, 4, vlo)
    modulus(mid, 4, planes, None)
    modulus(hi_d, planes + 4, 4, vhi)

    lane = lax.broadcasted_iota(jnp.int32, (8, 128), 1)
    first_lane, last_lane = lane == 0, lane == 127

    def above(a):
        r0, r1 = pltpu.roll(a[0], 127, 1), pltpu.roll(a[1], 127, 1)
        return [jnp.where(last_lane, r1, r0), r1]

    def below(a):
        r0, r1 = pltpu.roll(a[0], 1, 1), pltpu.roll(a[1], 1, 1)
        return [r0, jnp.where(first_lane, r0, r1)]

    def get(ref, i, row):
        return [ref[i, z, pl.ds(row, 8), :] for z in range(2)]

    for copy in copies:
        copy.wait()

    def first(i, carry):
        p, r = i // tiles, pl.multiple_of(i % tiles * 8, 8)
        row = PAD + r
        m = get(m_v, p + 1, row)
        zup, zdn = above(m), below(m)
        zup[1] = jnp.where(last_lane, 0.0, zup[1])
        zdn[0] = jnp.where(first_lane, 0.0, zdn[0])
        beside = [get(m_v, p + 2, row), get(m_v, p, row), get(m_v, p + 1, row + 1), get(m_v, p + 1, row - 1), zup, zdn]
        ok = jnp.where(p < 3, vlo, jnp.where(p >= planes + 3, vhi, 1.0))
        scale = []
        for z in range(2):
            face = [(m[z] + b[z]) * 0.5 for b in beside]
            diagonal = face[0] + face[1] + face[2] + face[3] + face[4] + face[5]
            diagonal = diagonal + SPRING * sup_v[p, pl.ds(r, 8), pl.ds(128 * z, 128)].astype(jnp.float32)
            w = ok / (diagonal + (1.0 - ok))
            scale.append(w * (RATIO / CENTRE))
            wb = w * B1
            weight = [f * wb for f in face]
            if z == 1:
                weight[4] = jnp.where(last_lane, 0.0, weight[4])
            else:
                weight[5] = jnp.where(first_lane, 0.0, weight[5])
            for j in range(6):
                k_v[p, j, z, pl.ds(r, 8), :] = weight[j]
        for case in range(2):
            for z in range(2):
                index = idx_v[case, p, pl.ds(r, 8), pl.ds(128 * z, 128)]
                b0, b1, b2 = (index & 1) != 0, (index & 2) != 0, (index & 4) != 0
                for c in range(3):
                    q = [jnp.where(b0, table[2 * j + 1, c], table[2 * j, c]) for j in range(4)]
                    f = jnp.where(b2, jnp.where(b1, q[3], q[2]), jnp.where(b1, q[1], q[0]))
                    s0_v[p * 6 + case * 3 + c, z, pl.ds(row, 8), :] = f * scale[z]
        return carry

    lax.fori_loop(0, wide * tiles, first, 0)

    def stencil(ref, at, row, k):
        c = get(ref, at, row)
        parts = [get(ref, at + 6, row), get(ref, at - 6, row), get(ref, at, row + 1), get(ref, at, row - 1), above(c), below(c)]
        out = []
        for z in range(2):
            t = [k[j][z] * parts[j][z] for j in range(6)]
            out.append(((t[0] + t[1]) + (t[2] + t[3])) + (t[4] + t[5]))
        return c, out

    def second(i, carry):
        p, r = i // tiles, pl.multiple_of(i % tiles * 8, 8)
        row = PAD + r
        k = [[k_v[p + 1, j, z, pl.ds(r, 8), :] for z in range(2)] for j in range(6)]
        for f in range(6):
            c, t = stencil(s0_v, (p + 1) * 6 + f, row, k)
            for z in range(2):
                s1_v[p * 6 + f, z, pl.ds(row, 8), :] = G0 * c[z] + t[z]
        return carry

    lax.fori_loop(0, (planes + 4) * tiles, second, 0)

    def third(i, carry):
        p, r = i // tiles, pl.multiple_of(i % tiles * 8, 8)
        row = PAD + r
        k = [[k_v[p + 2, j, z, pl.ds(r, 8), :] for z in range(2)] for j in range(6)]
        for f in range(6):
            c, t = stencil(s1_v, (p + 1) * 6 + f, row, k)
            base = get(s0_v, (p + 2) * 6 + f, row)
            for z in range(2):
                u_v[p * 6 + f, z, pl.ds(row, 8), :] = (A0 / RATIO) * base[z] + (A1 / RATIO) * c[z] + t[z]
        return carry

    lax.fori_loop(0, (planes + 2) * tiles, third, 0)

    half = rows - EXTRA
    skip = pl.multiple_of(h * EXTRA, 8)
    outs = []
    for z in range(2):
        for p in range(planes):
            for f in range(6):
                outs.append(pltpu.make_async_copy(
                    u_v.at[(p + 1) * 6 + f, z, pl.ds(PAD + skip, half), :],
                    u_out.at[f // 3, f % 3, p, pl.ds(pl.multiple_of(h * half, 8), half), pl.ds(128 * z, 128)],
                    out_sem.at[(z * planes + p) * 6 + f]))
    for copy in outs:
        copy.start()

    def energy(i, carry):
        p, r = i // tiles, pl.multiple_of(i % tiles * 8, 8)
        row = PAD + r
        acc = [jnp.zeros((8, 128), jnp.float32) for _ in range(2)]
        for f in range(6):
            at = (p + 1) * 6 + f
            c = get(u_v, at, row)
            zup, zdn = above(c), below(c)
            zup[1] = jnp.where(last_lane, 0.0, zup[1])
            zdn[0] = jnp.where(first_lane, 0.0, zdn[0])
            for b in (get(u_v, at + 6, row), get(u_v, at - 6, row), get(u_v, at, row + 1), get(u_v, at, row - 1), zup, zdn):
                for z in range(2):
                    d = c[z] - b[z]
                    acc[z] = acc[z] + d * d
        for z in range(2):
            e_out[p, pl.ds(r, 8), pl.ds(128 * z, 128)] = 0.5 * acc[z]
        return carry

    lax.fori_loop(0, planes * tiles, energy, 0)
    for copy in outs:
        copy.wait()


def step(h, gap, valid, table, loads, support, mid, lo_d, hi_d, lo_i, hi_i, u):
    planes, rows, cols = mid.shape
    tiles_rows = rows + 2 * PAD
    f32 = jnp.float32
    any_spec = pl.BlockSpec(memory_space=pl.ANY)
    smem = pl.BlockSpec(memory_space=pltpu.SMEM)
    vmem = pl.BlockSpec(memory_space=pltpu.VMEM)
    full = loads.shape[2]
    args = [jnp.stack([h, gap]).astype(jnp.int32), table, valid, loads, support, mid, lo_d, hi_d, lo_i, hi_i]
    specs = [smem, smem, smem, any_spec, any_spec, vmem, vmem, vmem, any_spec, any_spec]
    aliases = {}
    if u is not None:
        args.append(u)
        specs.append(any_spec)
        aliases = {len(args) - 1: 0}

    def kernel(*refs):
        step_kernel(planes, rows, *refs)

    return pl.pallas_call(
        kernel,
        out_shape=(jax.ShapeDtypeStruct((2, 3, planes, full, cols), f32), jax.ShapeDtypeStruct((planes, rows, cols), f32)),
        in_specs=specs,
        out_specs=(any_spec, vmem),
        input_output_aliases=aliases,
        scratch_shapes=[
            pltpu.VMEM((2, planes + 6, rows, cols), jnp.int32),
            pltpu.VMEM((planes + 6, rows, cols), jnp.int32),
            pltpu.VMEM((planes + 8, 2, tiles_rows, 128), f32),
            pltpu.VMEM((planes + 6, 6, 2, rows, 128), f32),
            pltpu.VMEM((6 * (planes + 6), 2, tiles_rows, 128), f32),
            pltpu.VMEM((6 * (planes + 4), 2, tiles_rows, 128), f32),
            pltpu.VMEM((6 * (planes + 2), 2, tiles_rows, 128), f32),
            pltpu.SemaphoreType.DMA((9,)),
            pltpu.SemaphoreType.DMA((2 * planes * 6,)),
        ],
        compiler_params=pltpu.CompilerParams(vmem_limit_bytes=56 * 1024 * 1024),
        cost_estimate=pl.CostEstimate(flops=40_000_000, bytes_accessed=40_000_000, transcendentals=0),
        name="relax",
    )(*args)


def filter_kernel(planes, rows, info, valid, lo, mid, hi, dens, out, r_v, a_v, b_v):
    tiles = rows // 8
    h = info[0]
    vlo, vhi = valid[0], valid[1]
    half = rows - EXTRA
    zero = jnp.zeros((PAD, 128), jnp.float32)
    lane = lax.broadcasted_iota(jnp.int32, (8, 128), 1)
    first_lane, last_lane = lane == 0, lane == 127

    def clear(i, carry):
        for ref in (r_v, a_v, b_v):
            for z in range(2):
                ref[i, z, pl.ds(0, PAD), :] = zero
                ref[i, z, pl.ds(PAD + rows, PAD), :] = zero
        return carry

    lax.fori_loop(0, planes + 8, clear, 0)

    def fill(source, first, count):
        def body(i, carry):
            p, r = i // tiles, pl.multiple_of(i % tiles * 8, 8)
            for z in range(2):
                r_v[first + p, z, pl.ds(PAD + r, 8), :] = source[p, pl.ds(r, 8), pl.ds(128 * z, 128)]
            return carry

        lax.fori_loop(0, count * tiles, body, 0)

    fill(lo, 0, 4)
    fill(mid, 4, planes)
    fill(hi, planes + 4, 4)

    def smoothed(src, p, row):
        ok = jnp.where(p < 4, vlo, jnp.where(p >= planes + 4, vhi, 1.0))
        c = [src[p, z, pl.ds(row, 8), :] for z in range(2)]
        u0, u1 = pltpu.roll(c[0], 127, 1), pltpu.roll(c[1], 127, 1)
        d0, d1 = pltpu.roll(c[0], 1, 1), pltpu.roll(c[1], 1, 1)
        zs = [
            jnp.where(last_lane, u1, u0) + jnp.where(first_lane, 0.0, d0),
            jnp.where(last_lane, 0.0, u1) + jnp.where(first_lane, d0, d1),
        ]
        new = []
        for z in range(2):
            total = (src[p + 1, z, pl.ds(row, 8), :] + src[p - 1, z, pl.ds(row, 8), :]) + (
                src[p, z, pl.ds(row + 1, 8), :] + src[p, z, pl.ds(row - 1, 8), :]) + zs[z]
            scale = ok * (1.0 / (1.0 + 6.0 * RADIUS_SQ))
            new.append((r_v[p, z, pl.ds(row, 8), :] + RADIUS_SQ * total) * scale)
        return new

    def sweep(src, dst, low, high):
        def body(i, carry):
            p, row = low + i // tiles, pl.multiple_of(PAD + i % tiles * 8, 8)
            new = smoothed(src, p, row)
            for z in range(2):
                dst[p, z, pl.ds(row, 8), :] = new[z]
            return carry

        lax.fori_loop(0, (high - low) * tiles, body, 0)

    sweep(r_v, a_v, 1, planes + 7)
    sweep(a_v, b_v, 2, planes + 6)
    sweep(b_v, a_v, 3, planes + 5)

    skip = h * EXTRA

    def last(i, carry):
        p, r = i // (half // 8), pl.multiple_of(i % (half // 8) * 8, 8)
        new = smoothed(a_v, p + 4, pl.multiple_of(PAD + r + skip, 8))
        for z in range(2):
            out[p, pl.ds(r, 8), pl.ds(128 * z, 128)] = new[z] / dens[p, pl.ds(r, 8), pl.ds(128 * z, 128)]
        return carry

    lax.fori_loop(0, planes * (half // 8), last, 0)


def smooth(h, gap, valid, lo, mid, hi, dens):
    planes, rows, cols = mid.shape
    f32 = jnp.float32
    smem = pl.BlockSpec(memory_space=pltpu.SMEM)
    vmem = pl.BlockSpec(memory_space=pltpu.VMEM)

    def kernel(*refs):
        filter_kernel(planes, rows, *refs)

    return pl.pallas_call(
        kernel,
        out_shape=jax.ShapeDtypeStruct(dens.shape, f32),
        in_specs=[smem, smem] + [vmem] * 4,
        out_specs=vmem,
        scratch_shapes=[pltpu.VMEM((planes + 8, 2, rows + 2 * PAD, 128), f32)] * 3,
        compiler_params=pltpu.CompilerParams(vmem_limit_bytes=32 * 1024 * 1024),
        cost_estimate=pl.CostEstimate(flops=5_000_000, bytes_accessed=5_000_000, transcendentals=0),
        name="smooth",
    )(jnp.stack([h, gap]).astype(jnp.int32), valid, lo, mid, hi, dens)


def local(density, support, loads, load_table):
    planes, half, cols = density.shape
    full = loads.shape[2]
    rows = half + EXTRA
    gap = full - rows
    mine = lax.axis_index("case")
    count = lax.axis_size("slab")
    at = lax.axis_index("slab")
    valid = jnp.stack([at > 0, at < count - 1]).astype(jnp.float32)
    rise = [(i, i + 1) for i in range(count - 1)]
    fall = [(i + 1, i) for i in range(count - 1)]
    swap = [(0, 1), (1, 0)]

    partner = lax.ppermute(density, "case", swap)

    def window(h):
        start = h * gap
        own = lax.dynamic_slice_in_dim(loads, start, rows, axis=2)
        sup = lax.dynamic_slice_in_dim(support, start, rows, axis=1)

        def pack(a, b):
            return jnp.concatenate([own[0, a:b], own[1, a:b], sup[a:b]], axis=0)

        lo_i = lax.ppermute(pack(planes - 3, planes), "slab", rise)
        hi_i = lax.ppermute(pack(0, 3), "slab", fall)
        return lo_i, hi_i

    def densities(h, main, other):
        low = jnp.concatenate([main, other[:, :EXTRA]], axis=1)
        high = jnp.concatenate([other[:, half - EXTRA:], main], axis=1)
        mid = jnp.where(h == 0, low, high)
        lo_d = lax.ppermute(mid[planes - 4:], "slab", rise)
        hi_d = lax.ppermute(mid[:4], "slab", fall)
        return mid, lo_d, hi_d

    ints_a = window(1 - mine)
    dens_a = densities(1 - mine, partner, density)
    ints_b = window(mine)
    dens_b = densities(mine, density, partner)
    u, e_a = step(1 - mine, gap, valid, load_table, loads, support, *dens_a, *ints_a, None)
    received = lax.ppermute(e_a, "case", swap)
    u, e_b = step(mine, gap, valid, load_table, loads, support, *dens_b, *ints_b, u)
    mid = dens_b[0]
    right = (-PENALTY * (1.0 - E_MIN)) * (mid * mid * mid) * (e_b + received)
    lo_r = lax.ppermute(right[planes - 4:], "slab", rise)
    hi_r = lax.ppermute(right[:4], "slab", fall)
    filtered = smooth(mine, gap, valid, lo_r, right, hi_r, density)
    return u, filtered


def solution(mesh):
    return jax.shard_map(
        local,
        mesh=mesh,
        in_specs=(
            P("slab", "case", None),
            P("slab", None, None),
            P("case", "slab", None, None),
            P(),
        ),
        out_specs=(P("case", None, "slab", None, None), P("slab", "case", None)),
        check_vma=False,
    )
```

time: 352 us -> 268 us (0.76)
  Pallas kernels: 0 us -> 158 us
  other arithmetic: 114 us -> 9.12 us
  waiting for transfers between devices: 132 us -> 64.2 us
  starting transfers between devices: 73.8 us -> 29.8 us
  between operations: 14.5 us -> 0.92 us
  local copies, waits for them, and re-layouts: 13.6 us -> 5.78 us
    pallas_call x0 -> x3, Pallas kernels: none -> 158 us  [the longest x2 117 us: step(): pl.pallas_call(kernel, out_shape=(jax.ShapeDtypeStruct((2, 3, planes, ful...]
    add x4 -> x0, other arithmetic: 54.9 us -> none  [the longest x1 25.5 us: local(): iterate = iterate + search]
    ppermute x24 -> x12, starting transfers between devices: 73.7 us -> 29.8 us  [the longest x2 7.01 us: window(): lo_i = lax.ppermute(pack(planes - 3, planes), 'slab', rise)]
    ppermute x24 -> x12, waiting for transfers between devices: 100 us -> 64.2 us  [the longest x2 38.6 us: densities(): hi_d = lax.ppermute(mid[:4], 'slab', fall)]
    reduce_scatter x1 -> x0, waiting for transfers between devices: 30.4 us -> none  [local(): owned = lax.psum_scatter(energy, 'case', scatter_dimension=1, tiled=True)]
    another operation x4 -> x2, other arithmetic: 30.3 us -> 1.24 us  [step(): jnp.stack([h, gap]).astype(jnp.int32)]
    reduce_sum x1 -> x0, other arithmetic: 19.9 us -> none  [local(): energy = energy + 0.5 * jnp.sum((middle - other) ** 2, axis=(0, 1))]
    unnamed x38 -> x25, local copies, waits for them, and re-layouts: 9.75 us -> 1.93 us
  transfers between devices with their start and end apart: 26 -> 12, of which waited for: 18 -> 4; matrix products, arithmetic and copies ran while one was open for 9% -> 5% of each run, Pallas kernels for 0% -> 44%
where the time goes in v1:
time: 268 us; the launch traced here: 267 us
  Pallas kernels  158 us (59%)
  waiting for transfers between devices  64.2 us (24%)
  starting transfers between devices  29.8 us (11%)
  other arithmetic  9.12 us (3%)
  local copies, waits for them, and re-layouts  5.78 us (2%)
    pallas_call x2, Pallas kernels, step(): pl.pallas_call(kernel, out_shape=(jax.ShapeDtypeStruct((2, 3, planes, ful...  117 us
    pallas_call x1, Pallas kernels, smooth(): pl.pallas_call(kernel, out_shape=jax.ShapeDtypeStruct(dens.shape, f32), i...  41 us
    ppermute x2, waiting for transfers between devices, densities(): hi_d = lax.ppermute(mid[:4], 'slab', fall)  38.6 us
    ppermute x2, waiting for transfers between devices, densities(): lo_d = lax.ppermute(mid[planes - 4:], 'slab', rise)  13.7 us
    ppermute x1, waiting for transfers between devices, local(): hi_r = lax.ppermute(right[:4], 'slab', fall)  11.2 us
    ppermute x2, starting transfers between devices, window(): lo_i = lax.ppermute(pack(planes - 3, planes), 'slab', rise)  7.01 us
    ppermute x2, starting transfers between devices, densities(): lo_d = lax.ppermute(mid[planes - 4:], 'slab', rise)  6.3 us
    ppermute x2, starting transfers between devices, densities(): hi_d = lax.ppermute(mid[:4], 'slab', fall)  5.36 us
  transfers between devices with their start and end apart: 12, of which 4 were waited for; matrix products, arithmetic and copies ran while one was open for 5% of the time, Pallas kernels for 44%

profile of v1, /device:TPU:9, one launch (start us, length us, event | category | flops | bytes accessed | tf_op | source)
XLA Modules:
  0.0 267.3 jit_solution(15406913451019667638)
XLA Ops:
  0.6 1.3 collective-permute-start
  1.9 0.0 copy-start.3
  1.9 2.2 dynamic-slice_bitcast_fusion.1
  4.1 0.0 copy-done.3
  4.1 0.9 constant_dynamic-slice_fusion.2
  5.0 1.2 pad_add_fusion.2
  6.2 4.0 %collective-permute-start.7 = (s32[9,136,256]{2,1,0:T(8,128)}, s32[9,136,256]{2,1,0:T(8,128)}, u32[]{:S(2)}, u32[]{:S(2)}) collective-permute-start(s32[9,136,256]{2,1,0:T(8,128)} %pad_add_fusion.2), channel_id=1, source_target_pairs={{0,1},{1,2},{2,3},{3,4},{4,5},{5,6},{6,7},{7,8},{8,9},{9,10},{10,1... | collective-permute-start | bytes 3760136 | tf_op jit(solution)/shard_map/ppermute | solution.py:367
  10.2 0.0 copy-start
  10.2 1.2 pad_add_fusion.3
  11.3 1.9 collective-permute-start.8
  13.2 0.0 copy-done
  13.3 0.5 collective-permute-done
  13.8 1.4 maximum_select_fusion.1.refs_5_
  15.2 0.0 copy-start.6
  15.2 3.5 %collective-permute-start.6 = (f32[4,136,256]{2,1,0:T(8,128)S(1)}, f32[4,136,256]{2,1,0:T(8,128)}, u32[]{:S(2)}, u32[]{:S(2)}) collective-permute-start(f32[4,136,256]{2,1,0:T(8,128)S(1)} %maximum_select_fusion.1.refs_5_), channel_id=1, source_target_pairs={{1,0},{2,1},{3,2},{4,3},{5,4},{6,5},{7,6},{8,7},{9,8},{10,9},{11,1... | collective-permute-start | bytes 1671176 | tf_op jit(solution)/shard_map/ppermute | solution.py:376
  18.7 0.0 copy-start.7
  18.7 1.2 pad_add_fusion
  19.8 3.0 %collective-permute-start.3 = (s32[9,136,256]{2,1,0:T(8,128)}, s32[9,136,256]{2,1,0:T(8,128)S(1)}, u32[]{:S(2)}, u32[]{:S(2)}) collective-permute-start(s32[9,136,256]{2,1,0:T(8,128)} %pad_add_fusion), channel_id=1, source_target_pairs={{0,1},{1,2},{2,3},{3,4},{4,5},{5,6},{6,7},{7,8},{8,9},{9,10},{10,1... | collective-permute-start | bytes 3760136 | tf_op jit(solution)/shard_map/ppermute | solution.py:367
  22.9 0.0 copy-done.7
  22.9 1.1 pad_add_fusion.1
  24.0 0.0 copy-start.11
  24.0 2.0 collective-permute-start.4
  26.1 38.6 %collective-permute-done.6.refs_7_ = f32[4,136,256]{2,1,0:T(8,128)} collective-permute-done((f32[4,136,256]{2,1,0:T(8,128)S(1)}, f32[4,136,256]{2,1,0:T(8,128)}, u32[]{:S(2)}, u32[]{:S(2)}) %collective-permute-start.6) | collective-permute-done | bytes 557088 | tf_op jit(solution)/shard_map/ppermute | solution.py:376
  64.7 0.0 copy-done.6
  64.7 1.9 collective-permute-start.5
  66.7 0.7 add_convert_fusion.refs_2_.refs_1_
  67.3 0.6 pad_add_fusion.4.refs_0_
  67.9 0.8 fusion.3
  68.8 0.0 copy-start.4
  68.8 13.7 %collective-permute-done.5.refs_6_ = f32[4,136,256]{2,1,0:T(8,128)S(1)} collective-permute-done((f32[4,136,256]{2,1,0:T(8,128)S(1)}, f32[4,136,256]{2,1,0:T(8,128)S(1)}, u32[]{:S(2)}, u32[]{:S(2)}) %collective-permute-start.5) | collective-permute-done | bytes 557088 | tf_op jit(solution)/shard_map/ppermute | solution.py:375
  82.5 0.0 copy-start.10
  82.5 1.9 collective-permute-start.2
  84.4 0.0 copy-done.10
  84.4 0.0 collective-permute-done.7.refs_8_
  84.4 4.4 %collective-permute-start.1 = (f32[4,136,256]{2,1,0:T(8,128)S(1)}, f32[4,136,256]{2,1,0:T(8,128)}, u32[]{:S(2)}, u32[]{:S(2)}) collective-permute-start(f32[4,136,256]{2,1,0:T(8,128)S(1)} %maximum_select_fusion.refs_5_), channel_id=1, source_target_pairs={{0,1},{1,2},{2,3},{3,4},{4,5},{5,6},{6,7},{7,8},{8,9},{9,10},{10,1... | collective-permute-start | bytes 1671176 | tf_op jit(solution)/shard_map/ppermute | solution.py:375
  88.8 0.0 copy-done.11
  88.8 0.7 copy.8.refs_1_
  89.5 0.0 collective-permute-done.8.refs_9_
  89.5 58.2 %relax.2 = (f32[2,3,4,256,256]{4,3,2,1,0:T(8,128)}, f32[4,136,256]{2,1,0:T(8,128)}) custom-call(s32[2]{0:T(128)} %pad_add_fusion.4.refs_0_, f32[8,3]{1,0:T(8,128)} %copy.8.refs_1_, f32[2]{0:T(128)} %add_convert_fusion.refs_2_.refs_1_, s32[2,4,256,256]{3,2,1,0:T(8,128)} %refs_3_.3, s32[4,256,256]{2,1,0:T(8,128)} %refs_4_.3, f32[4,136,256]{2,1,0:T(8,128)} %copy-done.6, ...), custom_call_target="tpu_custom_call" | custom-call | flops 40000000 | bytes 40000000 | tf_op jit(solution)/shard_map/relax/pallas_call | solution.py:226
  147.7 0.0 copy-done.4
  147.7 0.3 collective-permute-start.9
  148.1 0.7 pad_add_fusion.5.refs_0_
  148.7 0.0 collective-permute-done.2.refs_7_
  148.7 0.0 copy-start.9
  148.7 0.0 collective-permute-done.1.refs_6_
  148.7 0.0 collective-permute-done.3.refs_8_
  148.7 0.0 copy-start.8
  148.7 0.0 collective-permute-done.4.refs_9_
  148.8 0.8 copy-done.9
  149.5 0.4 copy-done.8
  149.9 0.0 copy-start.5
  149.9 58.3 %relax.3 = (f32[2,3,4,256,256]{4,3,2,1,0:T(8,128)}, f32[4,136,256]{2,1,0:T(8,128)}) custom-call(s32[2]{0:T(128)} %pad_add_fusion.5.refs_0_, f32[8,3]{1,0:T(8,128)} %copy.8.refs_1_, f32[2]{0:T(128)} %add_convert_fusion.refs_2_.refs_1_, s32[2,4,256,256]{3,2,1,0:T(8,128)} %refs_3_.3, s32[4,256,256]{2,1,0:T(8,128)} %refs_4_.3, ...), custom_call_target="tpu_custom_call", output_to_operand_aliasing={{0}: (10, {})} | custom-call | flops 40000000 | bytes 40000000 | tf_op jit(solution)/shard_map/relax/pallas_call | solution.py:226
  208.3 0.0 copy-start.1
  208.3 0.0 copy-start.2
  208.3 0.0 collective-permute-done.9
  208.3 0.0 copy-done.5
  208.3 1.2 fusion.1.refs_3_
  209.5 1.9 collective-permute-start.11
  211.4 3.6 %collective-permute-start.10 = (f32[4,136,256]{2,1,0:T(8,128)S(1)}, f32[4,136,256]{2,1,0:T(8,128)S(1)}, u32[]{:S(2)}, u32[]{:S(2)}) collective-permute-start(f32[4,136,256]{2,1,0:T(8,128)S(1)} %fusion.1.refs_3_), channel_id=1, source_target_pairs={{0,1},{1,2},{2,3},{3,4},{4,5},{5,6},{6,7},{7,8},{8,9},{9,10},{10,1... | collective-permute-start | bytes 1671176 | tf_op jit(solution)/shard_map/ppermute | solution.py:388
  215.0 11.2 %collective-permute-done.11.refs_4_ = f32[4,136,256]{2,1,0:T(8,128)S(1)} collective-permute-done((f32[4,136,256]{2,1,0:T(8,128)S(1)}, f32[4,136,256]{2,1,0:T(8,128)S(1)}, u32[]{:S(2)}, u32[]{:S(2)}) %collective-permute-start.11) | collective-permute-done | bytes 557088 | tf_op jit(solution)/shard_map/ppermute | solution.py:389
  226.3 0.0 collective-permute-done.10.refs_2_
  226.3 0.0 copy-done.1
  226.3 0.0 copy-done.2
  226.3 41.0 %smooth.1 = f32[4,128,256]{2,1,0:T(8,128)} custom-call(s32[2]{0:T(128)S(1)} %copy-done.2, f32[2]{0:T(128)S(1)} %copy-done.1, f32[4,136,256]{2,1,0:T(8,128)S(1)} %collective-permute-done.10.refs_2_, f32[4,136,256]{2,1,0:T(8,128)S(1)} %fusion.1.refs_3_, f32[4,136,256]{2,1,0:T(8,128)S(1)} %collective-permute-done.11.refs_4_, f32[4,128,256]{2,1,0:T(8,128)S(1)} %copy-done), custom_call_target="tpu_custom_call" | custom-call | flops 5000000 | bytes 5000000 | tf_op jit(solution)/shard_map/smooth/pallas_call | solution.py:332
  (2 shorter events, 0.1 us)
Async XLA Ops:
  0.6 13.2 %collective-permute-start = (f32[4,128,256]{2,1,0:T(8,128)}, f32[4,128,256]{2,1,0:T(8,128)}, u32[]{:S(2)}, u32[]{:S(2)}) collective-permute-start(f32[4,128,256]{2,1,0:T(8,128)} %refs_5_.1), channel_id=1, source_target_pairs={{0,16},{16,0},{1,17},{17,1},{2,18},{18,2},{3,19},{19,3},{4,20},{20... | collective-permute-start | bytes 1572872 | tf_op jit(solution)/shard_map/ppermute | solution.py:357
  1.9 2.2 copy-start.3
  6.2 78.2 %collective-permute-start.7 = (s32[9,136,256]{2,1,0:T(8,128)}, s32[9,136,256]{2,1,0:T(8,128)}, u32[]{:S(2)}, u32[]{:S(2)}) collective-permute-start(s32[9,136,256]{2,1,0:T(8,128)} %pad_add_fusion.2), channel_id=1, source_target_pairs={{0,1},{1,2},{2,3},{3,4},{4,5},{5,6},{6,7},{7,8},{8,9},{9,10},{10,1... | collective-permute-start | bytes 3760136 | tf_op jit(solution)/shard_map/ppermute | solution.py:367
  10.2 3.1 %copy-start = (f32[4,128,256]{2,1,0:T(8,128)S(1)}, f32[4,128,256]{2,1,0:T(8,128)}, u32[]{:S(2)}) copy-start(f32[4,128,256]{2,1,0:T(8,128)} %refs_5_.1) | copy-start | bytes 1572868
  11.3 78.2 %collective-permute-start.8 = (s32[9,136,256]{2,1,0:T(8,128)}, s32[9,136,256]{2,1,0:T(8,128)}, u32[]{:S(2)}, u32[]{:S(2)}) collective-permute-start(s32[9,136,256]{2,1,0:T(8,128)} %pad_add_fusion.3), channel_id=1, source_target_pairs={{1,0},{2,1},{3,2},{4,3},{5,4},{6,5},{7,6},{8,7},{9,8},{10,9},{11,1... | collective-permute-start | bytes 3760136 | tf_op jit(solution)/shard_map/ppermute | solution.py:368
  15.2 49.6 %copy-start.6 = (f32[4,136,256]{2,1,0:T(8,128)}, f32[4,136,256]{2,1,0:T(8,128)S(1)}, u32[]{:S(2)}) copy-start(f32[4,136,256]{2,1,0:T(8,128)S(1)} %maximum_select_fusion.1.refs_5_) | copy-start | bytes 1671172
  15.2 49.5 %collective-permute-start.6 = (f32[4,136,256]{2,1,0:T(8,128)S(1)}, f32[4,136,256]{2,1,0:T(8,128)}, u32[]{:S(2)}, u32[]{:S(2)}) collective-permute-start(f32[4,136,256]{2,1,0:T(8,128)S(1)} %maximum_select_fusion.1.refs_5_), channel_id=1, source_target_pairs={{1,0},{2,1},{3,2},{4,3},{5,4},{6,5},{7,6},{8,7},{9,8},{10,9},{11,1... | collective-permute-start | bytes 1671176 | tf_op jit(solution)/shard_map/ppermute | solution.py:376
  18.7 4.2 %copy-start.7 = (s32[3,136,256]{2,1,0:T(8,128)S(1)}, s32[3,136,256]{2,1,0:T(8,128)}, u32[]{:S(2)}) copy-start(s32[3,136,256]{2,1,0:T(8,128)} %get-tuple-element.21) | copy-start | bytes 1253380
  19.8 128.9 %collective-permute-start.3 = (s32[9,136,256]{2,1,0:T(8,128)}, s32[9,136,256]{2,1,0:T(8,128)S(1)}, u32[]{:S(2)}, u32[]{:S(2)}) collective-permute-start(s32[9,136,256]{2,1,0:T(8,128)} %pad_add_fusion), channel_id=1, source_target_pairs={{0,1},{1,2},{2,3},{3,4},{4,5},{5,6},{6,7},{7,8},{8,9},{9,10},{10,1... | collective-permute-start | bytes 3760136 | tf_op jit(solution)/shard_map/ppermute | solution.py:367
  24.0 64.8 %copy-start.11 = (f32[8,3]{0,1:T(4,128)S(1)}, f32[8,3]{0,1:T(4,128)}, u32[]{:S(2)}) copy-start(f32[8,3]{0,1:T(4,128)} %param.7) | copy-start | bytes 292
  24.0 124.7 %collective-permute-start.4 = (s32[9,136,256]{2,1,0:T(8,128)}, s32[9,136,256]{2,1,0:T(8,128)}, u32[]{:S(2)}, u32[]{:S(2)}) collective-permute-start(s32[9,136,256]{2,1,0:T(8,128)} %pad_add_fusion.1), channel_id=1, source_target_pairs={{1,0},{2,1},{3,2},{4,3},{5,4},{6,5},{7,6},{8,7},{9,8},{10,9},{11,1... | collective-permute-start | bytes 3760136 | tf_op jit(solution)/shard_map/ppermute | solution.py:368
  64.7 17.7 %collective-permute-start.5 = (f32[4,136,256]{2,1,0:T(8,128)S(1)}, f32[4,136,256]{2,1,0:T(8,128)S(1)}, u32[]{:S(2)}, u32[]{:S(2)}) collective-permute-start(f32[4,136,256]{2,1,0:T(8,128)S(1)} %maximum_select_fusion.1.refs_5_), channel_id=1, source_target_pairs={{0,1},{1,2},{2,3},{3,4},{4,5},{5,6},{6,7},{7,8},{8,9},{9,10},{10,1... | collective-permute-start | bytes 1671176 | tf_op jit(solution)/shard_map/ppermute | solution.py:375
  68.8 79.0 %copy-start.4 = (f32[4,136,256]{2,1,0:T(8,128)}, f32[4,136,256]{2,1,0:T(8,128)S(1)}, u32[]{:S(2)}) copy-start(f32[4,136,256]{2,1,0:T(8,128)S(1)} %maximum_select_fusion.refs_5_) | copy-start | bytes 1671172
  82.5 1.9 copy-start.10
  82.5 66.2 %collective-permute-start.2 = (f32[4,136,256]{2,1,0:T(8,128)S(1)}, f32[4,136,256]{2,1,0:T(8,128)S(1)}, u32[]{:S(2)}, u32[]{:S(2)}) collective-permute-start(f32[4,136,256]{2,1,0:T(8,128)S(1)} %maximum_select_fusion.refs_5_), channel_id=1, source_target_pairs={{1,0},{2,1},{3,2},{4,3},{5,4},{6,5},{7,6},{8,7},{9,8},{10,9},{11,1... | collective-permute-start | bytes 1671176 | tf_op jit(solution)/shard_map/ppermute | solution.py:376
  84.4 64.3 %collective-permute-start.1 = (f32[4,136,256]{2,1,0:T(8,128)S(1)}, f32[4,136,256]{2,1,0:T(8,128)}, u32[]{:S(2)}, u32[]{:S(2)}) collective-permute-start(f32[4,136,256]{2,1,0:T(8,128)S(1)} %maximum_select_fusion.refs_5_), channel_id=1, source_target_pairs={{0,1},{1,2},{2,3},{3,4},{4,5},{5,6},{6,7},{7,8},{8,9},{9,10},{10,1... | collective-permute-start | bytes 1671176 | tf_op jit(solution)/shard_map/ppermute | solution.py:375
  147.7 60.5 %collective-permute-start.9 = (f32[4,136,256]{2,1,0:T(8,128)}, f32[4,136,256]{2,1,0:T(8,128)S(1)}, u32[]{:S(2)}, u32[]{:S(2)}) collective-permute-start(f32[4,136,256]{2,1,0:T(8,128)} %get-tuple-element.9), channel_id=1, source_target_pairs={{0,16},{16,0},{1,17},{17,1},{2,18},{18,2},{3,19},{19,3},{4,20},{20... | collective-permute-start | bytes 1671176 | tf_op jit(solution)/shard_map/ppermute | solution.py:384
  148.7 0.8 copy-start.9
  148.7 1.2 copy-start.8
  149.9 58.4 %copy-start.5 = (f32[4,136,256]{2,1,0:T(8,128)S(1)}, f32[4,136,256]{2,1,0:T(8,128)}, u32[]{:S(2)}) copy-start(f32[4,136,256]{2,1,0:T(8,128)} %copy-done.4) | copy-start | bytes 1671172
  208.3 18.0 %copy-start.1 = (f32[2]{0:T(128)S(1)}, f32[2]{0:T(128)}, u32[]{:S(2)}) copy-start(f32[2]{0:T(128)} %add_convert_fusion.refs_2_.refs_1_) | copy-start | bytes 28
  208.3 18.0 %copy-start.2 = (s32[2]{0:T(128)S(1)}, s32[2]{0:T(128)}, u32[]{:S(2)}) copy-start(s32[2]{0:T(128)} %pad_add_fusion.5.refs_0_) | copy-start | bytes 28
  209.5 16.8 %collective-permute-start.11 = (f32[4,136,256]{2,1,0:T(8,128)S(1)}, f32[4,136,256]{2,1,0:T(8,128)S(1)}, u32[]{:S(2)}, u32[]{:S(2)}) collective-permute-start(f32[4,136,256]{2,1,0:T(8,128)S(1)} %fusion.1.refs_3_), channel_id=1, source_target_pairs={{1,0},{2,1},{3,2},{4,3},{5,4},{6,5},{7,6},{8,7},{9,8},{10,9},{11,1... | collective-permute-start | bytes 1671176 | tf_op jit(solution)/shard_map/ppermute | solution.py:389
  211.4 14.9 %collective-permute-start.10 = (f32[4,136,256]{2,1,0:T(8,128)S(1)}, f32[4,136,256]{2,1,0:T(8,128)S(1)}, u32[]{:S(2)}, u32[]{:S(2)}) collective-permute-start(f32[4,136,256]{2,1,0:T(8,128)S(1)} %fusion.1.refs_3_), channel_id=1, source_target_pairs={{0,1},{1,2},{2,3},{3,4},{4,5},{5,6},{6,7},{7,8},{8,9},{9,10},{10,1... | collective-permute-start | bytes 1671176 | tf_op jit(solution)/shard_map/ppermute | solution.py:388

commit v2 on v1

--- a/solution.py
+++ b/solution.py
@@ -28,9 +28,24 @@
 A1 = 1.0 + ALPHA2 + B2 / B1 - B2
 RATIO = B2 / B1
 
+UM = 17
+U0 = 17
+U1 = 17
+U2 = 17
+UE = 17
+UF = 8
 HALO = 4
 EXTRA = 8
 PAD = 8
+
+
+def sweep_rows(count, tiles, body, unroll):
+    def outer(p, carry):
+        def inner(j, c):
+            body(p, pl.multiple_of(j * 8, 8))
+            return c
+        return lax.fori_loop(0, tiles, inner, carry, unroll=unroll)
+    lax.fori_loop(0, count, outer, 0)
 
 
 def step_kernel(planes, rows, info, table, valid, loads, support, mid, lo_d, hi_d, lo_i, hi_i, *rest):
@@ -66,16 +81,14 @@
         clear(6 * (planes + 2), u_v)
 
     def modulus(source, first, count, scale):
-        def body(i, carry):
-            p, r = i // tiles, pl.multiple_of(i % tiles * 8, 8)
+        def body(p, r):
             for z in range(2):
                 d = source[p, pl.ds(r, 8), pl.ds(128 * z, 128)]
                 m = E_MIN + d * d * d * (1.0 - E_MIN)
                 if scale is not None:
                     m = m * scale
                 m_v[first + p, z, pl.ds(PAD + r, 8), :] = m
-            return carry
-        lax.fori_loop(0, count * tiles, body, 0)
+        sweep_rows(count, tiles, body, UM)
 
     modulus(lo_d, 0, 4, vlo)
     modulus(mid, 4, planes, None)
@@ -98,8 +111,7 @@
     for copy in copies:
         copy.wait()
 
-    def first(i, carry):
-        p, r = i // tiles, pl.multiple_of(i % tiles * 8, 8)
+    def first(p, r):
         row = PAD + r
         m = get(m_v, p + 1, row)
         zup, zdn = above(m), below(m)
@@ -130,9 +142,8 @@
                     q = [jnp.where(b0, table[2 * j + 1, c], table[2 * j, c]) for j in range(4)]
                     f = jnp.where(b2, jnp.where(b1, q[3], q[2]), jnp.where(b1, q[1], q[0]))
                     s0_v[p * 6 + case * 3 + c, z, pl.ds(row, 8), :] = f * scale[z]
-        return carry
-
-    lax.fori_loop(0, wide * tiles, first, 0)
+
+    sweep_rows(wide, tiles, first, U0)
 
     def stencil(ref, at, row, k):
         c = get(ref, at, row)
@@ -143,20 +154,17 @@
             out.append(((t[0] + t[1]) + (t[2] + t[3])) + (t[4] + t[5]))
         return c, out
 
-    def second(i, carry):
-        p, r = i // tiles, pl.multiple_of(i % tiles * 8, 8)
+    def second(p, r):
         row = PAD + r
         k = [[k_v[p + 1, j, z, pl.ds(r, 8), :] for z in range(2)] for j in range(6)]
         for f in range(6):
             c, t = stencil(s0_v, (p + 1) * 6 + f, row, k)
             for z in range(2):
                 s1_v[p * 6 + f, z, pl.ds(row, 8), :] = G0 * c[z] + t[z]
-        return carry
-
-    lax.fori_loop(0, (planes + 4) * tiles, second, 0)
-
-    def third(i, carry):
-        p, r = i // tiles, pl.multiple_of(i % tiles * 8, 8)
+
+    sweep_rows((planes + 4), tiles, second, U1)
+
+    def third(p, r):
         row = PAD + r
         k = [[k_v[p + 2, j, z, pl.ds(r, 8), :] for z in range(2)] for j in range(6)]
         for f in range(6):
@@ -164,9 +172,8 @@
             base = get(s0_v, (p + 2) * 6 + f, row)
             for z in range(2):
                 u_v[p * 6 + f, z, pl.ds(row, 8), :] = (A0 / RATIO) * base[z] + (A1 / RATIO) * c[z] + t[z]
-        return carry
-
-    lax.fori_loop(0, (planes + 2) * tiles, third, 0)
+
+    sweep_rows((planes + 2), tiles, third, U2)
 
     half = rows - EXTRA
     skip = pl.multiple_of(h * EXTRA, 8)
@@ -181,8 +188,7 @@
     for copy in outs:
         copy.start()
 
-    def energy(i, carry):
-        p, r = i // tiles, pl.multiple_of(i % tiles * 8, 8)
+    def energy(p, r):
         row = PAD + r
         acc = [jnp.zeros((8, 128), jnp.float32) for _ in range(2)]
         for f in range(6):
@@ -197,9 +203,8 @@
                     acc[z] = acc[z] + d * d
         for z in range(2):
             e_out[p, pl.ds(r, 8), pl.ds(128 * z, 128)] = 0.5 * acc[z]
-        return carry
-
-    lax.fori_loop(0, planes * tiles, energy, 0)
+
+    sweep_rows(planes, tiles, energy, UE)
     for copy in outs:
         copy.wait()
 
@@ -265,13 +270,11 @@
     lax.fori_loop(0, planes + 8, clear, 0)
 
     def fill(source, first, count):
-        def body(i, carry):
-            p, r = i // tiles, pl.multiple_of(i % tiles * 8, 8)
+        def body(p, r):
             for z in range(2):
                 r_v[first + p, z, pl.ds(PAD + r, 8), :] = source[p, pl.ds(r, 8), pl.ds(128 * z, 128)]
-            return carry
-
-        lax.fori_loop(0, count * tiles, body, 0)
+
+        sweep_rows(count, tiles, body, UM)
 
     fill(lo, 0, 4)
     fill(mid, 4, planes)
@@ -295,14 +298,13 @@
         return new
 
     def sweep(src, dst, low, high):
-        def body(i, carry):
-            p, row = low + i // tiles, pl.multiple_of(PAD + i % tiles * 8, 8)
+        def body(p, r):
+            p, row = low + p, PAD + r
             new = smoothed(src, p, row)
             for z in range(2):
                 dst[p, z, pl.ds(row, 8), :] = new[z]
-            return carry
-
-        lax.fori_loop(0, (high - low) * tiles, body, 0)
+
+        sweep_rows((high - low), tiles, body, UF)
 
     sweep(r_v, a_v, 1, planes + 7)
     sweep(a_v, b_v, 2, planes + 6)
@@ -310,14 +312,12 @@
 
     skip = h * EXTRA
 
-    def last(i, carry):
-        p, r = i // (half // 8), pl.multiple_of(i % (half // 8) * 8, 8)
+    def last(p, r):
         new = smoothed(a_v, p + 4, pl.multiple_of(PAD + r + skip, 8))
         for z in range(2):
             out[p, pl.ds(r, 8), pl.ds(128 * z, 128)] = new[z] / dens[p, pl.ds(r, 8), pl.ds(128 * z, 128)]
-        return carry
-
-    lax.fori_loop(0, planes * (half // 8), last, 0)
+
+    sweep_rows(planes, half // 8, last, UF)
 
 
 def smooth(h, gap, valid, lo, mid, hi, dens):

time: 268 us -> 159 us (0.59)
  Pallas kernels: 158 us -> 48.4 us
    pallas_call x2, Pallas kernels: 117 us -> 39.2 us  [step(): pl.pallas_call(kernel, out_shape=(jax.ShapeDtypeStruct((2, 3, planes, ful...]
    pallas_call x1, Pallas kernels: 41 us -> 9.14 us  [smooth(): pl.pallas_call(kernel, out_shape=jax.ShapeDtypeStruct(dens.shape, f32), i...]
  transfers between devices with their start and end apart: 12 -> 12, of which waited for: 4 -> 4; matrix products, arithmetic and copies ran while one was open for 5% -> 8% of each run, Pallas kernels for 44% -> 25%
where the time goes in v2:
time: 159 us; the launch traced here: 158 us
  waiting for transfers between devices  64.2 us (40%)
  Pallas kernels  48.4 us (30%)
  starting transfers between devices  29.8 us (19%)
  other arithmetic  9.12 us (6%)
  local copies, waits for them, and re-layouts  5.78 us (4%)
    pallas_call x2, Pallas kernels, step(): pl.pallas_call(kernel, out_shape=(jax.ShapeDtypeStruct((2, 3, planes, ful...  39.2 us
    ppermute x2, waiting for transfers between devices, densities(): hi_d = lax.ppermute(mid[:4], 'slab', fall)  38.6 us
    ppermute x2, waiting for transfers between devices, densities(): lo_d = lax.ppermute(mid[planes - 4:], 'slab', rise)  13.7 us
    ppermute x1, waiting for transfers between devices, local(): hi_r = lax.ppermute(right[:4], 'slab', fall)  11.2 us
    pallas_call x1, Pallas kernels, smooth(): pl.pallas_call(kernel, out_shape=jax.ShapeDtypeStruct(dens.shape, f32), i...  9.14 us
    ppermute x2, starting transfers between devices, window(): lo_i = lax.ppermute(pack(planes - 3, planes), 'slab', rise)  7.01 us
    ppermute x2, starting transfers between devices, densities(): lo_d = lax.ppermute(mid[planes - 4:], 'slab', rise)  6.3 us
    ppermute x2, starting transfers between devices, densities(): hi_d = lax.ppermute(mid[:4], 'slab', fall)  5.36 us
  transfers between devices with their start and end apart: 12, of which 4 were waited for; matrix products, arithmetic and copies ran while one was open for 8% of the time, Pallas kernels for 25%

profile of v2, /device:TPU:9, one launch (start us, length us, event | category | flops | bytes accessed | tf_op | source)
XLA Modules:
  0.0 158.1 jit_solution(12536949846373432761)
XLA Ops:
  0.6 1.3 collective-permute-start
  1.9 0.0 copy-start.3
  1.9 2.2 %dynamic-slice_bitcast_fusion.1 = (s32[3,136,256]{2,1,0:T(8,128)S(1)}, s32[3,136,256]{2,1,0:T(8,128)S(1)}, s32[3,136,256]{2,1,0:T(8,128)S(1)}, s32[3,136,256]{2,...) fusion(s32[2,4,256,256]{3,2,1,0:T(8,128)} %refs_3_.3, ...), kind=kLoop, calls=%fused_computation.10 | loop fusion | bytes 6684684 | tf_op jit(solution)/shard_map/squeeze | solution.py:365
  4.1 0.0 copy-done.3
  4.1 0.9 constant_dynamic-slice_fusion.2
  5.0 1.2 pad_add_fusion.2
  6.2 4.0 %collective-permute-start.7 = (s32[9,136,256]{2,1,0:T(8,128)}, s32[9,136,256]{2,1,0:T(8,128)}, u32[]{:S(2)}, u32[]{:S(2)}) collective-permute-start(s32[9,136,256]{2,1,0:T(8,128)} %pad_add_fusion.2), channel_id=1, source_target_pairs={{0,1},{1,2},{2,3},{3,4},{4,5},{5,6},{6,7},{7,8},{8,9},{9,10},{10,1... | collective-permute-start | bytes 3760136 | tf_op jit(solution)/shard_map/ppermute | solution.py:367
  10.2 0.0 copy-start
  10.2 1.2 pad_add_fusion.3
  11.3 1.9 %collective-permute-start.8 = (s32[9,136,256]{2,1,0:T(8,128)}, s32[9,136,256]{2,1,0:T(8,128)}, u32[]{:S(2)}, u32[]{:S(2)}) collective-permute-start(s32[9,136,256]{2,1,0:T(8,128)} %pad_add_fusion.3), channel_id=1, source_target_pairs={{1,0},{2,1},{3,2},{4,3},{5,4},{6,5},{7,6},{8,7},{9,8},{10,9},{11,1... | collective-permute-start | bytes 3760136 | tf_op jit(solution)/shard_map/ppermute | solution.py:368
  13.2 0.0 copy-done
  13.3 0.5 collective-permute-done
  13.8 1.4 maximum_select_fusion.1.refs_5_
  15.2 0.0 copy-start.6
  15.2 3.5 %collective-permute-start.6 = (f32[4,136,256]{2,1,0:T(8,128)S(1)}, f32[4,136,256]{2,1,0:T(8,128)}, u32[]{:S(2)}, u32[]{:S(2)}) collective-permute-start(f32[4,136,256]{2,1,0:T(8,128)S(1)} %maximum_select_fusion.1.refs_5_), channel_id=1, source_target_pairs={{1,0},{2,1},{3,2},{4,3},{5,4},{6,5},{7,6},{8,7},{9,8},{10,9},{11,1... | collective-permute-start | bytes 1671176 | tf_op jit(solution)/shard_map/ppermute | solution.py:376
  18.7 0.0 copy-start.7
  18.7 1.2 pad_add_fusion
  19.8 3.0 %collective-permute-start.3 = (s32[9,136,256]{2,1,0:T(8,128)}, s32[9,136,256]{2,1,0:T(8,128)S(1)}, u32[]{:S(2)}, u32[]{:S(2)}) collective-permute-start(s32[9,136,256]{2,1,0:T(8,128)} %pad_add_fusion), channel_id=1, source_target_pairs={{0,1},{1,2},{2,3},{3,4},{4,5},{5,6},{6,7},{7,8},{8,9},{9,10},{10,1... | collective-permute-start | bytes 3760136 | tf_op jit(solution)/shard_map/ppermute | solution.py:367
  22.9 0.0 copy-done.7
  22.9 1.1 pad_add_fusion.1
  24.0 0.0 copy-start.11
  24.0 2.0 %collective-permute-start.4 = (s32[9,136,256]{2,1,0:T(8,128)}, s32[9,136,256]{2,1,0:T(8,128)}, u32[]{:S(2)}, u32[]{:S(2)}) collective-permute-start(s32[9,136,256]{2,1,0:T(8,128)} %pad_add_fusion.1), channel_id=1, source_target_pairs={{1,0},{2,1},{3,2},{4,3},{5,4},{6,5},{7,6},{8,7},{9,8},{10,9},{11,1... | collective-permute-start | bytes 3760136 | tf_op jit(solution)/shard_map/ppermute | solution.py:368
  26.1 38.6 %collective-permute-done.6.refs_7_ = f32[4,136,256]{2,1,0:T(8,128)} collective-permute-done((f32[4,136,256]{2,1,0:T(8,128)S(1)}, f32[4,136,256]{2,1,0:T(8,128)}, u32[]{:S(2)}, u32[]{:S(2)}) %collective-permute-start.6) | collective-permute-done | bytes 557088 | tf_op jit(solution)/shard_map/ppermute | solution.py:376
  64.7 0.0 copy-done.6
  64.7 1.9 %collective-permute-start.5 = (f32[4,136,256]{2,1,0:T(8,128)S(1)}, f32[4,136,256]{2,1,0:T(8,128)S(1)}, u32[]{:S(2)}, u32[]{:S(2)}) collective-permute-start(f32[4,136,256]{2,1,0:T(8,128)S(1)} %maximum_select_fusion.1.refs_5_), channel_id=1, source_target_pairs={{0,1},{1,2},{2,3},{3,4},{4,5},{5,6},{6,7},{7,8},{8,9},{9,10},{10,1... | collective-permute-start | bytes 1671176 | tf_op jit(solution)/shard_map/ppermute | solution.py:375
  66.7 0.7 add_convert_fusion.refs_2_.refs_1_
  67.3 0.6 pad_add_fusion.4.refs_0_
  67.9 0.8 fusion.3
  68.8 0.0 copy-start.4
  68.8 13.7 %collective-permute-done.5.refs_6_ = f32[4,136,256]{2,1,0:T(8,128)S(1)} collective-permute-done((f32[4,136,256]{2,1,0:T(8,128)S(1)}, f32[4,136,256]{2,1,0:T(8,128)S(1)}, u32[]{:S(2)}, u32[]{:S(2)}) %collective-permute-start.5) | collective-permute-done | bytes 557088 | tf_op jit(solution)/shard_map/ppermute | solution.py:375
  82.5 0.0 copy-start.10
  82.5 1.9 %collective-permute-start.2 = (f32[4,136,256]{2,1,0:T(8,128)S(1)}, f32[4,136,256]{2,1,0:T(8,128)S(1)}, u32[]{:S(2)}, u32[]{:S(2)}) collective-permute-start(f32[4,136,256]{2,1,0:T(8,128)S(1)} %maximum_select_fusion.refs_5_), channel_id=1, source_target_pairs={{1,0},{2,1},{3,2},{4,3},{5,4},{6,5},{7,6},{8,7},{9,8},{10,9},{11,1... | collective-permute-start | bytes 1671176 | tf_op jit(solution)/shard_map/ppermute | solution.py:376
  84.4 0.0 copy-done.10
  84.4 0.0 collective-permute-done.7.refs_8_
  84.4 4.4 %collective-permute-start.1 = (f32[4,136,256]{2,1,0:T(8,128)S(1)}, f32[4,136,256]{2,1,0:T(8,128)}, u32[]{:S(2)}, u32[]{:S(2)}) collective-permute-start(f32[4,136,256]{2,1,0:T(8,128)S(1)} %maximum_select_fusion.refs_5_), channel_id=1, source_target_pairs={{0,1},{1,2},{2,3},{3,4},{4,5},{5,6},{6,7},{7,8},{8,9},{9,10},{10,1... | collective-permute-start | bytes 1671176 | tf_op jit(solution)/shard_map/ppermute | solution.py:375
  88.8 0.0 copy-done.11
  88.8 0.7 copy.8.refs_1_
  89.5 0.0 collective-permute-done.8.refs_9_
  89.5 19.6 %relax.2 = (f32[2,3,4,256,256]{4,3,2,1,0:T(8,128)}, f32[4,136,256]{2,1,0:T(8,128)}) custom-call(s32[2]{0:T(128)} %pad_add_fusion.4.refs_0_, f32[8,3]{1,0:T(8,128)} %copy.8.refs_1_, f32[2]{0:T(128)} %add_convert_fusion.refs_2_.refs_1_, s32[2,4,256,256]{3,2,1,0:T(8,128)} %refs_3_.3, s32[4,256,256]{2,1,0:T(8,128)} %refs_4_.3, f32[4,136,256]{2,1,0:T(8,128)} %copy-done.6, ...), custom_call_target="tpu_custom_call" | custom-call | flops 40000000 | bytes 40000000 | tf_op jit(solution)/shard_map/relax/pallas_call | solution.py:231
  109.1 0.0 copy-done.4
  109.1 0.3 collective-permute-start.9
  109.4 0.7 pad_add_fusion.5.refs_0_
  110.1 0.0 collective-permute-done.2.refs_7_
  110.1 0.0 copy-start.9
  110.1 0.0 collective-permute-done.1.refs_6_
  110.1 0.0 collective-permute-done.3.refs_8_
  110.1 0.0 copy-start.8
  110.1 0.0 collective-permute-done.4.refs_9_
  110.1 0.8 copy-done.9
  110.9 0.4 copy-done.8
  111.3 0.0 copy-start.5
  111.3 19.7 %relax.3 = (f32[2,3,4,256,256]{4,3,2,1,0:T(8,128)}, f32[4,136,256]{2,1,0:T(8,128)}) custom-call(s32[2]{0:T(128)} %pad_add_fusion.5.refs_0_, f32[8,3]{1,0:T(8,128)} %copy.8.refs_1_, f32[2]{0:T(128)} %add_convert_fusion.refs_2_.refs_1_, s32[2,4,256,256]{3,2,1,0:T(8,128)} %refs_3_.3, s32[4,256,256]{2,1,0:T(8,128)} %refs_4_.3, ...), custom_call_target="tpu_custom_call", output_to_operand_aliasing={{0}: (10, {})} | custom-call | flops 40000000 | bytes 40000000 | tf_op jit(solution)/shard_map/relax/pallas_call | solution.py:231
  131.0 0.0 copy-start.1
  131.0 0.0 copy-start.2
  131.0 0.0 collective-permute-done.9
  131.0 0.0 copy-done.5
  131.0 1.2 fusion.1.refs_3_
  132.2 1.9 %collective-permute-start.11 = (f32[4,136,256]{2,1,0:T(8,128)S(1)}, f32[4,136,256]{2,1,0:T(8,128)S(1)}, u32[]{:S(2)}, u32[]{:S(2)}) collective-permute-start(f32[4,136,256]{2,1,0:T(8,128)S(1)} %fusion.1.refs_3_), channel_id=1, source_target_pairs={{1,0},{2,1},{3,2},{4,3},{5,4},{6,5},{7,6},{8,7},{9,8},{10,9},{11,1... | collective-permute-start | bytes 1671176 | tf_op jit(solution)/shard_map/ppermute | solution.py:389
  134.1 3.6 %collective-permute-start.10 = (f32[4,136,256]{2,1,0:T(8,128)S(1)}, f32[4,136,256]{2,1,0:T(8,128)S(1)}, u32[]{:S(2)}, u32[]{:S(2)}) collective-permute-start(f32[4,136,256]{2,1,0:T(8,128)S(1)} %fusion.1.refs_3_), channel_id=1, source_target_pairs={{0,1},{1,2},{2,3},{3,4},{4,5},{5,6},{6,7},{7,8},{8,9},{9,10},{10,1... | collective-permute-start | bytes 1671176 | tf_op jit(solution)/shard_map/ppermute | solution.py:388
  137.7 11.2 %collective-permute-done.11.refs_4_ = f32[4,136,256]{2,1,0:T(8,128)S(1)} collective-permute-done((f32[4,136,256]{2,1,0:T(8,128)S(1)}, f32[4,136,256]{2,1,0:T(8,128)S(1)}, u32[]{:S(2)}, u32[]{:S(2)}) %collective-permute-start.11) | collective-permute-done | bytes 557088 | tf_op jit(solution)/shard_map/ppermute | solution.py:389
  149.0 0.0 collective-permute-done.10.refs_2_
  149.0 0.0 copy-done.1
  149.0 0.0 copy-done.2
  149.0 9.1 %smooth.1 = f32[4,128,256]{2,1,0:T(8,128)} custom-call(s32[2]{0:T(128)S(1)} %copy-done.2, f32[2]{0:T(128)S(1)} %copy-done.1, f32[4,136,256]{2,1,0:T(8,128)S(1)} %collective-permute-done.10.refs_2_, f32[4,136,256]{2,1,0:T(8,128)S(1)} %fusion.1.refs_3_, f32[4,136,256]{2,1,0:T(8,128)S(1)} %collective-permute-done.11.refs_4_, f32[4,128,256]{2,1,0:T(8,128)S(1)} %copy-done), custom_call_target="tpu_custom_call" | custom-call | flops 5000000 | bytes 5000000 | tf_op jit(solution)/shard_map/smooth/pallas_call | solution.py:332
  (2 shorter events, 0.1 us)
Async XLA Ops:
  0.6 13.2 %collective-permute-start = (f32[4,128,256]{2,1,0:T(8,128)}, f32[4,128,256]{2,1,0:T(8,128)}, u32[]{:S(2)}, u32[]{:S(2)}) collective-permute-start(f32[4,128,256]{2,1,0:T(8,128)} %refs_5_.1), channel_id=1, source_target_pairs={{0,16},{16,0},{1,17},{17,1},{2,18},{18,2},{3,19},{19,3},{4,20},{20... | collective-permute-start | bytes 1572872 | tf_op jit(solution)/shard_map/ppermute | solution.py:357
  1.9 2.2 %copy-start.3 = (s32[4,256,256]{2,1,0:T(8,128)S(1)}, s32[4,256,256]{2,1,0:T(8,128)}, u32[]{:S(2)}) copy-start(s32[4,256,256]{2,1,0:T(8,128)} %refs_4_.3) | copy-start | bytes 3145732
  6.2 78.2 %collective-permute-start.7 = (s32[9,136,256]{2,1,0:T(8,128)}, s32[9,136,256]{2,1,0:T(8,128)}, u32[]{:S(2)}, u32[]{:S(2)}) collective-permute-start(s32[9,136,256]{2,1,0:T(8,128)} %pad_add_fusion.2), channel_id=1, source_target_pairs={{0,1},{1,2},{2,3},{3,4},{4,5},{5,6},{6,7},{7,8},{8,9},{9,10},{10,1... | collective-permute-start | bytes 3760136 | tf_op jit(solution)/shard_map/ppermute | solution.py:367
  10.2 3.1 %copy-start = (f32[4,128,256]{2,1,0:T(8,128)S(1)}, f32[4,128,256]{2,1,0:T(8,128)}, u32[]{:S(2)}) copy-start(f32[4,128,256]{2,1,0:T(8,128)} %refs_5_.1) | copy-start | bytes 1572868
  11.3 78.2 %collective-permute-start.8 = (s32[9,136,256]{2,1,0:T(8,128)}, s32[9,136,256]{2,1,0:T(8,128)}, u32[]{:S(2)}, u32[]{:S(2)}) collective-permute-start(s32[9,136,256]{2,1,0:T(8,128)} %pad_add_fusion.3), channel_id=1, source_target_pairs={{1,0},{2,1},{3,2},{4,3},{5,4},{6,5},{7,6},{8,7},{9,8},{10,9},{11,1... | collective-permute-start | bytes 3760136 | tf_op jit(solution)/shard_map/ppermute | solution.py:368
  15.2 49.6 %copy-start.6 = (f32[4,136,256]{2,1,0:T(8,128)}, f32[4,136,256]{2,1,0:T(8,128)S(1)}, u32[]{:S(2)}) copy-start(f32[4,136,256]{2,1,0:T(8,128)S(1)} %maximum_select_fusion.1.refs_5_) | copy-start | bytes 1671172
  15.2 49.5 %collective-permute-start.6 = (f32[4,136,256]{2,1,0:T(8,128)S(1)}, f32[4,136,256]{2,1,0:T(8,128)}, u32[]{:S(2)}, u32[]{:S(2)}) collective-permute-start(f32[4,136,256]{2,1,0:T(8,128)S(1)} %maximum_select_fusion.1.refs_5_), channel_id=1, source_target_pairs={{1,0},{2,1},{3,2},{4,3},{5,4},{6,5},{7,6},{8,7},{9,8},{10,9},{11,1... | collective-permute-start | bytes 1671176 | tf_op jit(solution)/shard_map/ppermute | solution.py:376
  18.7 4.2 %copy-start.7 = (s32[3,136,256]{2,1,0:T(8,128)S(1)}, s32[3,136,256]{2,1,0:T(8,128)}, u32[]{:S(2)}) copy-start(s32[3,136,256]{2,1,0:T(8,128)} %get-tuple-element.21) | copy-start | bytes 1253380
  19.8 90.2 %collective-permute-start.3 = (s32[9,136,256]{2,1,0:T(8,128)}, s32[9,136,256]{2,1,0:T(8,128)S(1)}, u32[]{:S(2)}, u32[]{:S(2)}) collective-permute-start(s32[9,136,256]{2,1,0:T(8,128)} %pad_add_fusion), channel_id=1, source_target_pairs={{0,1},{1,2},{2,3},{3,4},{4,5},{5,6},{6,7},{7,8},{8,9},{9,10},{10,1... | collective-permute-start | bytes 3760136 | tf_op jit(solution)/shard_map/ppermute | solution.py:367
  24.0 64.8 %copy-start.11 = (f32[8,3]{0,1:T(4,128)S(1)}, f32[8,3]{0,1:T(4,128)}, u32[]{:S(2)}) copy-start(f32[8,3]{0,1:T(4,128)} %param.7) | copy-start | bytes 292
  24.0 86.1 %collective-permute-start.4 = (s32[9,136,256]{2,1,0:T(8,128)}, s32[9,136,256]{2,1,0:T(8,128)}, u32[]{:S(2)}, u32[]{:S(2)}) collective-permute-start(s32[9,136,256]{2,1,0:T(8,128)} %pad_add_fusion.1), channel_id=1, source_target_pairs={{1,0},{2,1},{3,2},{4,3},{5,4},{6,5},{7,6},{8,7},{9,8},{10,9},{11,1... | collective-permute-start | bytes 3760136 | tf_op jit(solution)/shard_map/ppermute | solution.py:368
  64.7 17.7 %collective-permute-start.5 = (f32[4,136,256]{2,1,0:T(8,128)S(1)}, f32[4,136,256]{2,1,0:T(8,128)S(1)}, u32[]{:S(2)}, u32[]{:S(2)}) collective-permute-start(f32[4,136,256]{2,1,0:T(8,128)S(1)} %maximum_select_fusion.1.refs_5_), channel_id=1, source_target_pairs={{0,1},{1,2},{2,3},{3,4},{4,5},{5,6},{6,7},{7,8},{8,9},{9,10},{10,1... | collective-permute-start | bytes 1671176 | tf_op jit(solution)/shard_map/ppermute | solution.py:375
  68.8 40.3 %copy-start.4 = (f32[4,136,256]{2,1,0:T(8,128)}, f32[4,136,256]{2,1,0:T(8,128)S(1)}, u32[]{:S(2)}) copy-start(f32[4,136,256]{2,1,0:T(8,128)S(1)} %maximum_select_fusion.refs_5_) | copy-start | bytes 1671172
  82.5 1.9 %copy-start.10 = (f32[4,136,256]{2,1,0:T(8,128)}, f32[4,136,256]{2,1,0:T(8,128)S(1)}, u32[]{:S(2)}) copy-start(f32[4,136,256]{2,1,0:T(8,128)S(1)} %collective-permute-done.5.refs_6_) | copy-start | bytes 1671172
  82.5 27.6 %collective-permute-start.2 = (f32[4,136,256]{2,1,0:T(8,128)S(1)}, f32[4,136,256]{2,1,0:T(8,128)S(1)}, u32[]{:S(2)}, u32[]{:S(2)}) collective-permute-start(f32[4,136,256]{2,1,0:T(8,128)S(1)} %maximum_select_fusion.refs_5_), channel_id=1, source_target_pairs={{1,0},{2,1},{3,2},{4,3},{5,4},{6,5},{7,6},{8,7},{9,8},{10,9},{11,1... | collective-permute-start | bytes 1671176 | tf_op jit(solution)/shard_map/ppermute | solution.py:376
  84.4 25.7 %collective-permute-start.1 = (f32[4,136,256]{2,1,0:T(8,128)S(1)}, f32[4,136,256]{2,1,0:T(8,128)}, u32[]{:S(2)}, u32[]{:S(2)}) collective-permute-start(f32[4,136,256]{2,1,0:T(8,128)S(1)} %maximum_select_fusion.refs_5_), channel_id=1, source_target_pairs={{0,1},{1,2},{2,3},{3,4},{4,5},{5,6},{6,7},{7,8},{8,9},{9,10},{10,1... | collective-permute-start | bytes 1671176 | tf_op jit(solution)/shard_map/ppermute | solution.py:375
  109.1 21.9 %collective-permute-start.9 = (f32[4,136,256]{2,1,0:T(8,128)}, f32[4,136,256]{2,1,0:T(8,128)S(1)}, u32[]{:S(2)}, u32[]{:S(2)}) collective-permute-start(f32[4,136,256]{2,1,0:T(8,128)} %get-tuple-element.9), channel_id=1, source_target_pairs={{0,16},{16,0},{1,17},{17,1},{2,18},{18,2},{3,19},{19,3},{4,20},{20... | collective-permute-start | bytes 1671176 | tf_op jit(solution)/shard_map/ppermute | solution.py:384
  110.1 0.8 copy-start.9
  110.1 1.2 copy-start.8
  111.3 19.7 %copy-start.5 = (f32[4,136,256]{2,1,0:T(8,128)S(1)}, f32[4,136,256]{2,1,0:T(8,128)}, u32[]{:S(2)}) copy-start(f32[4,136,256]{2,1,0:T(8,128)} %copy-done.4) | copy-start | bytes 1671172
  131.0 18.0 %copy-start.1 = (f32[2]{0:T(128)S(1)}, f32[2]{0:T(128)}, u32[]{:S(2)}) copy-start(f32[2]{0:T(128)} %add_convert_fusion.refs_2_.refs_1_) | copy-start | bytes 28
  131.0 18.0 %copy-start.2 = (s32[2]{0:T(128)S(1)}, s32[2]{0:T(128)}, u32[]{:S(2)}) copy-start(s32[2]{0:T(128)} %pad_add_fusion.5.refs_0_) | copy-start | bytes 28
  132.2 16.8 %collective-permute-start.11 = (f32[4,136,256]{2,1,0:T(8,128)S(1)}, f32[4,136,256]{2,1,0:T(8,128)S(1)}, u32[]{:S(2)}, u32[]{:S(2)}) collective-permute-start(f32[4,136,256]{2,1,0:T(8,128)S(1)} %fusion.1.refs_3_), channel_id=1, source_target_pairs={{1,0},{2,1},{3,2},{4,3},{5,4},{6,5},{7,6},{8,7},{9,8},{10,9},{11,1... | collective-permute-start | bytes 1671176 | tf_op jit(solution)/shard_map/ppermute | solution.py:389
  134.1 14.9 %collective-permute-start.10 = (f32[4,136,256]{2,1,0:T(8,128)S(1)}, f32[4,136,256]{2,1,0:T(8,128)S(1)}, u32[]{:S(2)}, u32[]{:S(2)}) collective-permute-start(f32[4,136,256]{2,1,0:T(8,128)S(1)} %fusion.1.refs_3_), channel_id=1, source_target_pairs={{0,1},{1,2},{2,3},{3,4},{4,5},{5,6},{6,7},{7,8},{8,9},{9,10},{10,1... | collective-permute-start | bytes 1671176 | tf_op jit(solution)/shard_map/ppermute | solution.py:388

commit v3 on v2

--- a/solution.py
+++ b/solution.py
@@ -48,14 +48,24 @@
     lax.fori_loop(0, count, outer, 0)
 
 
-def step_kernel(planes, rows, info, table, valid, loads, support, mid, lo_d, hi_d, lo_i, hi_i, *rest):
-    (u_out, e_out, idx_v, sup_v, m_v, k_v, s0_v, s1_v, u_v, in_sem, out_sem) = rest[-11:]
+def step_kernel(planes, rows, info, table, valid, loads, support, lo_d, mid, hi_d, lo_x, mid_x, hi_x, lo_i, hi_i, *rest):
+    (u_out, e_out, d_v, idx_v, sup_v, m_v, k_v, s0_v, s1_v, u_v, in_sem, out_sem) = rest[-12:]
     tiles = rows // 8
     h = info[0]
     vlo, vhi = valid[0], valid[1]
     start = pl.multiple_of(h * info[1], 8)
     wide = planes + 6
+    half = rows - EXTRA
+    skip = pl.multiple_of(h * EXTRA, 8)
     copies = []
+    for j, (own, other, first_p, count_p) in enumerate((
+            (lo_d, lo_x, 0, 4), (mid, mid_x, 4, planes), (hi_d, hi_x, planes + 4, 4))):
+        copies.append(pltpu.make_async_copy(
+            own, d_v.at[pl.ds(first_p, count_p), pl.ds(skip, half), :], in_sem.at[9 + 2 * j]))
+        copies.append(pltpu.make_async_copy(
+            other.at[:, pl.ds(pl.multiple_of(h * (half - EXTRA), 8), EXTRA), :],
+            d_v.at[pl.ds(first_p, count_p), pl.ds(pl.multiple_of((1 - h) * half, 8), EXTRA), :], in_sem.at[10 + 2 * j]))
+    densities = len(copies)
     for case in range(2):
         copies.append(pltpu.make_async_copy(
             loads.at[case, :, pl.ds(start, rows), :], idx_v.at[case, pl.ds(3, planes)], in_sem.at[case]))
@@ -80,19 +90,16 @@
         clear(6 * (planes + 4), s1_v)
         clear(6 * (planes + 2), u_v)
 
-    def modulus(source, first, count, scale):
-        def body(p, r):
-            for z in range(2):
-                d = source[p, pl.ds(r, 8), pl.ds(128 * z, 128)]
-                m = E_MIN + d * d * d * (1.0 - E_MIN)
-                if scale is not None:
-                    m = m * scale
-                m_v[first + p, z, pl.ds(PAD + r, 8), :] = m
-        sweep_rows(count, tiles, body, UM)
-
-    modulus(lo_d, 0, 4, vlo)
-    modulus(mid, 4, planes, None)
-    modulus(hi_d, planes + 4, 4, vhi)
+    for copy in copies[:densities]:
+        copy.wait()
+
+    def modulus(p, r):
+        ok = jnp.where(p < 4, vlo, jnp.where(p >= planes + 4, vhi, 1.0))
+        for z in range(2):
+            d = d_v[p, pl.ds(r, 8), pl.ds(128 * z, 128)]
+            m_v[p, z, pl.ds(PAD + r, 8), :] = (E_MIN + d * d * d * (1.0 - E_MIN)) * ok
+
+    sweep_rows(planes + 8, tiles, modulus, UM)
 
     lane = lax.broadcasted_iota(jnp.int32, (8, 128), 1)
     first_lane, last_lane = lane == 0, lane == 127
@@ -108,7 +115,7 @@
     def get(ref, i, row):
         return [ref[i, z, pl.ds(row, 8), :] for z in range(2)]
 
-    for copy in copies:
+    for copy in copies[densities:]:
         copy.wait()
 
     def first(p, r):
@@ -175,8 +182,6 @@
 
     sweep_rows((planes + 2), tiles, third, U2)
 
-    half = rows - EXTRA
-    skip = pl.multiple_of(h * EXTRA, 8)
     outs = []
     for z in range(2):
         for p in range(planes):
@@ -209,16 +214,17 @@
         copy.wait()
 
 
-def step(h, gap, valid, table, loads, support, mid, lo_d, hi_d, lo_i, hi_i, u):
-    planes, rows, cols = mid.shape
+def step(h, gap, valid, table, loads, support, main, other, ints, u):
+    planes, half, cols = main[1].shape
+    rows = half + EXTRA
     tiles_rows = rows + 2 * PAD
     f32 = jnp.float32
     any_spec = pl.BlockSpec(memory_space=pl.ANY)
     smem = pl.BlockSpec(memory_space=pltpu.SMEM)
     vmem = pl.BlockSpec(memory_space=pltpu.VMEM)
     full = loads.shape[2]
-    args = [jnp.stack([h, gap]).astype(jnp.int32), table, valid, loads, support, mid, lo_d, hi_d, lo_i, hi_i]
-    specs = [smem, smem, smem, any_spec, any_spec, vmem, vmem, vmem, any_spec, any_spec]
+    args = [jnp.stack([h, gap]).astype(jnp.int32), table, valid, loads, support, *main, *other, *ints]
+    specs = [smem, smem, smem] + [any_spec] * 10
     aliases = {}
     if u is not None:
         args.append(u)
@@ -235,6 +241,7 @@
         out_specs=(any_spec, vmem),
         input_output_aliases=aliases,
         scratch_shapes=[
+            pltpu.VMEM((planes + 8, rows, cols), f32),
             pltpu.VMEM((2, planes + 6, rows, cols), jnp.int32),
             pltpu.VMEM((planes + 6, rows, cols), jnp.int32),
             pltpu.VMEM((planes + 8, 2, tiles_rows, 128), f32),
@@ -242,7 +249,7 @@
             pltpu.VMEM((6 * (planes + 6), 2, tiles_rows, 128), f32),
             pltpu.VMEM((6 * (planes + 4), 2, tiles_rows, 128), f32),
             pltpu.VMEM((6 * (planes + 2), 2, tiles_rows, 128), f32),
-            pltpu.SemaphoreType.DMA((9,)),
+            pltpu.SemaphoreType.DMA((15,)),
             pltpu.SemaphoreType.DMA((2 * planes * 6,)),
         ],
         compiler_params=pltpu.CompilerParams(vmem_limit_bytes=56 * 1024 * 1024),
@@ -355,38 +362,35 @@
     swap = [(0, 1), (1, 0)]
 
     partner = lax.ppermute(density, "case", swap)
-
-    def window(h):
-        start = h * gap
-        own = lax.dynamic_slice_in_dim(loads, start, rows, axis=2)
-        sup = lax.dynamic_slice_in_dim(support, start, rows, axis=1)
+    lo_c = lax.ppermute(density[planes - 4:], "slab", rise)
+    hi_c = lax.ppermute(density[:4], "slab", fall)
+
+    def packed(h):
+        own = lax.dynamic_slice_in_dim(loads, h * gap, rows, axis=2)
+        sup = lax.dynamic_slice_in_dim(support, h * gap, rows, axis=1)
 
         def pack(a, b):
             return jnp.concatenate([own[0, a:b], own[1, a:b], sup[a:b]], axis=0)
 
-        lo_i = lax.ppermute(pack(planes - 3, planes), "slab", rise)
-        hi_i = lax.ppermute(pack(0, 3), "slab", fall)
-        return lo_i, hi_i
-
-    def densities(h, main, other):
-        low = jnp.concatenate([main, other[:, :EXTRA]], axis=1)
-        high = jnp.concatenate([other[:, half - EXTRA:], main], axis=1)
-        mid = jnp.where(h == 0, low, high)
-        lo_d = lax.ppermute(mid[planes - 4:], "slab", rise)
-        hi_d = lax.ppermute(mid[:4], "slab", fall)
-        return mid, lo_d, hi_d
-
-    ints_a = window(1 - mine)
-    dens_a = densities(1 - mine, partner, density)
-    ints_b = window(mine)
-    dens_b = densities(mine, density, partner)
-    u, e_a = step(1 - mine, gap, valid, load_table, loads, support, *dens_a, *ints_a, None)
+        return pack(planes - 3, planes), pack(0, 3)
+
+    def exchange(up, down):
+        return lax.ppermute(up, "slab", rise), lax.ppermute(down, "slab", fall)
+
+    ints_a = exchange(*packed(1 - mine))
+    both = lax.ppermute(jnp.concatenate([lo_c, hi_c]), "case", swap)
+    lo_o, hi_o = both[:4], both[4:]
+    ints_b = exchange(*packed(mine))
+    own = (lo_c, density, hi_c)
+    opposite = (lo_o, partner, hi_o)
+    u, e_a = step(1 - mine, gap, valid, load_table, loads, support, opposite, own, ints_a, None)
     received = lax.ppermute(e_a, "case", swap)
-    u, e_b = step(mine, gap, valid, load_table, loads, support, *dens_b, *ints_b, u)
-    mid = dens_b[0]
+    u, e_b = step(mine, gap, valid, load_table, loads, support, own, opposite, ints_b, u)
+    low = jnp.concatenate([density, partner[:, :EXTRA]], axis=1)
+    high = jnp.concatenate([partner[:, half - EXTRA:], density], axis=1)
+    mid = jnp.where(mine == 0, low, high)
     right = (-PENALTY * (1.0 - E_MIN)) * (mid * mid * mid) * (e_b + received)
-    lo_r = lax.ppermute(right[planes - 4:], "slab", rise)
-    hi_r = lax.ppermute(right[:4], "slab", fall)
+    lo_r, hi_r = exchange(right[planes - 4:], right[:4])
     filtered = smooth(mine, gap, valid, lo_r, right, hi_r, density)
     return u, filtered
 

time: 159 us -> 136 us (0.86)
  waiting for transfers between devices: 64.2 us -> 44.5 us
  starting transfers between devices: 29.8 us -> 25.6 us
  local copies, waits for them, and re-layouts: 5.78 us -> 8.28 us
    ppermute x10 -> x9, waiting for transfers between devices: 63.6 us -> 38.7 us  [the longest x6 23.4 us: exchange(): return (lax.ppermute(up, 'slab', rise), lax.ppermute(down, 'slab', fall))]
    ppermute x1, waiting for transfers between devices: 0.53 us -> 5.81 us  [local(): partner = lax.ppermute(density, 'case', swap)]
    ppermute x10 -> x9, starting transfers between devices: 28.2 us -> 24 us  [the longest x6 17.1 us: exchange(): return (lax.ppermute(up, 'slab', rise), lax.ppermute(down, 'slab', fall))]
    slice x2, local copies, waits for them, and re-layouts: 0.79 us -> 3.11 us  [the longest x1 2.33 us: local(): lo_o, hi_o = (both[:4], both[4:])]
  transfers between devices with their start and end apart: 12 -> 11, of which waited for: 4 -> 6; matrix products, arithmetic and copies ran while one was open for 8% -> 10% of each run, Pallas kernels for 25% -> 29%
where the time goes in v3:
time: 136 us; the launch traced here: 135 us
  Pallas kernels  48.4 us (36%)
  waiting for transfers between devices  44.5 us (33%)
  starting transfers between devices  25.6 us (19%)
  local copies, waits for them, and re-layouts  8.28 us (6%)
  other arithmetic  7.86 us (6%)
    pallas_call x2, Pallas kernels, step(): pl.pallas_call(kernel, out_shape=(jax.ShapeDtypeStruct((2, 3, planes, ful...  39.3 us
    ppermute x6, waiting for transfers between devices, exchange(): return (lax.ppermute(up, 'slab', rise), lax.ppermute(down, 'slab', fall))  23.4 us
    ppermute x6, starting transfers between devices, exchange(): return (lax.ppermute(up, 'slab', rise), lax.ppermute(down, 'slab', fall))  17.1 us
    pallas_call x1, Pallas kernels, smooth(): pl.pallas_call(kernel, out_shape=jax.ShapeDtypeStruct(dens.shape, f32), i...  9.14 us
    ppermute x1, waiting for transfers between devices, local(): lo_c = lax.ppermute(density[planes - 4:], 'slab', rise)  7.87 us
    ppermute x1, waiting for transfers between devices, local(): both = lax.ppermute(jnp.concatenate([lo_c, hi_c]), 'case', swap)  5.95 us
    ppermute x1, waiting for transfers between devices, local(): partner = lax.ppermute(density, 'case', swap)  5.81 us
    concatenate x4, other arithmetic, pack(): return jnp.concatenate([own[0, a:b], own[1, a:b], sup[a:b]], axis=0)  4.69 us
  transfers between devices with their start and end apart: 11, of which 6 were waited for; matrix products, arithmetic and copies ran while one was open for 10% of the time, Pallas kernels for 29%

profile of v3, /device:TPU:9, one launch (start us, length us, event | category | flops | bytes accessed | tf_op | source)
XLA Modules:
  0.0 135.5 jit_solution(18373761822294356086)
XLA Ops:
  0.6 3.7 %collective-permute-start = (f32[4,128,256]{2,1,0:T(8,128)}, f32[4,128,256]{2,1,0:T(8,128)S(1)}, u32[]{:S(2)}, u32[]{:S(2)}) collective-permute-start(f32[4,128,256]{2,1,0:T(8,128)} %refs_5_.1), channel_id=1, source_target_pairs={{0,1},{1,2},{2,3},{3,4},{4,5},{5,6},{6,7},{7,8},{8,9},{9,10},{10,1... | collective-permute-start | bytes 1572872 | tf_op jit(solution)/shard_map/ppermute | solution.py:365
  4.3 1.9 %collective-permute-start.1 = (f32[4,128,256]{2,1,0:T(8,128)}, f32[4,128,256]{2,1,0:T(8,128)S(1)}, u32[]{:S(2)}, u32[]{:S(2)}) collective-permute-start(f32[4,128,256]{2,1,0:T(8,128)} %refs_5_.1), channel_id=1, source_target_pairs={{1,0},{2,1},{3,2},{4,3},{5,4},{6,5},{7,6},{8,7},{9,8},{10,9},{11,1... | collective-permute-start | bytes 1572872 | tf_op jit(solution)/shard_map/ppermute | solution.py:366
  6.3 2.2 %dynamic-slice_bitcast_fusion.1 = (s32[3,136,256]{2,1,0:T(8,128)S(1)}, s32[3,136,256]{2,1,0:T(8,128)S(1)}, s32[3,136,256]{2,1,0:T(8,128)S(1)}, s32[3,136,256]{2,...) fusion(s32[2,4,256,256]{3,2,1,0:T(8,128)} %refs_3_.3, ...), kind=kLoop, calls=%fused_computation.10 | loop fusion | bytes 6684684 | tf_op jit(solution)/shard_map/squeeze | solution.py:373
  8.5 0.0 copy-start.4
  8.5 7.9 %collective-permute-done.refs_8_.refs_5_ = f32[4,128,256]{2,1,0:T(8,128)S(1)} collective-permute-done((f32[4,128,256]{2,1,0:T(8,128)}, f32[4,128,256]{2,1,0:T(8,128)S(1)}, u32[]{:S(2)}, u32[]{:S(2)}) %collective-permute-start) | collective-permute-done | bytes 524320 | tf_op jit(solution)/shard_map/ppermute | solution.py:365
  16.4 0.0 copy-start.5
  16.4 1.5 %collective-permute-done.1.refs_10_.refs_7_ = f32[4,128,256]{2,1,0:T(8,128)S(1)} collective-permute-done((f32[4,128,256]{2,1,0:T(8,128)}, f32[4,128,256]{2,1,0:T(8,128)S(1)}, u32[]{:S(2)}, u32[]{:S(2)}) %collective-permute-start.1) | collective-permute-done | bytes 524320 | tf_op jit(solution)/shard_map/ppermute | solution.py:366
  17.8 0.0 copy-start.6
  17.8 0.1 pad_maximum_fusion
  17.9 1.3 collective-permute-start.2
  19.2 0.0 copy-done.4
  19.2 0.1 constant_dynamic-slice_fusion.2
  19.4 0.0 copy-done.5
  19.4 0.0 copy-done.6
  19.4 1.2 pad_add_fusion.2
  20.5 3.1 %collective-permute-start.6 = (s32[9,136,256]{2,1,0:T(8,128)}, s32[9,136,256]{2,1,0:T(8,128)}, u32[]{:S(2)}, u32[]{:S(2)}) collective-permute-start(s32[9,136,256]{2,1,0:T(8,128)} %pad_add_fusion.2), channel_id=1, source_target_pairs={{0,1},{1,2},{2,3},{3,4},{4,5},{5,6},{6,7},{7,8},{8,9},{9,10},{10,1... | collective-permute-start | bytes 3760136 | tf_op jit(solution)/shard_map/ppermute | solution.py:378
  23.6 1.2 pad_add_fusion.3
  24.8 1.9 %collective-permute-start.7 = (s32[9,136,256]{2,1,0:T(8,128)}, s32[9,136,256]{2,1,0:T(8,128)}, u32[]{:S(2)}, u32[]{:S(2)}) collective-permute-start(s32[9,136,256]{2,1,0:T(8,128)} %pad_add_fusion.3), channel_id=1, source_target_pairs={{1,0},{2,1},{3,2},{4,3},{5,4},{6,5},{7,6},{8,7},{9,8},{10,9},{11,1... | collective-permute-start | bytes 3760136 | tf_op jit(solution)/shard_map/ppermute | solution.py:378
  26.8 1.2 pad_add_fusion
  27.9 3.6 %collective-permute-start.4 = (s32[9,136,256]{2,1,0:T(8,128)}, s32[9,136,256]{2,1,0:T(8,128)S(1)}, u32[]{:S(2)}, u32[]{:S(2)}) collective-permute-start(s32[9,136,256]{2,1,0:T(8,128)} %pad_add_fusion), channel_id=1, source_target_pairs={{0,1},{1,2},{2,3},{3,4},{4,5},{5,6},{6,7},{7,8},{8,9},{9,10},{10,1... | collective-permute-start | bytes 3760136 | tf_op jit(solution)/shard_map/ppermute | solution.py:378
  31.6 0.0 copy-start
  31.6 1.2 pad_add_fusion.1
  32.7 1.9 %collective-permute-start.5 = (s32[9,136,256]{2,1,0:T(8,128)}, s32[9,136,256]{2,1,0:T(8,128)S(1)}, u32[]{:S(2)}, u32[]{:S(2)}) collective-permute-start(s32[9,136,256]{2,1,0:T(8,128)} %pad_add_fusion.1), channel_id=1, source_target_pairs={{1,0},{2,1},{3,2},{4,3},{5,4},{6,5},{7,6},{8,7},{9,8},{10,9},{11,1... | collective-permute-start | bytes 3760136 | tf_op jit(solution)/shard_map/ppermute | solution.py:378
  34.7 6.0 %collective-permute-done.2 = f32[8,128,256]{2,1,0:T(8,128)} collective-permute-done((f32[8,128,256]{2,1,0:T(8,128)S(1)}, f32[8,128,256]{2,1,0:T(8,128)}, u32[]{:S(2)}, u32[]{:S(2)}) %collective-permute-start.2) | collective-permute-done | bytes 1048608 | tf_op jit(solution)/shard_map/ppermute | solution.py:381
  40.6 0.0 copy-done
  40.6 1.2 collective-permute-start.3
  41.8 1.3 copy.8.refs_1_
  43.2 0.6 add_convert_fusion.refs_2_.refs_1_
  43.8 0.6 pad_add_fusion.4.refs_0_
  44.5 2.3 %fusion.2 = (f32[4,128,256]{2,1,0:T(8,128)}, f32[4,128,256]{2,1,0:T(8,128)}) fusion(f32[8,128,256]{2,1,0:T(8,128)} %collective-permute-done.2), kind=kLoop, calls=%fused_computation.24 | loop fusion | bytes 2097152 | tf_op jit(solution)/shard_map/slice | solution.py:382
  46.8 5.8 %collective-permute-done.3.refs_6_.refs_9_ = f32[4,128,256]{2,1,0:T(8,128)S(1)} collective-permute-done((f32[4,128,256]{2,1,0:T(8,128)S(1)}, f32[4,128,256]{2,1,0:T(8,128)S(1)}, u32[]{:S(2)}, u32[]{:S(2)}) %collective-permute-start.3) | collective-permute-done | bytes 524320 | tf_op jit(solution)/shard_map/ppermute | solution.py:364
  52.6 0.0 copy-start.7
  52.6 12.1 %collective-permute-done.6.refs_11_ = s32[9,136,256]{2,1,0:T(8,128)} collective-permute-done((s32[9,136,256]{2,1,0:T(8,128)}, s32[9,136,256]{2,1,0:T(8,128)}, u32[]{:S(2)}, u32[]{:S(2)}) %collective-permute-start.6) | collective-permute-done | bytes 1253408 | tf_op jit(solution)/shard_map/ppermute | solution.py:378
  64.7 0.0 collective-permute-done.7.refs_12_
  64.7 0.0 copy-done.7
  64.7 19.6 %relax.2 = (f32[2,3,4,256,256]{4,3,2,1,0:T(8,128)}, f32[4,136,256]{2,1,0:T(8,128)}) custom-call(s32[2]{0:T(128)} %pad_add_fusion.4.refs_0_, f32[8,3]{1,0:T(8,128)} %copy.8.refs_1_, f32[2]{0:T(128)} %add_convert_fusion.refs_2_.refs_1_, s32[2,4,256,256]{3,2,1,0:T(8,128)} %refs_3_.3, s32[4,256,256]{2,1,0:T(8,128)} %refs_4_.3, ...), custom_call_target="tpu_custom_call" | custom-call | flops 40000000 | bytes 40000000 | tf_op jit(solution)/shard_map/relax/pallas_call | solution.py:237
  84.4 0.4 collective-permute-start.8
  84.8 0.6 pad_add_fusion.5.refs_0_
  85.4 0.8 fusion.3
  86.2 0.0 collective-permute-done.4.refs_11_
  86.2 0.0 copy-start.8
  86.2 0.0 collective-permute-done.5.refs_12_
  86.2 0.0 copy-start.9
  86.2 1.0 copy-done.8
  87.2 0.4 copy-done.9
  87.7 0.0 copy-start.1
  87.7 19.6 %relax.3 = (f32[2,3,4,256,256]{4,3,2,1,0:T(8,128)}, f32[4,136,256]{2,1,0:T(8,128)}) custom-call(s32[2]{0:T(128)} %pad_add_fusion.5.refs_0_, f32[8,3]{1,0:T(8,128)} %copy.8.refs_1_, f32[2]{0:T(128)} %add_convert_fusion.refs_2_.refs_1_, s32[2,4,256,256]{3,2,1,0:T(8,128)} %refs_3_.3, s32[4,256,256]{2,1,0:T(8,128)} %refs_4_.3, ...), custom_call_target="tpu_custom_call", output_to_operand_aliasing={{0}: (13, {})} | custom-call | flops 40000000 | bytes 40000000 | tf_op jit(solution)/shard_map/relax/pallas_call | solution.py:237
  107.3 0.0 copy-start.2
  107.3 0.0 copy-start.3
  107.3 0.0 collective-permute-done.8
  107.3 0.0 copy-done.1
  107.3 1.2 fusion.1.refs_3_
  108.5 1.9 %collective-permute-start.10 = (f32[4,136,256]{2,1,0:T(8,128)S(1)}, f32[4,136,256]{2,1,0:T(8,128)S(1)}, u32[]{:S(2)}, u32[]{:S(2)}) collective-permute-start(f32[4,136,256]{2,1,0:T(8,128)S(1)} %fusion.1.refs_3_), channel_id=1, source_target_pairs={{1,0},{2,1},{3,2},{4,3},{5,4},{6,5},{7,6},{8,7},{9,8},{10,9},{11,1... | collective-permute-start | bytes 1671176 | tf_op jit(solution)/shard_map/ppermute | solution.py:378
  110.4 4.7 %collective-permute-start.9 = (f32[4,136,256]{2,1,0:T(8,128)S(1)}, f32[4,136,256]{2,1,0:T(8,128)S(1)}, u32[]{:S(2)}, u32[]{:S(2)}) collective-permute-start(f32[4,136,256]{2,1,0:T(8,128)S(1)} %fusion.1.refs_3_), channel_id=1, source_target_pairs={{0,1},{1,2},{2,3},{3,4},{4,5},{5,6},{6,7},{7,8},{8,9},{9,10},{10,1... | collective-permute-start | bytes 1671176 | tf_op jit(solution)/shard_map/ppermute | solution.py:378
  115.1 11.2 %collective-permute-done.10.refs_4_ = f32[4,136,256]{2,1,0:T(8,128)S(1)} collective-permute-done((f32[4,136,256]{2,1,0:T(8,128)S(1)}, f32[4,136,256]{2,1,0:T(8,128)S(1)}, u32[]{:S(2)}, u32[]{:S(2)}) %collective-permute-start.10) | collective-permute-done | bytes 557088 | tf_op jit(solution)/shard_map/ppermute | solution.py:378
  126.3 0.0 collective-permute-done.9.refs_2_
  126.3 0.0 copy-done.2
  126.3 0.0 copy-done.3
  126.3 9.1 %smooth.1 = f32[4,128,256]{2,1,0:T(8,128)} custom-call(s32[2]{0:T(128)S(1)} %copy-done.3, f32[2]{0:T(128)S(1)} %copy-done.2, f32[4,136,256]{2,1,0:T(8,128)S(1)} %collective-permute-done.9.refs_2_, f32[4,136,256]{2,1,0:T(8,128)S(1)} %fusion.1.refs_3_, f32[4,136,256]{2,1,0:T(8,128)S(1)} %collective-permute-done.10.refs_4_, f32[4,128,256]{2,1,0:T(8,128)S(1)} %copy-done.1), custom_call_target="tpu_custom_call" | custom-call | flops 5000000 | bytes 5000000 | tf_op jit(solution)/shard_map/smooth/pallas_call | solution.py:339
Async XLA Ops:
  0.6 15.8 %collective-permute-start = (f32[4,128,256]{2,1,0:T(8,128)}, f32[4,128,256]{2,1,0:T(8,128)S(1)}, u32[]{:S(2)}, u32[]{:S(2)}) collective-permute-start(f32[4,128,256]{2,1,0:T(8,128)} %refs_5_.1), channel_id=1, source_target_pairs={{0,1},{1,2},{2,3},{3,4},{4,5},{5,6},{6,7},{7,8},{8,9},{9,10},{10,1... | collective-permute-start | bytes 1572872 | tf_op jit(solution)/shard_map/ppermute | solution.py:365
  4.3 13.5 %collective-permute-start.1 = (f32[4,128,256]{2,1,0:T(8,128)}, f32[4,128,256]{2,1,0:T(8,128)S(1)}, u32[]{:S(2)}, u32[]{:S(2)}) collective-permute-start(f32[4,128,256]{2,1,0:T(8,128)} %refs_5_.1), channel_id=1, source_target_pairs={{1,0},{2,1},{3,2},{4,3},{5,4},{6,5},{7,6},{8,7},{9,8},{10,9},{11,1... | collective-permute-start | bytes 1572872 | tf_op jit(solution)/shard_map/ppermute | solution.py:366
  8.5 10.7 %copy-start.4 = (s32[4,256,256]{2,1,0:T(8,128)S(1)}, s32[4,256,256]{2,1,0:T(8,128)}, u32[]{:S(2)}) copy-start(s32[4,256,256]{2,1,0:T(8,128)} %refs_4_.3) | copy-start | bytes 3145732
  16.4 3.0 %copy-start.5 = (f32[4,128,256]{2,1,0:T(8,128)}, f32[4,128,256]{2,1,0:T(8,128)S(1)}, u32[]{:S(2)}) copy-start(f32[4,128,256]{2,1,0:T(8,128)S(1)} %collective-permute-done.refs_8_.refs_5_) | copy-start | bytes 1572868
  17.8 1.5 %copy-start.6 = (f32[4,128,256]{2,1,0:T(8,128)}, f32[4,128,256]{2,1,0:T(8,128)S(1)}, u32[]{:S(2)}) copy-start(f32[4,128,256]{2,1,0:T(8,128)S(1)} %collective-permute-done.1.refs_10_.refs_7_) | copy-start | bytes 1572868
  17.9 22.7 %collective-permute-start.2 = (f32[8,128,256]{2,1,0:T(8,128)S(1)}, f32[8,128,256]{2,1,0:T(8,128)}, u32[]{:S(2)}, u32[]{:S(2)}) collective-permute-start(f32[8,128,256]{2,1,0:T(8,128)S(1)} %pad_maximum_fusion), channel_id=1, source_target_pairs={{0,16},{16,0},{1,17},{17,1},{2,18},{18,2},{3,19},{19,3},{4,20},{20... | collective-permute-start | bytes 3145736 | tf_op jit(solution)/shard_map/ppermute | solution.py:381
  20.5 44.2 %collective-permute-start.6 = (s32[9,136,256]{2,1,0:T(8,128)}, s32[9,136,256]{2,1,0:T(8,128)}, u32[]{:S(2)}, u32[]{:S(2)}) collective-permute-start(s32[9,136,256]{2,1,0:T(8,128)} %pad_add_fusion.2), channel_id=1, source_target_pairs={{0,1},{1,2},{2,3},{3,4},{4,5},{5,6},{6,7},{7,8},{8,9},{9,10},{10,1... | collective-permute-start | bytes 3760136 | tf_op jit(solution)/shard_map/ppermute | solution.py:378
  24.8 39.9 %collective-permute-start.7 = (s32[9,136,256]{2,1,0:T(8,128)}, s32[9,136,256]{2,1,0:T(8,128)}, u32[]{:S(2)}, u32[]{:S(2)}) collective-permute-start(s32[9,136,256]{2,1,0:T(8,128)} %pad_add_fusion.3), channel_id=1, source_target_pairs={{1,0},{2,1},{3,2},{4,3},{5,4},{6,5},{7,6},{8,7},{9,8},{10,9},{11,1... | collective-permute-start | bytes 3760136 | tf_op jit(solution)/shard_map/ppermute | solution.py:378
  27.9 58.3 %collective-permute-start.4 = (s32[9,136,256]{2,1,0:T(8,128)}, s32[9,136,256]{2,1,0:T(8,128)S(1)}, u32[]{:S(2)}, u32[]{:S(2)}) collective-permute-start(s32[9,136,256]{2,1,0:T(8,128)} %pad_add_fusion), channel_id=1, source_target_pairs={{0,1},{1,2},{2,3},{3,4},{4,5},{5,6},{6,7},{7,8},{8,9},{9,10},{10,1... | collective-permute-start | bytes 3760136 | tf_op jit(solution)/shard_map/ppermute | solution.py:378
  31.6 9.1 %copy-start = (f32[4,128,256]{2,1,0:T(8,128)S(1)}, f32[4,128,256]{2,1,0:T(8,128)}, u32[]{:S(2)}) copy-start(f32[4,128,256]{2,1,0:T(8,128)} %refs_5_.1) | copy-start | bytes 1572868
  32.7 53.5 %collective-permute-start.5 = (s32[9,136,256]{2,1,0:T(8,128)}, s32[9,136,256]{2,1,0:T(8,128)S(1)}, u32[]{:S(2)}, u32[]{:S(2)}) collective-permute-start(s32[9,136,256]{2,1,0:T(8,128)} %pad_add_fusion.1), channel_id=1, source_target_pairs={{1,0},{2,1},{3,2},{4,3},{5,4},{6,5},{7,6},{8,7},{9,8},{10,9},{11,1... | collective-permute-start | bytes 3760136 | tf_op jit(solution)/shard_map/ppermute | solution.py:378
  40.6 12.0 %collective-permute-start.3 = (f32[4,128,256]{2,1,0:T(8,128)S(1)}, f32[4,128,256]{2,1,0:T(8,128)S(1)}, u32[]{:S(2)}, u32[]{:S(2)}) collective-permute-start(f32[4,128,256]{2,1,0:T(8,128)S(1)} %copy-done), channel_id=1, source_target_pairs={{0,16},{16,0},{1,17},{17,1},{2,18},{18,2},{3,19},{19,3},{4,20},{20... | collective-permute-start | bytes 1572872 | tf_op jit(solution)/shard_map/ppermute | solution.py:364
  52.6 12.1 %copy-start.7 = (f32[4,128,256]{2,1,0:T(8,128)}, f32[4,128,256]{2,1,0:T(8,128)S(1)}, u32[]{:S(2)}) copy-start(f32[4,128,256]{2,1,0:T(8,128)S(1)} %collective-permute-done.3.refs_6_.refs_9_) | copy-start | bytes 1572868
  84.4 22.9 %collective-permute-start.8 = (f32[4,136,256]{2,1,0:T(8,128)}, f32[4,136,256]{2,1,0:T(8,128)S(1)}, u32[]{:S(2)}, u32[]{:S(2)}) collective-permute-start(f32[4,136,256]{2,1,0:T(8,128)} %get-tuple-element.9), channel_id=1, source_target_pairs={{0,16},{16,0},{1,17},{17,1},{2,18},{18,2},{3,19},{19,3},{4,20},{20... | collective-permute-start | bytes 1671176 | tf_op jit(solution)/shard_map/ppermute | solution.py:387
  86.2 1.0 copy-start.8
  86.2 1.4 %copy-start.9 = (s32[9,136,256]{2,1,0:T(8,128)}, s32[9,136,256]{2,1,0:T(8,128)S(1)}, u32[]{:S(2)}) copy-start(s32[9,136,256]{2,1,0:T(8,128)S(1)} %collective-permute-done.5.refs_12_) | copy-start | bytes 3760132
  87.7 19.6 %copy-start.1 = (f32[4,128,256]{2,1,0:T(8,128)S(1)}, f32[4,128,256]{2,1,0:T(8,128)}, u32[]{:S(2)}) copy-start(f32[4,128,256]{2,1,0:T(8,128)} %refs_5_.1) | copy-start | bytes 1572868
  107.3 19.1 %copy-start.2 = (f32[2]{0:T(128)S(1)}, f32[2]{0:T(128)}, u32[]{:S(2)}) copy-start(f32[2]{0:T(128)} %add_convert_fusion.refs_2_.refs_1_) | copy-start | bytes 28
  107.3 19.1 %copy-start.3 = (s32[2]{0:T(128)S(1)}, s32[2]{0:T(128)}, u32[]{:S(2)}) copy-start(s32[2]{0:T(128)} %pad_add_fusion.5.refs_0_) | copy-start | bytes 28
  108.5 17.8 %collective-permute-start.10 = (f32[4,136,256]{2,1,0:T(8,128)S(1)}, f32[4,136,256]{2,1,0:T(8,128)S(1)}, u32[]{:S(2)}, u32[]{:S(2)}) collective-permute-start(f32[4,136,256]{2,1,0:T(8,128)S(1)} %fusion.1.refs_3_), channel_id=1, source_target_pairs={{1,0},{2,1},{3,2},{4,3},{5,4},{6,5},{7,6},{8,7},{9,8},{10,9},{11,1... | collective-permute-start | bytes 1671176 | tf_op jit(solution)/shard_map/ppermute | solution.py:378
  110.4 15.9 %collective-permute-start.9 = (f32[4,136,256]{2,1,0:T(8,128)S(1)}, f32[4,136,256]{2,1,0:T(8,128)S(1)}, u32[]{:S(2)}, u32[]{:S(2)}) collective-permute-start(f32[4,136,256]{2,1,0:T(8,128)S(1)} %fusion.1.refs_3_), channel_id=1, source_target_pairs={{0,1},{1,2},{2,3},{3,4},{4,5},{5,6},{6,7},{7,8},{8,9},{9,10},{10,1... | collective-permute-start | bytes 1671176 | tf_op jit(solution)/shard_map/ppermute | solution.py:378

commit v4 on v3

v4 whole, which is shorter than its diff:
```python
import jax
import jax.numpy as jnp
from jax import lax
from jax.experimental import pallas as pl
from jax.experimental.pallas import tpu as pltpu
from jax.sharding import PartitionSpec as P

ITERS = 3
FSWEEPS = 4

E_MIN = 0.001
PENALTY = 3.0
SPRING = 4.0
LOWER = 0.05
UPPER = 2.0
RADIUS_SQ = 2.0

CENTRE = (UPPER + LOWER) / 2.0
HALF = (UPPER - LOWER) / 2.0
SIGMA = CENTRE / HALF
RHO0 = 1.0 / SIGMA
RHO1 = 1.0 / (2.0 * SIGMA - RHO0)
RHO2 = 1.0 / (2.0 * SIGMA - RHO1)
ALPHA1, B1 = RHO1 * RHO0, 2.0 * RHO1 / HALF
ALPHA2, B2 = RHO2 * RHO1, 2.0 * RHO2 / HALF
G0 = ALPHA1 + B1 * (CENTRE - 1.0)
A0 = 1.0 - B2 * ALPHA1 / B1
A1 = 1.0 + ALPHA2 + B2 / B1 - B2
RATIO = B2 / B1

HALO = 4
EXTRA = 8
PAD = 8


def over_rows(tiles, body):
    lax.fori_loop(0, tiles, lambda j, c: body(pl.multiple_of(j * 8, 8)), None, unroll=True)


def step_kernel(planes, rows, info, table, valid, loads, support, lo_d, mid, hi_d, lo_x, mid_x, hi_x, lo_i, hi_i, *rest):
    lo_s, hi_s = rest[:2] if len(rest) > 14 else (None, None)
    (u_out, e_out, d_v, idx_v, sup_v, m_v, k_v, s0_v, s1_v, u_v, in_sem, out_sem) = rest[-12:]
    tiles = rows // 8
    h = info[0]
    vlo, vhi = valid[0], valid[1]
    start = pl.multiple_of(h * info[1], 8)
    wide = planes + 6
    half = rows - EXTRA
    skip = pl.multiple_of(h * EXTRA, 8)

    def density_copies(j):
        own, other, at, count = (
            (lo_d, lo_x, 0, 4), (mid, mid_x, 4, planes), (hi_d, hi_x, planes + 4, 4))[j]
        edge = pl.ds(pl.multiple_of(h * (half - EXTRA), 8), EXTRA)
        beyond = pl.ds(pl.multiple_of((1 - h) * half, 8), EXTRA)
        return [
            pltpu.make_async_copy(own, d_v.at[pl.ds(at, count), pl.ds(skip, half), :], in_sem.at[2 * j]),
            pltpu.make_async_copy(other.at[:, edge, :], d_v.at[pl.ds(at, count), beyond, :], in_sem.at[2 * j + 1]),
        ]

    def halo_copies(j):
        source, shared, at = ((lo_i, lo_s, 0), (hi_i, hi_s, planes + 3))[j]
        made = []
        for part in range(3):
            goal = (idx_v.at[0], idx_v.at[1], sup_v)[part].at[pl.ds(at, 3)]
            group = pl.ds(3 * part, 3)
            sem = 6 + 6 * j + 2 * part
            if lo_s is None:
                made.append(pltpu.make_async_copy(source.at[group], goal, in_sem.at[sem]))
                continue
            fresh, common = rows - 2 * EXTRA, 2 * EXTRA
            made.append(pltpu.make_async_copy(
                source.at[group], goal.at[:, pl.ds(pl.multiple_of(h * common, 8), fresh), :], in_sem.at[sem]))
            made.append(pltpu.make_async_copy(
                shared.at[group, pl.ds(pl.multiple_of(h * fresh, 8), common), :],
                goal.at[:, pl.ds(pl.multiple_of((1 - h) * fresh, 8), common), :], in_sem.at[sem + 1]))
        return made

    def plane_copies(p):
        span = pl.ds(start, rows)
        sem = 18 + 3 * p
        return [
            pltpu.make_async_copy(loads.at[0, p, span, :], idx_v.at[0, p + 3], in_sem.at[sem]),
            pltpu.make_async_copy(loads.at[1, p, span, :], idx_v.at[1, p + 3], in_sem.at[sem + 1]),
            pltpu.make_async_copy(support.at[p, span, :], sup_v.at[p + 3], in_sem.at[sem + 2]),
        ]

    copies = density_copies(0) + density_copies(1) + halo_copies(0)
    for p in range(planes):
        copies += plane_copies(p)
    for copy in copies + density_copies(2) + halo_copies(1):
        copy.start()

    zero = jnp.zeros((PAD, 128), jnp.float32)

    def clear(count, ref):
        def body(i, carry):
            for z in range(2):
                ref[i, z, pl.ds(0, PAD), :] = zero
                ref[i, z, pl.ds(PAD + rows, PAD), :] = zero
            return carry

        lax.fori_loop(0, count, body, 0, unroll=4)

    clear(planes + 8, m_v)
    clear(6 * (planes + 6), s0_v)
    clear(6 * (planes + 4), s1_v)
    clear(6 * (planes + 2), u_v)

    lane = lax.broadcasted_iota(jnp.int32, (8, 128), 1)
    first_lane, last_lane = lane == 0, lane == 127

    def above(a):
        r0, r1 = pltpu.roll(a[0], 127, 1), pltpu.roll(a[1], 127, 1)
        return [jnp.where(last_lane, r1, r0), r1]

    def below(a):
        r0, r1 = pltpu.roll(a[0], 1, 1), pltpu.roll(a[1], 1, 1)
        return [r0, jnp.where(first_lane, r0, r1)]

    def get(ref, i, row):
        return [ref[i, z, pl.ds(row, 8), :] for z in range(2)]

    def modulus(p):
        ok = jnp.where(p < 4, vlo, jnp.where(p >= planes + 4, vhi, 1.0))

        def body(r):
            for z in range(2):
                d = d_v[p, pl.ds(r, 8), pl.ds(128 * z, 128)]
                m_v[p, z, pl.ds(PAD + r, 8), :] = (E_MIN + d * d * d * (1.0 - E_MIN)) * ok

        over_rows(tiles, body)

    def first(p):
        ok = jnp.where(p < 3, vlo, jnp.where(p >= planes + 3, vhi, 1.0))

        def body(r):
            row = PAD + r
            m = get(m_v, p + 1, row)
            zup, zdn = above(m), below(m)
            zup[1] = jnp.where(last_lane, 0.0, zup[1])
            zdn[0] = jnp.where(first_lane, 0.0, zdn[0])
            beside = [get(m_v, p + 2, row), get(m_v, p, row), get(m_v, p + 1, row + 1), get(m_v, p + 1, row - 1), zup, zdn]
            stores = []
            for z in range(2):
                face = [m[z] + b[z] for b in beside]
                double = ((face[0] + face[1]) + (face[2] + face[3])) + (face[4] + face[5])
                diagonal = 0.5 * double + SPRING * sup_v[p, pl.ds(r, 8), pl.ds(128 * z, 128)].astype(jnp.float32)
                w = ok / (diagonal + (1.0 - ok))
                wb = w * (0.5 * B1)
                weight = [f * wb for f in face]
                if z == 1:
                    weight[4] = jnp.where(last_lane, 0.0, weight[4])
                else:
                    weight[5] = jnp.where(first_lane, 0.0, weight[5])
                scale = w * (RATIO / CENTRE)
                for case in range(2):
                    index = idx_v[case, p, pl.ds(r, 8), pl.ds(128 * z, 128)]
                    b0, b1, b2 = (index & 1) != 0, (index & 2) != 0, (index & 4) != 0
                    forces = []
                    for c in range(3):
                        q = [jnp.where(b0, table[2 * j + 1, c], table[2 * j, c]) for j in range(4)]
                        forces.append(jnp.where(b2, jnp.where(b1, q[3], q[2]), jnp.where(b1, q[1], q[0])))
                    for c in range(3):
                        stores.append((s0_v, (p * 6 + case * 3 + c, z, pl.ds(row, 8)), forces[c] * scale))
                for j in range(6):
                    stores.append((k_v, (p, j, z, pl.ds(r, 8)), weight[j]))
            for ref, at, value in stores:
                ref[at] = value

        over_rows(tiles, body)

    def stencil(ref, at, row, k):
        c = get(ref, at, row)
        parts = [get(ref, at + 6, row), get(ref, at - 6, row), get(ref, at, row + 1), get(ref, at, row - 1), above(c), below(c)]
        out = []
        for z in range(2):
            t = [k[j][z] * parts[j][z] for j in range(6)]
            out.append(((t[0] + t[1]) + (t[2] + t[3])) + (t[4] + t[5]))
        return c, out

    def second(p):
        def body(r):
            row = PAD + r
            k = [[k_v[p + 1, j, z, pl.ds(r, 8), :] for z in range(2)] for j in range(6)]
            new = []
            for f in range(6):
                c, t = stencil(s0_v, (p + 1) * 6 + f, row, k)
                new.append([G0 * c[z] + t[z] for z in range(2)])
            for f in range(6):
                for z in range(2):
                    s1_v[p * 6 + f, z, pl.ds(row, 8), :] = new[f][z]

        over_rows(tiles, body)

    def third(p):
        def body(r):
            row = PAD + r
            k = [[k_v[p + 2, j, z, pl.ds(r, 8), :] for z in range(2)] for j in range(6)]
            new = []
            for f in range(6):
                c, t = stencil(s1_v, (p + 1) * 6 + f, row, k)
                base = get(s0_v, (p + 2) * 6 + f, row)
                new.append([(A0 / RATIO) * base[z] + (A1 / RATIO) * c[z] + t[z] for z in range(2)])
            for f in range(6):
                for z in range(2):
                    u_v[p * 6 + f, z, pl.ds(row, 8), :] = new[f][z]

        over_rows(tiles, body)

    def out_copies(p):
        return [
            pltpu.make_async_copy(
                u_v.at[(p + 1) * 6 + f, z, pl.ds(PAD + skip, half), :],
                u_out.at[f // 3, f % 3, p, pl.ds(pl.multiple_of(h * half, 8), half), pl.ds(128 * z, 128)],
                out_sem.at[p * 12 + f * 2 + z])
            for f in range(6) for z in range(2)
        ]

    def energy(p):
        def body(r):
            row = PAD + r
            acc = [[], []]
            for f in range(6):
                at = (p + 1) * 6 + f
                c = get(u_v, at, row)
                zup, zdn = above(c), below(c)
                zup[1] = jnp.where(last_lane, 0.0, zup[1])
                zdn[0] = jnp.where(first_lane, 0.0, zdn[0])
                for b in (get(u_v, at + 6, row), get(u_v, at - 6, row), get(u_v, at, row + 1), get(u_v, at, row - 1), zup, zdn):
                    for z in range(2):
                        d = c[z] - b[z]
                        if len(acc[z]) < 3:
                            acc[z].append(d * d)
                        else:
                            acc[z] = acc[z][1:] + [acc[z][0] + d * d]
            for z in range(2):
                e_out[p, pl.ds(r, 8), pl.ds(128 * z, 128)] = 0.5 * (acc[z][0] + acc[z][1] + acc[z][2])

        over_rows(tiles, body)

    for copy in density_copies(0) + density_copies(1):
        copy.wait()
    modulus(0)
    modulus(1)

    def each(count, body):
        def go(p, carry):
            body(p)
            return carry

        lax.fori_loop(0, count, go, 0)

    for copy in density_copies(2):
        copy.wait()
    each(planes + 6, lambda p: modulus(p + 2))
    for copy in halo_copies(0) + halo_copies(1):
        copy.wait()
    for p in range(planes):
        for copy in plane_copies(p):
            copy.wait()
    each(planes + 6, first)
    each(planes + 4, second)
    each(planes + 2, third)
    for p in range(planes):
        for copy in out_copies(p):
            copy.start()
    each(planes, energy)
    for p in range(planes):
        for copy in out_copies(p):
            copy.wait()


def step(h, gap, valid, table, loads, support, main, other, ints, u):
    planes, half, cols = main[1].shape
    rows = half + EXTRA
    tiles_rows = rows + 2 * PAD
    f32 = jnp.float32
    any_spec = pl.BlockSpec(memory_space=pl.ANY)
    smem = pl.BlockSpec(memory_space=pltpu.SMEM)
    vmem = pl.BlockSpec(memory_space=pltpu.VMEM)
    full = loads.shape[2]
    args = [jnp.stack([h, gap]).astype(jnp.int32), table, valid, loads, support, *main, *other, *ints]
    specs = [smem, smem, smem] + [any_spec] * (len(args) - 3)
    aliases = {}
    if u is not None:
        args.append(u)
        specs.append(any_spec)
        aliases = {len(args) - 1: 0}

    def kernel(*refs):
        step_kernel(planes, rows, *refs)

    return pl.pallas_call(
        kernel,
        out_shape=(jax.ShapeDtypeStruct((2, 3, planes, full, cols), f32), jax.ShapeDtypeStruct((planes, rows, cols), f32)),
        in_specs=specs,
        out_specs=(any_spec, vmem),
        input_output_aliases=aliases,
        scratch_shapes=[
            pltpu.VMEM((planes + 8, rows, cols), f32),
            pltpu.VMEM((2, planes + 6, rows, cols), jnp.int32),
            pltpu.VMEM((planes + 6, rows, cols), jnp.int32),
            pltpu.VMEM((planes + 8, 2, tiles_rows, 128), f32),
            pltpu.VMEM((planes + 6, 6, 2, rows, 128), f32),
            pltpu.VMEM((6 * (planes + 6), 2, tiles_rows, 128), f32),
            pltpu.VMEM((6 * (planes + 4), 2, tiles_rows, 128), f32),
            pltpu.VMEM((6 * (planes + 2), 2, tiles_rows, 128), f32),
            pltpu.SemaphoreType.DMA((18 + 3 * planes,)),
            pltpu.SemaphoreType.DMA((12 * planes,)),
        ],
        compiler_params=pltpu.CompilerParams(vmem_limit_bytes=56 * 1024 * 1024),
        cost_estimate=pl.CostEstimate(flops=40_000_000, bytes_accessed=40_000_000, transcendentals=0),
        name="relax",
    )(*args)


def filter_kernel(planes, rows, info, valid, lo, mid, hi, dens, out, r_v, a_v, b_v):
    tiles = rows // 8
    h = info[0]
    vlo, vhi = valid[0], valid[1]
    half = rows - EXTRA
    zero = jnp.zeros((PAD, 128), jnp.float32)
    lane = lax.broadcasted_iota(jnp.int32, (8, 128), 1)
    first_lane, last_lane = lane == 0, lane == 127

    def clear(i, carry):
        for ref in (r_v, a_v, b_v):
            for z in range(2):
                ref[i, z, pl.ds(0, PAD), :] = zero
                ref[i, z, pl.ds(PAD + rows, PAD), :] = zero
        return carry

    lax.fori_loop(0, planes + 8, clear, 0, unroll=4)

    def batches(total, body):
        for at in range(0, total, 5):
            body([8 * j for j in range(at, min(at + 5, total))])

    def fill(source, at, count):
        def plane(p, carry):
            def body(offsets):
                new = [[source[p, pl.ds(r, 8), pl.ds(128 * z, 128)] for z in range(2)] for r in offsets]
                for r, v in zip(offsets, new):
                    for z in range(2):
                        r_v[at + p, z, pl.ds(PAD + r, 8), :] = v[z]

            batches(tiles, body)
            return carry

        lax.fori_loop(0, count, plane, 0)

    fill(lo, 0, 4)
    fill(mid, 4, planes)
    fill(hi, planes + 4, 4)

    def smoothed(src, p, row, scale):
        c = [src[p, z, pl.ds(row, 8), :] for z in range(2)]
        u0, u1 = pltpu.roll(c[0], 127, 1), pltpu.roll(c[1], 127, 1)
        d0, d1 = pltpu.roll(c[0], 1, 1), pltpu.roll(c[1], 1, 1)
        zs = [
            jnp.where(last_lane, u1, u0) + jnp.where(first_lane, 0.0, d0),
            jnp.where(last_lane, 0.0, u1) + jnp.where(first_lane, d0, d1),
        ]
        new = []
        for z in range(2):
            total = (src[p + 1, z, pl.ds(row, 8), :] + src[p - 1, z, pl.ds(row, 8), :]) + (
                src[p, z, pl.ds(row + 1, 8), :] + src[p, z, pl.ds(row - 1, 8), :]) + zs[z]
            new.append((r_v[p, z, pl.ds(row, 8), :] + RADIUS_SQ * total) * scale)
        return new

    def sweep(src, dst, low, high):
        def plane(i, carry):
            p = low + i
            ok = jnp.where(p < 4, vlo, jnp.where(p >= planes + 4, vhi, 1.0))
            scale = ok * (1.0 / (1.0 + 6.0 * RADIUS_SQ))

            def body(offsets):
                new = [smoothed(src, p, pl.multiple_of(PAD + r, 8) if not isinstance(r, int) else PAD + r, scale) for r in offsets]
                for r, v in zip(offsets, new):
                    for z in range(2):
                        dst[p, z, pl.ds(PAD + r, 8), :] = v[z]

            batches(tiles, body)
            return carry

        lax.fori_loop(0, high - low, plane, 0)

    sweep(r_v, a_v, 1, planes + 7)
    sweep(a_v, b_v, 2, planes + 6)
    sweep(b_v, a_v, 3, planes + 5)

    skip = pl.multiple_of(h * EXTRA, 8)

    def last(p, carry):
        def body(offsets):
            new = [smoothed(a_v, p + 4, pl.multiple_of(PAD + r + skip, 8), 1.0 / (1.0 + 6.0 * RADIUS_SQ)) for r in offsets]
            for r, v in zip(offsets, new):
                for z in range(2):
                    out[p, pl.ds(r, 8), pl.ds(128 * z, 128)] = v[z] / dens[p, pl.ds(r, 8), pl.ds(128 * z, 128)]

        batches(half // 8, body)
        return carry

    lax.fori_loop(0, planes, last, 0)


def smooth(h, gap, valid, lo, mid, hi, dens):
    planes, rows, cols = mid.shape
    f32 = jnp.float32
    smem = pl.BlockSpec(memory_space=pltpu.SMEM)
    vmem = pl.BlockSpec(memory_space=pltpu.VMEM)

    def kernel(*refs):
        filter_kernel(planes, rows, *refs)

    return pl.pallas_call(
        kernel,
        out_shape=jax.ShapeDtypeStruct(dens.shape, f32),
        in_specs=[smem, smem] + [vmem] * 4,
        out_specs=vmem,
        scratch_shapes=[pltpu.VMEM((planes + 8, 2, rows + 2 * PAD, 128), f32)] * 3,
        compiler_params=pltpu.CompilerParams(vmem_limit_bytes=32 * 1024 * 1024),
        cost_estimate=pl.CostEstimate(flops=5_000_000, bytes_accessed=5_000_000, transcendentals=0),
        name="smooth",
    )(jnp.stack([h, gap]).astype(jnp.int32), valid, lo, mid, hi, dens)


def local(density, support, loads, load_table):
    planes, half, cols = density.shape
    full = loads.shape[2]
    rows = half + EXTRA
    gap = full - rows
    mine = lax.axis_index("case")
    count = lax.axis_size("slab")
    at = lax.axis_index("slab")
    valid = jnp.stack([at > 0, at < count - 1]).astype(jnp.float32)
    rise = [(i, i + 1) for i in range(count - 1)]
    fall = [(i + 1, i) for i in range(count - 1)]
    swap = [(0, 1), (1, 0)]

    partner = lax.ppermute(density, "case", swap)
    lo_c = lax.ppermute(density[planes - 4:], "slab", rise)
    hi_c = lax.ppermute(density[:4], "slab", fall)

    def packed(start, length):
        own = lax.dynamic_slice_in_dim(loads, start, length, axis=2)
        sup = lax.dynamic_slice_in_dim(support, start, length, axis=1)

        def pack(a, b):
            return jnp.concatenate([own[0, a:b], own[1, a:b], sup[a:b]], axis=0)

        return pack(planes - 3, planes), pack(0, 3)

    def exchange(up, down):
        return lax.ppermute(up, "slab", rise), lax.ppermute(down, "slab", fall)

    payload_a = packed((1 - mine) * gap, rows)
    payload_b = packed(mine * rows, rows - 2 * EXTRA)
    ints_a = exchange(*payload_a)
    lo_c, hi_c, partner, _ = lax.optimization_barrier((lo_c, hi_c, partner, payload_a))
    both = lax.ppermute(jnp.concatenate([lo_c, hi_c]), "case", swap)
    both, payload_b = lax.optimization_barrier((both, payload_b))
    lo_o, hi_o = both[:4], both[4:]
    ints_b = exchange(*payload_b) + ints_a
    own = (lo_c, density, hi_c)
    opposite = (lo_o, partner, hi_o)
    u, e_a = step(1 - mine, gap, valid, load_table, loads, support, opposite, own, ints_a, None)
    received = lax.ppermute(e_a, "case", swap)
    u, e_b = step(mine, gap, valid, load_table, loads, support, own, opposite, ints_b, u)
    low = jnp.concatenate([density, partner[:, :EXTRA]], axis=1)
    high = jnp.concatenate([partner[:, half - EXTRA:], density], axis=1)
    mid = jnp.where(mine == 0, low, high)
    right = (-PENALTY * (1.0 - E_MIN)) * (mid * mid * mid) * (e_b + received)
    lo_r, hi_r = exchange(right[planes - 4:], right[:4])
    filtered = smooth(mine, gap, valid, lo_r, right, hi_r, density)
    return u, filtered


def solution(mesh):
    return jax.shard_map(
        local,
        mesh=mesh,
        in_specs=(
            P("slab", "case", None),
            P("slab", None, None),
            P("case", "slab", None, None),
            P(),
        ),
        out_specs=(P("case", None, "slab", None, None), P("slab", "case", None)),
        check_vma=False,
    )
```

time: 136 us -> 134 us (0.985)
  starting transfers between devices: 25.6 us -> 30.9 us
  Pallas kernels: 48.4 us -> 44 us
  waiting for transfers between devices: 44.5 us -> 40.6 us
    ppermute x1, waiting for transfers between devices: 5.95 us -> 12.2 us  [local(): both = lax.ppermute(jnp.concatenate([lo_c, hi_c]), 'case', swap)]
    ppermute x1, waiting for transfers between devices: 5.81 us -> 0.32 us  [local(): partner = lax.ppermute(density, 'case', swap)]
    ppermute x6, starting transfers between devices: 17.1 us -> 22.5 us  [exchange(): return (lax.ppermute(up, 'slab', rise), lax.ppermute(down, 'slab', fall))]
    ppermute x1, waiting for transfers between devices: 7.87 us -> 3.79 us  [local(): lo_c = lax.ppermute(density[planes - 4:], 'slab', rise)]
    pallas_call x1, Pallas kernels: 9.14 us -> 5.55 us  [smooth(): pl.pallas_call(kernel, out_shape=jax.ShapeDtypeStruct(dens.shape, f32), i...]
    concatenate x1, other arithmetic: 0.07 us -> 2.42 us  [local(): both = lax.ppermute(jnp.concatenate([lo_c, hi_c]), 'case', swap)]
    concatenate x4 -> x3, other arithmetic: 4.69 us -> 3.52 us  [pack(): return jnp.concatenate([own[0, a:b], own[1, a:b], sup[a:b]], axis=0)]
    unnamed x21 -> x19, local copies, waits for them, and re-layouts: 2.82 us -> 2.08 us
  transfers between devices with their start and end apart: 11 -> 11, of which waited for: 6 -> 6; matrix products, arithmetic and copies ran while one was open for 10% -> 9% of each run, Pallas kernels for 29% -> 29%
where the time goes in v4:
time: 134 us
  Pallas kernels  44 us (33%)
  waiting for transfers between devices  40.6 us (30%)
  starting transfers between devices  30.9 us (23%)
  other arithmetic  9.16 us (7%)
  local copies, waits for them, and re-layouts  8.05 us (6%)
    pallas_call x2, Pallas kernels, step(): pl.pallas_call(kernel, out_shape=(jax.ShapeDtypeStruct((2, 3, planes, ful...  38.4 us
    ppermute x6, starting transfers between devices, exchange(): return (lax.ppermute(up, 'slab', rise), lax.ppermute(down, 'slab', fall))  22.5 us
    ppermute x6, waiting for transfers between devices, exchange(): return (lax.ppermute(up, 'slab', rise), lax.ppermute(down, 'slab', fall))  22.4 us
    ppermute x1, waiting for transfers between devices, local(): both = lax.ppermute(jnp.concatenate([lo_c, hi_c]), 'case', swap)  12.2 us
    pallas_call x1, Pallas kernels, smooth(): pl.pallas_call(kernel, out_shape=jax.ShapeDtypeStruct(dens.shape, f32), i...  5.55 us
    ppermute x1, waiting for transfers between devices, local(): lo_c = lax.ppermute(density[planes - 4:], 'slab', rise)  3.79 us
    ppermute x1, starting transfers between devices, local(): lo_c = lax.ppermute(density[planes - 4:], 'slab', rise)  3.71 us
    concatenate x3, other arithmetic, pack(): return jnp.concatenate([own[0, a:b], own[1, a:b], sup[a:b]], axis=0)  3.52 us
  transfers between devices with their start and end apart: 11, of which 6 were waited for; matrix products, arithmetic and copies ran while one was open for 9% of the time, Pallas kernels for 29%

profile of v4, /device:TPU:9, one launch (start us, length us, event | category | flops | bytes accessed | tf_op | source)
XLA Modules:
  0.0 133.5 jit_solution(1732135385746205180)
XLA Ops:
  0.6 3.7 %collective-permute-start = (f32[4,128,256]{2,1,0:T(8,128)}, f32[4,128,256]{2,1,0:T(8,128)S(1)}, u32[]{:S(2)}, u32[]{:S(2)}) collective-permute-start(f32[4,128,256]{2,1,0:T(8,128)} %refs_5_.1), channel_id=1, source_target_pairs={{0,1},{1,2},{2,3},{3,4},{4,5},{5,6},{6,7},{7,8},{8,9},{9,10},{10,1... | collective-permute-start | bytes 1572872 | tf_op jit(solution)/shard_map/ppermute | solution.py:443
  4.3 1.9 %collective-permute-start.1 = (f32[4,128,256]{2,1,0:T(8,128)}, f32[4,128,256]{2,1,0:T(8,128)}, u32[]{:S(2)}, u32[]{:S(2)}) collective-permute-start(f32[4,128,256]{2,1,0:T(8,128)} %refs_5_.1), channel_id=1, source_target_pairs={{1,0},{2,1},{3,2},{4,3},{5,4},{6,5},{7,6},{8,7},{9,8},{10,9},{11,1... | collective-permute-start | bytes 1572872 | tf_op jit(solution)/shard_map/ppermute | solution.py:444
  6.3 1.3 collective-permute-start.2
  7.6 1.2 constant_dynamic-slice_fusion.3
  8.7 1.5 %dynamic-slice_bitcast_fusion.1 = (s32[3,136,256]{2,1,0:T(8,128)S(1)}, s32[3,136,256]{2,1,0:T(8,128)S(1)}, s32[3,136,256]{2,1,0:T(8,128)S(1)}, s32[3,136,256]{2,1,0:T(8,128)S(1)}) fusion(s32[2,4,256,256]{3,2,1,0:T(8,128)} %refs_3_.3, s32[]{:T(128)S(6)} %select_n.16, s32[]{:T(128)S(6)} %add.25), kind=kLoop, calls=%fused_computation.10 | loop fusion | bytes 3342344 | tf_op jit(solution)/shard_map/squeeze | solution.py:451
  10.3 1.2 pad_add_fusion.1
  11.4 1.2 pad_add_fusion
  12.6 0.0 copy-start.4
  12.6 3.8 %collective-permute-done.refs_8_.refs_5_ = f32[4,128,256]{2,1,0:T(8,128)S(1)} collective-permute-done((f32[4,128,256]{2,1,0:T(8,128)}, f32[4,128,256]{2,1,0:T(8,128)S(1)}, u32[]{:S(2)}, u32[]{:S(2)}) %collective-permute-start) | collective-permute-done | bytes 524320 | tf_op jit(solution)/shard_map/ppermute | solution.py:443
  16.4 0.0 copy-start.5
  16.4 1.9 %collective-permute-done.1.refs_10_.refs_7_ = f32[4,128,256]{2,1,0:T(8,128)} collective-permute-done((f32[4,128,256]{2,1,0:T(8,128)}, f32[4,128,256]{2,1,0:T(8,128)}, u32[]{:S(2)}, u32[]{:S(2)}) %collective-permute-start.1) | collective-permute-done | bytes 524320 | tf_op jit(solution)/shard_map/ppermute | solution.py:444
  18.2 0.0 copy-done.5
  18.2 0.3 collective-permute-done.2.refs_6_.refs_9_
  18.6 0.0 copy-start.3
  18.6 2.4 %pad_maximum_fusion = f32[8,128,256]{2,1,0:T(8,128)} fusion(f32[4,128,256]{2,1,0:T(8,128)} %collective-permute-done.1.refs_10_.refs_7_, f32[4,128,256]{2,1,0:T(8,128)} %copy-done.5), kind=kLoop, calls=%fused_computation.4 | loop fusion | flops 262144 | bytes 2097152 | tf_op jit(solution)/shard_map/concatenate | solution.py:462
  21.0 1.2 collective-permute-start.3
  22.2 4.6 %collective-permute-start.7 = (s32[9,136,256]{2,1,0:T(8,128)}, s32[9,136,256]{2,1,0:T(8,128)}, u32[]{:S(2)}, u32[]{:S(2)}) collective-permute-start(s32[9,136,256]{2,1,0:T(8,128)} %pad_add_fusion.1), channel_id=1, source_target_pairs={{1,0},{2,1},{3,2},{4,3},{5,4},{6,5},{7,6},{8,7},{9,8},{10,9},{11,1... | collective-permute-start | bytes 3760136 | tf_op jit(solution)/shard_map/ppermute | solution.py:456
  26.8 3.0 %collective-permute-start.6 = (s32[9,136,256]{2,1,0:T(8,128)}, s32[9,136,256]{2,1,0:T(8,128)}, u32[]{:S(2)}, u32[]{:S(2)}) collective-permute-start(s32[9,136,256]{2,1,0:T(8,128)} %pad_add_fusion), channel_id=1, source_target_pairs={{0,1},{1,2},{2,3},{3,4},{4,5},{5,6},{6,7},{7,8},{8,9},{9,10},{10,1... | collective-permute-start | bytes 3760136 | tf_op jit(solution)/shard_map/ppermute | solution.py:456
  29.9 0.0 copy-done.4
  29.9 0.1 constant_dynamic-slice_fusion.2
  29.9 0.0 copy-done.3
  30.0 0.1 dynamic-slice_bitcast_fusion.5
  30.1 0.0 copy-start.8
  30.1 1.2 pad_add_fusion.2
  31.3 12.2 %collective-permute-done.3 = f32[8,128,256]{2,1,0:T(8,128)} collective-permute-done((f32[8,128,256]{2,1,0:T(8,128)}, f32[8,128,256]{2,1,0:T(8,128)}, u32[]{:S(2)}, u32[]{:S(2)}) %collective-permute-start.3) | collective-permute-done | bytes 1048608 | tf_op jit(solution)/shard_map/ppermute | solution.py:462
  43.5 7.3 %collective-permute-start.4 = (s32[9,120,256]{2,1,0:T(8,128)}, s32[9,120,256]{2,1,0:T(8,128)S(1)}, u32[]{:S(2)}, u32[]{:S(2)}) collective-permute-start(s32[9,120,256]{2,1,0:T(8,128)} %get-tuple-element.16), channel_id=1, source_target_pairs={{0,1},{1,2},{2,3},{3,4},{4,5},{5,6},{6,7},{7,8},{8,9},{9,10},{10,1... | collective-permute-start | bytes 3317768 | tf_op jit(solution)/shard_map/ppermute | solution.py:456
  50.9 1.9 %collective-permute-start.5 = (s32[9,120,256]{2,1,0:T(8,128)S(1)}, s32[9,120,256]{2,1,0:T(8,128)S(1)}, u32[]{:S(2)}, u32[]{:S(2)}) collective-permute-start(s32[9,120,256]{2,1,0:T(8,128)S(1)} %get-tuple-element.17), channel_id=1, source_target_pairs={{1,0},{2,1},{3,2},{4,3},{5,4},{6,5},{7,6},{8,7},{9,8},{10,9},{11,1... | collective-permute-start | bytes 3317768 | tf_op jit(solution)/shard_map/ppermute | solution.py:456
  52.8 0.0 copy-done.8
  52.8 0.7 copy.8.refs_1_
  53.5 0.7 add_convert_fusion.refs_2_.refs_1_
  54.2 0.6 pad_add_fusion.4.refs_0_
  54.8 2.3 %fusion.2 = (f32[4,128,256]{2,1,0:T(8,128)}, f32[4,128,256]{2,1,0:T(8,128)}) fusion(f32[8,128,256]{2,1,0:T(8,128)} %collective-permute-done.3), kind=kLoop, calls=%fused_computation.24 | loop fusion | bytes 2097152 | tf_op jit(solution)/shard_map/slice | solution.py:464
  57.1 11.1 %collective-permute-done.7.refs_12_.refs_14_ = s32[9,136,256]{2,1,0:T(8,128)} collective-permute-done((s32[9,136,256]{2,1,0:T(8,128)}, s32[9,136,256]{2,1,0:T(8,128)}, u32[]{:S(2)}, u32[]{:S(2)}) %collective-permute-start.7) | collective-permute-done | bytes 1253408 | tf_op jit(solution)/shard_map/ppermute | solution.py:456
  68.2 0.0 collective-permute-done.6.refs_11_.refs_13_
  68.2 19.2 %relax.2 = (f32[2,3,4,256,256]{4,3,2,1,0:T(8,128)}, f32[4,136,256]{2,1,0:T(8,128)}) custom-call(s32[2]{0:T(128)} %pad_add_fusion.4.refs_0_, f32[8,3]{1,0:T(8,128)} %copy.8.refs_1_, f32[2]{0:T(128)} %add_convert_fusion.refs_2_.refs_1_, s32[2,4,256,256]{3,2,1,0:T(8,128)} %refs_3_.3, s32[4,256,256]{2,1,0:T(8,128)} %refs_4_.3, ...), custom_call_target="tpu_custom_call" | custom-call | flops 40000000 | bytes 40000000 | tf_op jit(solution)/shard_map/relax/pallas_call | solution.py:294
  87.4 0.3 collective-permute-start.8
  87.7 0.6 pad_add_fusion.5.refs_0_
  88.3 0.8 fusion.3
  89.1 0.0 collective-permute-done.4.refs_11_
  89.1 0.0 copy-start.6
  89.1 0.0 collective-permute-done.5.refs_12_
  89.1 0.0 copy-start.7
  89.1 1.0 copy-done.6
  90.1 0.4 copy-done.7
  90.5 0.0 copy-start
  90.5 19.3 %relax.3 = (f32[2,3,4,256,256]{4,3,2,1,0:T(8,128)}, f32[4,136,256]{2,1,0:T(8,128)}) custom-call(s32[2]{0:T(128)} %pad_add_fusion.5.refs_0_, f32[8,3]{1,0:T(8,128)} %copy.8.refs_1_, f32[2]{0:T(128)} %add_convert_fusion.refs_2_.refs_1_, s32[2,4,256,256]{3,2,1,0:T(8,128)} %refs_3_.3, s32[4,256,256]{2,1,0:T(8,128)} %refs_4_.3, ...), custom_call_target="tpu_custom_call", output_to_operand_aliasing={{0}: (15, {})} | custom-call | flops 40000000 | bytes 40000000 | tf_op jit(solution)/shard_map/relax/pallas_call | solution.py:294
  109.8 0.0 copy-start.1
  109.8 0.0 copy-start.2
  109.8 0.0 collective-permute-done.8
  109.8 0.0 copy-done
  109.8 1.3 %fusion.1.refs_3_ = f32[4,136,256]{2,1,0:T(8,128)S(1)} fusion(f32[4,8,256]{2,1,0:T(8,128)S(1)} %get-tuple-element.37, f32[4,128,256]{2,1,0:T(8,128)S(1)} %copy-done, f32[4,8,256]{2,1,0:T(8,128)S(1)} %get-tuple-element.36, f32[4,136,256]{2,1,0:T(8,128)} %get-tuple-element.20, f32[4,136,256]{2,1,0:T(8,128)} %collective-permute-done.8, pred[]{:T(512)S(6)} %eq.3), kind=kLoop, calls=%fused_computation.7 | loop fusion | flops 1114112 | bytes 2260993 | tf_op jit(solution)/shard_map/mul | solution.py:474
  111.2 1.9 %collective-permute-start.10 = (f32[4,136,256]{2,1,0:T(8,128)S(1)}, f32[4,136,256]{2,1,0:T(8,128)S(1)}, u32[]{:S(2)}, u32[]{:S(2)}) collective-permute-start(f32[4,136,256]{2,1,0:T(8,128)S(1)} %fusion.1.refs_3_), channel_id=1, source_target_pairs={{1,0},{2,1},{3,2},{4,3},{5,4},{6,5},{7,6},{8,7},{9,8},{10,9},{11,1... | collective-permute-start | bytes 1671176 | tf_op jit(solution)/shard_map/ppermute | solution.py:456
  113.1 3.6 %collective-permute-start.9 = (f32[4,136,256]{2,1,0:T(8,128)S(1)}, f32[4,136,256]{2,1,0:T(8,128)S(1)}, u32[]{:S(2)}, u32[]{:S(2)}) collective-permute-start(f32[4,136,256]{2,1,0:T(8,128)S(1)} %fusion.1.refs_3_), channel_id=1, source_target_pairs={{0,1},{1,2},{2,3},{3,4},{4,5},{5,6},{6,7},{7,8},{8,9},{9,10},{10,1... | collective-permute-start | bytes 1671176 | tf_op jit(solution)/shard_map/ppermute | solution.py:456
  116.7 11.2 %collective-permute-done.10.refs_4_ = f32[4,136,256]{2,1,0:T(8,128)S(1)} collective-permute-done((f32[4,136,256]{2,1,0:T(8,128)S(1)}, f32[4,136,256]{2,1,0:T(8,128)S(1)}, u32[]{:S(2)}, u32[]{:S(2)}) %collective-permute-start.10) | collective-permute-done | bytes 557088 | tf_op jit(solution)/shard_map/ppermute | solution.py:456
  128.0 0.0 collective-permute-done.9.refs_2_
  128.0 0.0 copy-done.1
  128.0 0.0 copy-done.2
  128.0 5.6 %smooth.1 = f32[4,128,256]{2,1,0:T(8,128)} custom-call(s32[2]{0:T(128)S(1)} %copy-done.2, f32[2]{0:T(128)S(1)} %copy-done.1, f32[4,136,256]{2,1,0:T(8,128)S(1)} %collective-permute-done.9.refs_2_, f32[4,136,256]{2,1,0:T(8,128)S(1)} %fusion.1.refs_3_, f32[4,136,256]{2,1,0:T(8,128)S(1)} %collective-permute-done.10.refs_4_, f32[4,128,256]{2,1,0:T(8,128)S(1)} %copy-done), custom_call_target="tpu_custom_call" | custom-call | flops 5000000 | bytes 5000000 | tf_op jit(solution)/shard_map/smooth/pallas_call | solution.py:417
Async XLA Ops:
  0.6 15.8 %collective-permute-start = (f32[4,128,256]{2,1,0:T(8,128)}, f32[4,128,256]{2,1,0:T(8,128)S(1)}, u32[]{:S(2)}, u32[]{:S(2)}) collective-permute-start(f32[4,128,256]{2,1,0:T(8,128)} %refs_5_.1), channel_id=1, source_target_pairs={{0,1},{1,2},{2,3},{3,4},{4,5},{5,6},{6,7},{7,8},{8,9},{9,10},{10,1... | collective-permute-start | bytes 1572872 | tf_op jit(solution)/shard_map/ppermute | solution.py:443
  4.3 13.9 %collective-permute-start.1 = (f32[4,128,256]{2,1,0:T(8,128)}, f32[4,128,256]{2,1,0:T(8,128)}, u32[]{:S(2)}, u32[]{:S(2)}) collective-permute-start(f32[4,128,256]{2,1,0:T(8,128)} %refs_5_.1), channel_id=1, source_target_pairs={{1,0},{2,1},{3,2},{4,3},{5,4},{6,5},{7,6},{8,7},{9,8},{10,9},{11,1... | collective-permute-start | bytes 1572872 | tf_op jit(solution)/shard_map/ppermute | solution.py:444
  6.3 12.3 %collective-permute-start.2 = (f32[4,128,256]{2,1,0:T(8,128)}, f32[4,128,256]{2,1,0:T(8,128)}, u32[]{:S(2)}, u32[]{:S(2)}) collective-permute-start(f32[4,128,256]{2,1,0:T(8,128)} %refs_5_.1), channel_id=1, source_target_pairs={{0,16},{16,0},{1,17},{17,1},{2,18},{18,2},{3,19},{19,3},{4,20},{20... | collective-permute-start | bytes 1572872 | tf_op jit(solution)/shard_map/ppermute | solution.py:442
  12.6 17.3 %copy-start.4 = (s32[4,256,256]{2,1,0:T(8,128)S(1)}, s32[4,256,256]{2,1,0:T(8,128)}, u32[]{:S(2)}) copy-start(s32[4,256,256]{2,1,0:T(8,128)} %refs_4_.3) | copy-start | bytes 3145732
  16.4 1.9 %copy-start.5 = (f32[4,128,256]{2,1,0:T(8,128)}, f32[4,128,256]{2,1,0:T(8,128)S(1)}, u32[]{:S(2)}) copy-start(f32[4,128,256]{2,1,0:T(8,128)S(1)} %collective-permute-done.refs_8_.refs_5_) | copy-start | bytes 1572868
  18.6 11.4 %copy-start.3 = (s32[2,4,256,256]{3,2,1,0:T(8,128)S(1)}, s32[2,4,256,256]{3,2,1,0:T(8,128)}, u32[]{:S(2)}) copy-start(s32[2,4,256,256]{3,2,1,0:T(8,128)} %refs_3_.3) | copy-start | bytes 6291460
  21.0 22.5 %collective-permute-start.3 = (f32[8,128,256]{2,1,0:T(8,128)}, f32[8,128,256]{2,1,0:T(8,128)}, u32[]{:S(2)}, u32[]{:S(2)}) collective-permute-start(f32[8,128,256]{2,1,0:T(8,128)} %pad_maximum_fusion), channel_id=1, source_target_pairs={{0,16},{16,0},{1,17},{17,1},{2,18},{18,2},{3,19},{19,3},{4,20},{20... | collective-permute-start | bytes 3145736 | tf_op jit(solution)/shard_map/ppermute | solution.py:462
  22.2 46.0 %collective-permute-start.7 = (s32[9,136,256]{2,1,0:T(8,128)}, s32[9,136,256]{2,1,0:T(8,128)}, u32[]{:S(2)}, u32[]{:S(2)}) collective-permute-start(s32[9,136,256]{2,1,0:T(8,128)} %pad_add_fusion.1), channel_id=1, source_target_pairs={{1,0},{2,1},{3,2},{4,3},{5,4},{6,5},{7,6},{8,7},{9,8},{10,9},{11,1... | collective-permute-start | bytes 3760136 | tf_op jit(solution)/shard_map/ppermute | solution.py:456
  26.8 41.4 %collective-permute-start.6 = (s32[9,136,256]{2,1,0:T(8,128)}, s32[9,136,256]{2,1,0:T(8,128)}, u32[]{:S(2)}, u32[]{:S(2)}) collective-permute-start(s32[9,136,256]{2,1,0:T(8,128)} %pad_add_fusion), channel_id=1, source_target_pairs={{0,1},{1,2},{2,3},{3,4},{4,5},{5,6},{6,7},{7,8},{8,9},{9,10},{10,1... | collective-permute-start | bytes 3760136 | tf_op jit(solution)/shard_map/ppermute | solution.py:456
  30.1 22.7 %copy-start.8 = (f32[8,3]{0,1:T(4,128)S(1)}, f32[8,3]{0,1:T(4,128)}, u32[]{:S(2)}) copy-start(f32[8,3]{0,1:T(4,128)} %param.7) | copy-start | bytes 292
  43.5 45.6 %collective-permute-start.4 = (s32[9,120,256]{2,1,0:T(8,128)}, s32[9,120,256]{2,1,0:T(8,128)S(1)}, u32[]{:S(2)}, u32[]{:S(2)}) collective-permute-start(s32[9,120,256]{2,1,0:T(8,128)} %get-tuple-element.16), channel_id=1, source_target_pairs={{0,1},{1,2},{2,3},{3,4},{4,5},{5,6},{6,7},{7,8},{8,9},{9,10},{10,1... | collective-permute-start | bytes 3317768 | tf_op jit(solution)/shard_map/ppermute | solution.py:456
  50.9 38.2 %collective-permute-start.5 = (s32[9,120,256]{2,1,0:T(8,128)S(1)}, s32[9,120,256]{2,1,0:T(8,128)S(1)}, u32[]{:S(2)}, u32[]{:S(2)}) collective-permute-start(s32[9,120,256]{2,1,0:T(8,128)S(1)} %get-tuple-element.17), channel_id=1, source_target_pairs={{1,0},{2,1},{3,2},{4,3},{5,4},{6,5},{7,6},{8,7},{9,8},{10,9},{11,1... | collective-permute-start | bytes 3317768 | tf_op jit(solution)/shard_map/ppermute | solution.py:456
  87.4 22.4 %collective-permute-start.8 = (f32[4,136,256]{2,1,0:T(8,128)}, f32[4,136,256]{2,1,0:T(8,128)}, u32[]{:S(2)}, u32[]{:S(2)}) collective-permute-start(f32[4,136,256]{2,1,0:T(8,128)} %get-tuple-element.21), channel_id=1, source_target_pairs={{0,16},{16,0},{1,17},{17,1},{2,18},{18,2},{3,19},{19,3},{4,20},{20... | collective-permute-start | bytes 1671176 | tf_op jit(solution)/shard_map/ppermute | solution.py:469
  89.1 1.0 copy-start.6
  89.1 1.4 %copy-start.7 = (s32[9,120,256]{2,1,0:T(8,128)}, s32[9,120,256]{2,1,0:T(8,128)S(1)}, u32[]{:S(2)}) copy-start(s32[9,120,256]{2,1,0:T(8,128)S(1)} %collective-permute-done.5.refs_12_) | copy-start | bytes 3317764
  90.5 19.3 %copy-start = (f32[4,128,256]{2,1,0:T(8,128)S(1)}, f32[4,128,256]{2,1,0:T(8,128)}, u32[]{:S(2)}) copy-start(f32[4,128,256]{2,1,0:T(8,128)} %refs_5_.1) | copy-start | bytes 1572868
  109.8 18.2 %copy-start.1 = (f32[2]{0:T(128)S(1)}, f32[2]{0:T(128)}, u32[]{:S(2)}) copy-start(f32[2]{0:T(128)} %add_convert_fusion.refs_2_.refs_1_) | copy-start | bytes 28
  109.8 18.2 %copy-start.2 = (s32[2]{0:T(128)S(1)}, s32[2]{0:T(128)}, u32[]{:S(2)}) copy-start(s32[2]{0:T(128)} %pad_add_fusion.5.refs_0_) | copy-start | bytes 28
  111.2 16.8 %collective-permute-start.10 = (f32[4,136,256]{2,1,0:T(8,128)S(1)}, f32[4,136,256]{2,1,0:T(8,128)S(1)}, u32[]{:S(2)}, u32[]{:S(2)}) collective-permute-start(f32[4,136,256]{2,1,0:T(8,128)S(1)} %fusion.1.refs_3_), channel_id=1, source_target_pairs={{1,0},{2,1},{3,2},{4,3},{5,4},{6,5},{7,6},{8,7},{9,8},{10,9},{11,1... | collective-permute-start | bytes 1671176 | tf_op jit(solution)/shard_map/ppermute | solution.py:456
  113.1 14.9 %collective-permute-start.9 = (f32[4,136,256]{2,1,0:T(8,128)S(1)}, f32[4,136,256]{2,1,0:T(8,128)S(1)}, u32[]{:S(2)}, u32[]{:S(2)}) collective-permute-start(f32[4,136,256]{2,1,0:T(8,128)S(1)} %fusion.1.refs_3_), channel_id=1, source_target_pairs={{0,1},{1,2},{2,3},{3,4},{4,5},{5,6},{6,7},{7,8},{8,9},{9,10},{10,1... | collective-permute-start | bytes 1671176 | tf_op jit(solution)/shard_map/ppermute | solution.py:456

commit v5 on v4

--- a/solution.py
+++ b/solution.py
@@ -37,58 +37,32 @@
     lax.fori_loop(0, tiles, lambda j, c: body(pl.multiple_of(j * 8, 8)), None, unroll=True)
 
 
-def step_kernel(planes, rows, info, table, valid, loads, support, lo_d, mid, hi_d, lo_x, mid_x, hi_x, lo_i, hi_i, *rest):
-    lo_s, hi_s = rest[:2] if len(rest) > 14 else (None, None)
-    (u_out, e_out, d_v, idx_v, sup_v, m_v, k_v, s0_v, s1_v, u_v, in_sem, out_sem) = rest[-12:]
+def over_planes(count, body):
+    def go(p, carry):
+        body(p)
+        return carry
+
+    lax.fori_loop(0, count, go, 0)
+
+
+def step_kernel(planes, rows, info, table, valid, loads, support, lo_d, mid, hi_d, edge_v, lo_i, hi_i, *rest):
+    lo_s, hi_s = rest[:2] if len(rest) > 12 else (None, None)
+    (u_out, e_out, idx_v, sup_v, m_v, k_v, s0_v, s1_v, u_v, in_sem, out_sem) = rest[-11:]
     tiles = rows // 8
     h = info[0]
     vlo, vhi = valid[0], valid[1]
     start = pl.multiple_of(h * info[1], 8)
-    wide = planes + 6
     half = rows - EXTRA
     skip = pl.multiple_of(h * EXTRA, 8)
-
-    def density_copies(j):
-        own, other, at, count = (
-            (lo_d, lo_x, 0, 4), (mid, mid_x, 4, planes), (hi_d, hi_x, planes + 4, 4))[j]
-        edge = pl.ds(pl.multiple_of(h * (half - EXTRA), 8), EXTRA)
-        beyond = pl.ds(pl.multiple_of((1 - h) * half, 8), EXTRA)
-        return [
-            pltpu.make_async_copy(own, d_v.at[pl.ds(at, count), pl.ds(skip, half), :], in_sem.at[2 * j]),
-            pltpu.make_async_copy(other.at[:, edge, :], d_v.at[pl.ds(at, count), beyond, :], in_sem.at[2 * j + 1]),
-        ]
-
-    def halo_copies(j):
-        source, shared, at = ((lo_i, lo_s, 0), (hi_i, hi_s, planes + 3))[j]
-        made = []
-        for part in range(3):
-            goal = (idx_v.at[0], idx_v.at[1], sup_v)[part].at[pl.ds(at, 3)]
-            group = pl.ds(3 * part, 3)
-            sem = 6 + 6 * j + 2 * part
-            if lo_s is None:
-                made.append(pltpu.make_async_copy(source.at[group], goal, in_sem.at[sem]))
-                continue
-            fresh, common = rows - 2 * EXTRA, 2 * EXTRA
-            made.append(pltpu.make_async_copy(
-                source.at[group], goal.at[:, pl.ds(pl.multiple_of(h * common, 8), fresh), :], in_sem.at[sem]))
-            made.append(pltpu.make_async_copy(
-                shared.at[group, pl.ds(pl.multiple_of(h * fresh, 8), common), :],
-                goal.at[:, pl.ds(pl.multiple_of((1 - h) * fresh, 8), common), :], in_sem.at[sem + 1]))
-        return made
-
-    def plane_copies(p):
-        span = pl.ds(start, rows)
-        sem = 18 + 3 * p
-        return [
-            pltpu.make_async_copy(loads.at[0, p, span, :], idx_v.at[0, p + 3], in_sem.at[sem]),
-            pltpu.make_async_copy(loads.at[1, p, span, :], idx_v.at[1, p + 3], in_sem.at[sem + 1]),
-            pltpu.make_async_copy(support.at[p, span, :], sup_v.at[p + 3], in_sem.at[sem + 2]),
-        ]
-
-    copies = density_copies(0) + density_copies(1) + halo_copies(0)
-    for p in range(planes):
-        copies += plane_copies(p)
-    for copy in copies + density_copies(2) + halo_copies(1):
+    fresh, common = rows - 2 * EXTRA, 2 * EXTRA
+
+    span = pl.ds(start, rows)
+    owned = [
+        pltpu.make_async_copy(loads.at[0, :, span, :], idx_v.at[0], in_sem.at[0]),
+        pltpu.make_async_copy(loads.at[1, :, span, :], idx_v.at[1], in_sem.at[1]),
+        pltpu.make_async_copy(support.at[:, span, :], sup_v, in_sem.at[2]),
+    ]
+    for copy in owned:
         copy.start()
 
     zero = jnp.zeros((PAD, 128), jnp.float32)
@@ -121,52 +95,80 @@
     def get(ref, i, row):
         return [ref[i, z, pl.ds(row, 8), :] for z in range(2)]
 
-    def modulus(p):
-        ok = jnp.where(p < 4, vlo, jnp.where(p >= planes + 4, vhi, 1.0))
-
+    def moduli(own, at, count, ok):
+        def plane(p):
+            def put(source, r, row):
+                for z in range(2):
+                    d = source[p, pl.ds(r, 8), pl.ds(128 * z, 128)]
+                    m_v[at + p, z, pl.ds(pl.multiple_of(PAD + row, 8), 8), :] = (E_MIN + d * d * d * (1.0 - E_MIN)) * ok
+
+            def put_edge(p):
+                for z in range(2):
+                    d = edge_v[at + p, :, pl.ds(128 * z, 128)]
+                    m_v[at + p, z, pl.ds(pl.multiple_of(PAD + (1 - h) * half, 8), 8), :] = (E_MIN + d * d * d * (1.0 - E_MIN)) * ok
+
+            over_rows(half // 8, lambda r: put(own, r, skip + r))
+            put_edge(p)
+
+        over_planes(count, plane)
+
+    def first(p, r, ok, index_at, support_at):
+        r = pl.multiple_of(r, 8)
+        row = pl.multiple_of(PAD + r, 8)
+        m = get(m_v, p + 1, row)
+        zup, zdn = above(m), below(m)
+        zup[1] = jnp.where(last_lane, 0.0, zup[1])
+        zdn[0] = jnp.where(first_lane, 0.0, zdn[0])
+        beside = [get(m_v, p + 2, row), get(m_v, p, row), get(m_v, p + 1, row + 1), get(m_v, p + 1, row - 1), zup, zdn]
+        stores = []
+        for z in range(2):
+            face = [m[z] + b[z] for b in beside]
+            double = ((face[0] + face[1]) + (face[2] + face[3])) + (face[4] + face[5])
+            diagonal = 0.5 * double + SPRING * support_at(z).astype(jnp.float32)
+            w = ok / (diagonal + (1.0 - ok))
+            wb = w * (0.5 * B1)
+            weight = [f * wb for f in face]
+            if z == 1:
+                weight[4] = jnp.where(last_lane, 0.0, weight[4])
+            else:
+                weight[5] = jnp.where(first_lane, 0.0, weight[5])
+            scale = w * (RATIO / CENTRE)
+            for case in range(2):
+                index = index_at(case, z)
+                b0, b1, b2 = (index & 1) != 0, (index & 2) != 0, (index & 4) != 0
+                forces = []
+                for c in range(3):
+                    q = [jnp.where(b0, table[2 * j + 1, c], table[2 * j, c]) for j in range(4)]
+                    forces.append(jnp.where(b2, jnp.where(b1, q[3], q[2]), jnp.where(b1, q[1], q[0])))
+                for c in range(3):
+                    stores.append((s0_v, (p * 6 + case * 3 + c, z, pl.ds(row, 8)), forces[c] * scale))
+            for j in range(6):
+                stores.append((k_v, (p, j, z, pl.ds(r, 8)), weight[j]))
+        for ref, at, value in stores:
+            ref[at] = value
+
+    def first_halo(source, side, at, ok):
+        def from_source(p, ref, r, row):
+            def cut(i, z):
+                return ref[i, pl.ds(pl.multiple_of(r, 8), 8), pl.ds(128 * z, 128)]
+
+            first(at + p, row, ok, lambda case, z: cut(3 * case + p, z), lambda z: cut(6 + p, z))
+
+        def plane(p):
+            if lo_s is None:
+                over_rows(tiles, lambda r: from_source(p, source, r, r))
+            else:
+                over_rows(fresh // 8, lambda r: from_source(p, source, r, h * common + r))
+                over_rows(common // 8, lambda r: from_source(p, (lo_s, hi_s)[side], r, (1 - h) * fresh + r))
+
+        over_planes(3, plane)
+
+    def first_own(p):
         def body(r):
-            for z in range(2):
-                d = d_v[p, pl.ds(r, 8), pl.ds(128 * z, 128)]
-                m_v[p, z, pl.ds(PAD + r, 8), :] = (E_MIN + d * d * d * (1.0 - E_MIN)) * ok
-
-        over_rows(tiles, body)
-
-    def first(p):
-        ok = jnp.where(p < 3, vlo, jnp.where(p >= planes + 3, vhi, 1.0))
-
-        def body(r):
-            row = PAD + r
-            m = get(m_v, p + 1, row)
-            zup, zdn = above(m), below(m)
-            zup[1] = jnp.where(last_lane, 0.0, zup[1])
-            zdn[0] = jnp.where(first_lane, 0.0, zdn[0])
-            beside = [get(m_v, p + 2, row), get(m_v, p, row), get(m_v, p + 1, row + 1), get(m_v, p + 1, row - 1), zup, zdn]
-            stores = []
-            for z in range(2):
-                face = [m[z] + b[z] for b in beside]
-                double = ((face[0] + face[1]) + (face[2] + face[3])) + (face[4] + face[5])
-                diagonal = 0.5 * double + SPRING * sup_v[p, pl.ds(r, 8), pl.ds(128 * z, 128)].astype(jnp.float32)
-                w = ok / (diagonal + (1.0 - ok))
-                wb = w * (0.5 * B1)
-                weight = [f * wb for f in face]
-                if z == 1:
-                    weight[4] = jnp.where(last_lane, 0.0, weight[4])
-                else:
-                    weight[5] = jnp.where(first_lane, 0.0, weight[5])
-                scale = w * (RATIO / CENTRE)
-                for case in range(2):
-                    index = idx_v[case, p, pl.ds(r, 8), pl.ds(128 * z, 128)]
-                    b0, b1, b2 = (index & 1) != 0, (index & 2) != 0, (index & 4) != 0
-                    forces = []
-                    for c in range(3):
-                        q = [jnp.where(b0, table[2 * j + 1, c], table[2 * j, c]) for j in range(4)]
-                        forces.append(jnp.where(b2, jnp.where(b1, q[3], q[2]), jnp.where(b1, q[1], q[0])))
-                    for c in range(3):
-                        stores.append((s0_v, (p * 6 + case * 3 + c, z, pl.ds(row, 8)), forces[c] * scale))
-                for j in range(6):
-                    stores.append((k_v, (p, j, z, pl.ds(r, 8)), weight[j]))
-            for ref, at, value in stores:
-                ref[at] = value
+            first(
+                p + 3, r, 1.0,
+                lambda case, z: idx_v[case, p, pl.ds(r, 8), pl.ds(128 * z, 128)],
+                lambda z: sup_v[p, pl.ds(r, 8), pl.ds(128 * z, 128)])
 
         over_rows(tiles, body)
 
@@ -239,39 +241,26 @@
 
         over_rows(tiles, body)
 
-    for copy in density_copies(0) + density_copies(1):
+    moduli(lo_d, 0, 4, vlo)
+    moduli(mid, 4, planes, 1.0)
+    moduli(hi_d, planes + 4, 4, vhi)
+    first_halo(lo_i, 0, 0, vlo)
+    first_halo(hi_i, 1, planes + 3, vhi)
+    for copy in owned:
         copy.wait()
-    modulus(0)
-    modulus(1)
-
-    def each(count, body):
-        def go(p, carry):
-            body(p)
-            return carry
-
-        lax.fori_loop(0, count, go, 0)
-
-    for copy in density_copies(2):
-        copy.wait()
-    each(planes + 6, lambda p: modulus(p + 2))
-    for copy in halo_copies(0) + halo_copies(1):
-        copy.wait()
-    for p in range(planes):
-        for copy in plane_copies(p):
-            copy.wait()
-    each(planes + 6, first)
-    each(planes + 4, second)
-    each(planes + 2, third)
+    over_planes(planes, first_own)
+    over_planes(planes + 4, second)
+    over_planes(planes + 2, third)
     for p in range(planes):
         for copy in out_copies(p):
             copy.start()
-    each(planes, energy)
+    over_planes(planes, energy)
     for p in range(planes):
         for copy in out_copies(p):
             copy.wait()
 
 
-def step(h, gap, valid, table, loads, support, main, other, ints, u):
+def step(h, gap, valid, table, loads, support, main, edge, ints, u):
     planes, half, cols = main[1].shape
     rows = half + EXTRA
     tiles_rows = rows + 2 * PAD
@@ -280,8 +269,8 @@
     smem = pl.BlockSpec(memory_space=pltpu.SMEM)
     vmem = pl.BlockSpec(memory_space=pltpu.VMEM)
     full = loads.shape[2]
-    args = [jnp.stack([h, gap]).astype(jnp.int32), table, valid, loads, support, *main, *other, *ints]
-    specs = [smem, smem, smem] + [any_spec] * (len(args) - 3)
+    args = [jnp.stack([h, gap]).astype(jnp.int32), table, valid, loads, support, *main, edge, *ints]
+    specs = [smem] * 3 + [pl.BlockSpec(memory_space=pltpu.HBM)] * 2 + [vmem] * (len(args) - 5)
     aliases = {}
     if u is not None:
         args.append(u)
@@ -298,18 +287,17 @@
         out_specs=(any_spec, vmem),
         input_output_aliases=aliases,
         scratch_shapes=[
-            pltpu.VMEM((planes + 8, rows, cols), f32),
-            pltpu.VMEM((2, planes + 6, rows, cols), jnp.int32),
-            pltpu.VMEM((planes + 6, rows, cols), jnp.int32),
+            pltpu.VMEM((2, planes, rows, cols), jnp.int32),
+            pltpu.VMEM((planes, rows, cols), jnp.int32),
             pltpu.VMEM((planes + 8, 2, tiles_rows, 128), f32),
             pltpu.VMEM((planes + 6, 6, 2, rows, 128), f32),
             pltpu.VMEM((6 * (planes + 6), 2, tiles_rows, 128), f32),
             pltpu.VMEM((6 * (planes + 4), 2, tiles_rows, 128), f32),
             pltpu.VMEM((6 * (planes + 2), 2, tiles_rows, 128), f32),
-            pltpu.SemaphoreType.DMA((18 + 3 * planes,)),
+            pltpu.SemaphoreType.DMA((3,)),
             pltpu.SemaphoreType.DMA((12 * planes,)),
         ],
-        compiler_params=pltpu.CompilerParams(vmem_limit_bytes=56 * 1024 * 1024),
+        compiler_params=pltpu.CompilerParams(vmem_limit_bytes=42 * 1024 * 1024),
         cost_estimate=pl.CostEstimate(flops=40_000_000, bytes_accessed=40_000_000, transcendentals=0),
         name="relax",
     )(*args)
@@ -462,12 +450,17 @@
     both = lax.ppermute(jnp.concatenate([lo_c, hi_c]), "case", swap)
     both, payload_b = lax.optimization_barrier((both, payload_b))
     lo_o, hi_o = both[:4], both[4:]
-    ints_b = exchange(*payload_b) + ints_a
+    common = [lax.dynamic_slice_in_dim(v, mine * (rows - 2 * EXTRA), 2 * EXTRA, axis=1) for v in ints_a]
+    ints_b = (*exchange(*payload_b), *common)
     own = (lo_c, density, hi_c)
     opposite = (lo_o, partner, hi_o)
-    u, e_a = step(1 - mine, gap, valid, load_table, loads, support, opposite, own, ints_a, None)
+
+    def edge(h, parts):
+        return jnp.concatenate([lax.dynamic_slice_in_dim(v, h * (half - EXTRA), EXTRA, axis=1) for v in parts])
+
+    u, e_a = step(1 - mine, gap, valid, load_table, loads, support, opposite, edge(1 - mine, own), ints_a, None)
     received = lax.ppermute(e_a, "case", swap)
-    u, e_b = step(mine, gap, valid, load_table, loads, support, own, opposite, ints_b, u)
+    u, e_b = step(mine, gap, valid, load_table, loads, support, own, edge(mine, opposite), ints_b, u)
     low = jnp.concatenate([density, partner[:, :EXTRA]], axis=1)
     high = jnp.concatenate([partner[:, half - EXTRA:], density], axis=1)
     mid = jnp.where(mine == 0, low, high)

time: 134 us -> 126 us (0.940)
  starting transfers between devices: 30.9 us -> 25.4 us
  waiting for transfers between devices: 40.6 us -> 45.7 us
  Pallas kernels: 44 us -> 39.1 us
  other arithmetic: 9.16 us -> 5.3 us
    ppermute x6, starting transfers between devices: 22.5 us -> 16.7 us  [exchange(): return (lax.ppermute(up, 'slab', rise), lax.ppermute(down, 'slab', fall))]
    pallas_call x2, Pallas kernels: 38.4 us -> 33.5 us  [step(): pl.pallas_call(kernel, out_shape=(jax.ShapeDtypeStruct((2, 3, planes, ful...]
    ppermute x1, waiting for transfers between devices: 3.79 us -> 0.01 us  [local(): lo_c = lax.ppermute(density[planes - 4:], 'slab', rise)]
    dynamic_slice x0 -> x6, local copies, waits for them, and re-layouts: none -> 3.4 us  [the longest x2 1.85 us: local(): lax.dynamic_slice_in_dim(v, mine * (rows - 2 * EXTRA), 2 * EXTRA, axis=1)]
    ppermute x6, waiting for transfers between devices: 22.4 us -> 25.7 us  [exchange(): return (lax.ppermute(up, 'slab', rise), lax.ppermute(down, 'slab', fall))]
    ppermute x1, waiting for transfers between devices: 1.86 us -> 4.77 us  [local(): hi_c = lax.ppermute(density[:4], 'slab', fall)]
    ppermute x1, waiting for transfers between devices: 12.2 us -> 14.3 us  [local(): both = lax.ppermute(jnp.concatenate([lo_c, hi_c]), 'case', swap)]
  transfers between devices with their start and end apart: 11 -> 11, of which waited for: 6 -> 5; matrix products, arithmetic and copies ran while one was open for 9% -> 8% of each run, Pallas kernels for 29% -> 27%
where the time goes in v5:
time: 126 us
  waiting for transfers between devices  45.7 us (36%)
  Pallas kernels  39.1 us (31%)
  starting transfers between devices  25.4 us (20%)
  local copies, waits for them, and re-layouts  9.33 us (7%)
  other arithmetic  5.3 us (4%)
    pallas_call x2, Pallas kernels, step(): pl.pallas_call(kernel, out_shape=(jax.ShapeDtypeStruct((2, 3, planes, ful...  33.5 us
    ppermute x6, waiting for transfers between devices, exchange(): return (lax.ppermute(up, 'slab', rise), lax.ppermute(down, 'slab', fall))  25.7 us
    ppermute x6, starting transfers between devices, exchange(): return (lax.ppermute(up, 'slab', rise), lax.ppermute(down, 'slab', fall))  16.7 us
    ppermute x1, waiting for transfers between devices, local(): both = lax.ppermute(jnp.concatenate([lo_c, hi_c]), 'case', swap)  14.3 us
    pallas_call x1, Pallas kernels, smooth(): pl.pallas_call(kernel, out_shape=jax.ShapeDtypeStruct(dens.shape, f32), i...  5.55 us
    ppermute x1, waiting for transfers between devices, local(): hi_c = lax.ppermute(density[:4], 'slab', fall)  4.77 us
    ppermute x1, starting transfers between devices, local(): lo_c = lax.ppermute(density[planes - 4:], 'slab', rise)  3.05 us
    ppermute x1, starting transfers between devices, local(): hi_c = lax.ppermute(density[:4], 'slab', fall)  2.85 us
  transfers between devices with their start and end apart: 11, of which 5 were waited for; matrix products, arithmetic and copies ran while one was open for 8% of the time, Pallas kernels for 27%

profile of v5, /device:TPU:9, one launch (start us, length us, event | category | flops | bytes accessed | tf_op | source)
XLA Modules:
  0.0 125.8 jit_solution(16137097225551196794)
XLA Ops:
  0.6 1.3 %collective-permute-start.2 = (f32[4,128,256]{2,1,0:T(8,128)}, f32[4,128,256]{2,1,0:T(8,128)S(1)}, u32[]{:S(2)}, u32[]{:S(2)}) collective-permute-start(f32[4,128,256]{2,1,0:T(8,128)} %refs_5_.1), channel_id=1, source_target_pairs={{0,16},{16,0},{1,17},{17,1},{2,18},{18,2},{3,19},{19,3},{4,20},{20... | collective-permute-start | bytes 1572872 | tf_op jit(solution)/shard_map/ppermute | solution.py:430
  1.9 2.9 %collective-permute-start.1 = (f32[4,128,256]{2,1,0:T(8,128)}, f32[4,128,256]{2,1,0:T(8,128)S(1)}, u32[]{:S(2)}, u32[]{:S(2)}) collective-permute-start(f32[4,128,256]{2,1,0:T(8,128)} %refs_5_.1), channel_id=1, source_target_pairs={{1,0},{2,1},{3,2},{4,3},{5,4},{6,5},{7,6},{8,7},{9,8},{10,9},{11,1... | collective-permute-start | bytes 1572872 | tf_op jit(solution)/shard_map/ppermute | solution.py:432
  4.8 3.0 %collective-permute-start = (f32[4,128,256]{2,1,0:T(8,128)}, f32[4,128,256]{2,1,0:T(8,128)}, u32[]{:S(2)}, u32[]{:S(2)}) collective-permute-start(f32[4,128,256]{2,1,0:T(8,128)} %refs_5_.1), channel_id=1, source_target_pairs={{0,1},{1,2},{2,3},{3,4},{4,5},{5,6},{6,7},{7,8},{8,9},{9,10},{10,1... | collective-permute-start | bytes 1572872 | tf_op jit(solution)/shard_map/ppermute | solution.py:431
  7.8 1.2 constant_dynamic-slice_fusion.11
  9.0 1.5 %dynamic-slice_bitcast_fusion.1 = (s32[3,136,256]{2,1,0:T(8,128)S(1)}, s32[3,136,256]{2,1,0:T(8,128)S(1)}, s32[3,136,256]{2,1,0:T(8,128)S(1)}, s32[3,136,256]{2,1,0:T(8,128)S(1)}) fusion(s32[2,4,256,256]{3,2,1,0:T(8,128)} %refs_3_.3, s32[]{:T(128)S(6)} %select_n.30, s32[]{:T(128)S(6)} %add.42), kind=kLoop, calls=%fused_computation.10 | loop fusion | bytes 3342344 | tf_op jit(solution)/shard_map/squeeze | solution.py:439
  10.6 1.2 pad_add_fusion.1
  11.7 1.1 pad_add_fusion
  12.9 0.0 copy-start.7
  12.9 0.0 copy-start.1
  12.9 0.9 collective-permute-done.2.refs_6_
  13.8 0.0 copy-start.5
  13.8 4.8 %collective-permute-done.1.refs_7_ = f32[4,128,256]{2,1,0:T(8,128)S(1)} collective-permute-done((f32[4,128,256]{2,1,0:T(8,128)}, f32[4,128,256]{2,1,0:T(8,128)S(1)}, u32[]{:S(2)}, u32[]{:S(2)}) %collective-permute-start.1) | collective-permute-done | bytes 524320 | tf_op jit(solution)/shard_map/ppermute | solution.py:432
  18.6 0.0 copy-done.5
  18.6 0.0 copy-start.3
  18.6 0.8 copy-done.3
  19.4 0.0 collective-permute-done.refs_5_
  19.4 0.0 copy-start
  19.4 2.4 %pad_maximum_fusion = f32[8,128,256]{2,1,0:T(8,128)} fusion(f32[4,128,256]{2,1,0:T(8,128)} %copy-done.3, f32[4,128,256]{2,1,0:T(8,128)} %collective-permute-done.refs_5_), kind=kLoop, calls=%fused_computation.4 | loop fusion | flops 262144 | bytes 2097152 | tf_op jit(solution)/shard_map/concatenate | solution.py:450
  21.8 0.3 collective-permute-start.3
  22.1 3.8 %collective-permute-start.6 = (s32[9,136,256]{2,1,0:T(8,128)}, s32[9,136,256]{2,1,0:T(8,128)}, u32[]{:S(2)}, u32[]{:S(2)}) collective-permute-start(s32[9,136,256]{2,1,0:T(8,128)} %pad_add_fusion), channel_id=1, source_target_pairs={{0,1},{1,2},{2,3},{3,4},{4,5},{5,6},{6,7},{7,8},{8,9},{9,10},{10,1... | collective-permute-start | bytes 3760136 | tf_op jit(solution)/shard_map/ppermute | solution.py:444
  25.9 1.9 %collective-permute-start.7 = (s32[9,136,256]{2,1,0:T(8,128)}, s32[9,136,256]{2,1,0:T(8,128)}, u32[]{:S(2)}, u32[]{:S(2)}) collective-permute-start(s32[9,136,256]{2,1,0:T(8,128)} %pad_add_fusion.1), channel_id=1, source_target_pairs={{1,0},{2,1},{3,2},{4,3},{5,4},{6,5},{7,6},{8,7},{9,8},{10,9},{11,1... | collective-permute-start | bytes 3760136 | tf_op jit(solution)/shard_map/ppermute | solution.py:444
  27.9 0.0 copy-done.7
  27.9 0.1 copy.8.refs_1_
  27.9 0.1 pad_add_fusion.5.refs_0_
  28.0 0.1 pad_add_fusion.4.refs_0_
  28.1 0.8 constant_dynamic-slice_fusion.3
  28.9 0.1 add_convert_fusion.refs_2_.refs_1_
  28.9 0.0 copy-done.1
  29.0 0.0 copy-done
  29.0 0.1 dynamic-slice_bitcast_fusion.5
  29.1 0.0 copy-start.4
  29.1 0.0 copy-start.6
  29.1 0.2 pad_add_fusion.2
  29.3 0.8 copy-done.4
  30.2 0.8 constant_dynamic-slice_fusion.2
  30.9 14.3 %collective-permute-done.3 = f32[8,128,256]{2,1,0:T(8,128)} collective-permute-done((f32[8,128,256]{2,1,0:T(8,128)}, f32[8,128,256]{2,1,0:T(8,128)}, u32[]{:S(2)}, u32[]{:S(2)}) %collective-permute-start.3) | collective-permute-done | bytes 1048608 | tf_op jit(solution)/shard_map/ppermute | solution.py:450
  45.2 1.9 %collective-permute-start.4 = (s32[9,120,256]{2,1,0:T(8,128)S(1)}, s32[9,120,256]{2,1,0:T(8,128)S(1)}, u32[]{:S(2)}, u32[]{:S(2)}) collective-permute-start(s32[9,120,256]{2,1,0:T(8,128)S(1)} %get-tuple-element.16), channel_id=1, source_target_pairs={{0,1},{1,2},{2,3},{3,4},{4,5},{5,6},{6,7},{7,8},{8,9},{9,10},{10,1... | collective-permute-start | bytes 3317768 | tf_op jit(solution)/shard_map/ppermute | solution.py:444
  47.2 2.4 %collective-permute-start.5 = (s32[9,120,256]{2,1,0:T(8,128)S(1)}, s32[9,120,256]{2,1,0:T(8,128)S(1)}, u32[]{:S(2)}, u32[]{:S(2)}) collective-permute-start(s32[9,120,256]{2,1,0:T(8,128)S(1)} %get-tuple-element.17), channel_id=1, source_target_pairs={{1,0},{2,1},{3,2},{4,3},{5,4},{6,5},{7,6},{8,7},{9,8},{10,9},{11,1... | collective-permute-start | bytes 3317768 | tf_op jit(solution)/shard_map/ppermute | solution.py:444
  49.6 0.0 copy-done.6
  49.6 1.3 %fusion.2 = (f32[4,128,256]{2,1,0:T(8,128)S(1)}, f32[4,128,256]{2,1,0:T(8,128)S(1)}) fusion(f32[8,128,256]{2,1,0:T(8,128)} %collective-permute-done.3), kind=kLoop, calls=%fused_computation.34 | loop fusion | bytes 2097152 | tf_op jit(solution)/shard_map/slice | solution.py:452
  50.9 14.5 %collective-permute-done.6.refs_9_ = s32[9,136,256]{2,1,0:T(8,128)} collective-permute-done((s32[9,136,256]{2,1,0:T(8,128)}, s32[9,136,256]{2,1,0:T(8,128)}, u32[]{:S(2)}, u32[]{:S(2)}) %collective-permute-start.6) | collective-permute-done | bytes 1253408 | tf_op jit(solution)/shard_map/ppermute | solution.py:444
  65.4 0.0 collective-permute-done.7.refs_10_
  65.4 17.1 %relax.2 = (f32[2,3,4,256,256]{4,3,2,1,0:T(8,128)}, f32[4,136,256]{2,1,0:T(8,128)S(1)}) custom-call(s32[2]{0:T(128)S(1)} %pad_add_fusion.4.refs_0_, f32[8,3]{1,0:T(8,128)S(1)} %copy.8.refs_1_, f32[2]{0:T(128)S(1)} %add_convert_fusion.refs_2_.refs_1_, s32[2,4,256,256]{3,2,1,0:T(8,128)S(1)} %copy-done, s32[4,256,256]{2,1,0:T(8,128)S(1)} %copy-done.1, ...), custom_call_target="tpu_custom_call" | custom-call | flops 40000000 | bytes 40000000 | tf_op jit(solution)/shard_map/relax/pallas_call | solution.py:283
  82.5 0.0 copy-start.2
  82.5 1.3 %collective-permute-start.8 = (f32[4,136,256]{2,1,0:T(8,128)S(1)}, f32[4,136,256]{2,1,0:T(8,128)S(1)}, u32[]{:S(2)}, u32[]{:S(2)}) collective-permute-start(f32[4,136,256]{2,1,0:T(8,128)S(1)} %get-tuple-element.21), channel_id=1, source_target_pairs={{0,16},{16,0},{1,17},{17,1},{2,18},{18,2},{3,19},{19,3},{4,20},{20... | collective-permute-start | bytes 1671176 | tf_op jit(solution)/shard_map/ppermute | solution.py:462
  83.8 0.9 constant_dynamic-slice_fusion.6.refs_11_
  84.7 0.9 constant_dynamic-slice_fusion.5.refs_12_
  85.7 0.0 collective-permute-done.4.refs_9_
  85.7 0.0 collective-permute-done.5.refs_10_
  85.7 0.0 copy-done.2
  85.7 16.5 %relax.3 = (f32[2,3,4,256,256]{4,3,2,1,0:T(8,128)}, f32[4,136,256]{2,1,0:T(8,128)S(1)}) custom-call(s32[2]{0:T(128)S(1)} %pad_add_fusion.5.refs_0_, f32[8,3]{1,0:T(8,128)S(1)} %copy.8.refs_1_, f32[2]{0:T(128)S(1)} %add_convert_fusion.refs_2_.refs_1_, s32[2,4,256,256]{3,2,1,0:T(8,128)S(1)} %copy-done, ...), custom_call_target="tpu_custom_call", output_to_operand_aliasing={{0}: (13, {})} | custom-call | flops 40000000 | bytes 40000000 | tf_op jit(solution)/shard_map/relax/pallas_call | solution.py:283
  102.2 0.0 collective-permute-done.8
  102.2 0.1 fusion.1.refs_3_
  102.4 1.9 %collective-permute-start.10 = (f32[4,136,256]{2,1,0:T(8,128)S(1)}, f32[4,136,256]{2,1,0:T(8,128)S(1)}, u32[]{:S(2)}, u32[]{:S(2)}) collective-permute-start(f32[4,136,256]{2,1,0:T(8,128)S(1)} %fusion.1.refs_3_), channel_id=1, source_target_pairs={{1,0},{2,1},{3,2},{4,3},{5,4},{6,5},{7,6},{8,7},{9,8},{10,9},{11,1... | collective-permute-start | bytes 1671176 | tf_op jit(solution)/shard_map/ppermute | solution.py:444
  104.3 4.7 %collective-permute-start.9 = (f32[4,136,256]{2,1,0:T(8,128)S(1)}, f32[4,136,256]{2,1,0:T(8,128)S(1)}, u32[]{:S(2)}, u32[]{:S(2)}) collective-permute-start(f32[4,136,256]{2,1,0:T(8,128)S(1)} %fusion.1.refs_3_), channel_id=1, source_target_pairs={{0,1},{1,2},{2,3},{3,4},{4,5},{5,6},{6,7},{7,8},{8,9},{9,10},{10,1... | collective-permute-start | bytes 1671176 | tf_op jit(solution)/shard_map/ppermute | solution.py:444
  109.0 11.2 %collective-permute-done.10.refs_4_ = f32[4,136,256]{2,1,0:T(8,128)S(1)} collective-permute-done((f32[4,136,256]{2,1,0:T(8,128)S(1)}, f32[4,136,256]{2,1,0:T(8,128)S(1)}, u32[]{:S(2)}, u32[]{:S(2)}) %collective-permute-start.10) | collective-permute-done | bytes 557088 | tf_op jit(solution)/shard_map/ppermute | solution.py:444
  120.2 0.0 collective-permute-done.9.refs_2_
  120.2 5.6 %smooth.1 = f32[4,128,256]{2,1,0:T(8,128)} custom-call(s32[2]{0:T(128)S(1)} %pad_add_fusion.5.refs_0_, f32[2]{0:T(128)S(1)} %add_convert_fusion.refs_2_.refs_1_, f32[4,136,256]{2,1,0:T(8,128)S(1)} %collective-permute-done.9.refs_2_, f32[4,136,256]{2,1,0:T(8,128)S(1)} %fusion.1.refs_3_, f32[4,136,256]{2,1,0:T(8,128)S(1)} %collective-permute-done.10.refs_4_, ...), custom_call_target="tpu_custom_call" | custom-call | flops 5000000 | bytes 5000000 | tf_op jit(solution)/shard_map/smooth/pallas_call | solution.py:405
  (6 shorter events, 0.1 us)
Async XLA Ops:
  0.6 13.2 %collective-permute-start.2 = (f32[4,128,256]{2,1,0:T(8,128)}, f32[4,128,256]{2,1,0:T(8,128)S(1)}, u32[]{:S(2)}, u32[]{:S(2)}) collective-permute-start(f32[4,128,256]{2,1,0:T(8,128)} %refs_5_.1), channel_id=1, source_target_pairs={{0,16},{16,0},{1,17},{17,1},{2,18},{18,2},{3,19},{19,3},{4,20},{20... | collective-permute-start | bytes 1572872 | tf_op jit(solution)/shard_map/ppermute | solution.py:430
  1.9 16.7 %collective-permute-start.1 = (f32[4,128,256]{2,1,0:T(8,128)}, f32[4,128,256]{2,1,0:T(8,128)S(1)}, u32[]{:S(2)}, u32[]{:S(2)}) collective-permute-start(f32[4,128,256]{2,1,0:T(8,128)} %refs_5_.1), channel_id=1, source_target_pairs={{1,0},{2,1},{3,2},{4,3},{5,4},{6,5},{7,6},{8,7},{9,8},{10,9},{11,1... | collective-permute-start | bytes 1572872 | tf_op jit(solution)/shard_map/ppermute | solution.py:432
  4.8 14.6 %collective-permute-start = (f32[4,128,256]{2,1,0:T(8,128)}, f32[4,128,256]{2,1,0:T(8,128)}, u32[]{:S(2)}, u32[]{:S(2)}) collective-permute-start(f32[4,128,256]{2,1,0:T(8,128)} %refs_5_.1), channel_id=1, source_target_pairs={{0,1},{1,2},{2,3},{3,4},{4,5},{5,6},{6,7},{7,8},{8,9},{9,10},{10,1... | collective-permute-start | bytes 1572872 | tf_op jit(solution)/shard_map/ppermute | solution.py:431
  12.9 15.0 %copy-start.7 = (f32[8,3]{0,1:T(4,128)S(1)}, f32[8,3]{0,1:T(4,128)}, u32[]{:S(2)}) copy-start(f32[8,3]{0,1:T(4,128)} %param.7) | copy-start | bytes 292
  12.9 16.0 %copy-start.1 = (s32[4,256,256]{2,1,0:T(8,128)S(1)}, s32[4,256,256]{2,1,0:T(8,128)}, u32[]{:S(2)}) copy-start(s32[4,256,256]{2,1,0:T(8,128)} %refs_4_.3) | copy-start | bytes 3145732
  13.8 4.8 %copy-start.5 = (f32[4,128,256]{2,1,0:T(8,128)}, f32[4,128,256]{2,1,0:T(8,128)S(1)}, u32[]{:S(2)}) copy-start(f32[4,128,256]{2,1,0:T(8,128)S(1)} %collective-permute-done.2.refs_6_) | copy-start | bytes 1572868
  18.6 0.8 copy-start.3
  19.4 9.6 %copy-start = (s32[2,4,256,256]{3,2,1,0:T(8,128)S(1)}, s32[2,4,256,256]{3,2,1,0:T(8,128)}, u32[]{:S(2)}) copy-start(s32[2,4,256,256]{3,2,1,0:T(8,128)} %refs_3_.3) | copy-start | bytes 6291460
  21.8 23.4 %collective-permute-start.3 = (f32[8,128,256]{2,1,0:T(8,128)}, f32[8,128,256]{2,1,0:T(8,128)}, u32[]{:S(2)}, u32[]{:S(2)}) collective-permute-start(f32[8,128,256]{2,1,0:T(8,128)} %pad_maximum_fusion), channel_id=1, source_target_pairs={{0,16},{16,0},{1,17},{17,1},{2,18},{18,2},{3,19},{19,3},{4,20},{20... | collective-permute-start | bytes 3145736 | tf_op jit(solution)/shard_map/ppermute | solution.py:450
  22.1 43.4 %collective-permute-start.6 = (s32[9,136,256]{2,1,0:T(8,128)}, s32[9,136,256]{2,1,0:T(8,128)}, u32[]{:S(2)}, u32[]{:S(2)}) collective-permute-start(s32[9,136,256]{2,1,0:T(8,128)} %pad_add_fusion), channel_id=1, source_target_pairs={{0,1},{1,2},{2,3},{3,4},{4,5},{5,6},{6,7},{7,8},{8,9},{9,10},{10,1... | collective-permute-start | bytes 3760136 | tf_op jit(solution)/shard_map/ppermute | solution.py:444
  25.9 39.5 %collective-permute-start.7 = (s32[9,136,256]{2,1,0:T(8,128)}, s32[9,136,256]{2,1,0:T(8,128)}, u32[]{:S(2)}, u32[]{:S(2)}) collective-permute-start(s32[9,136,256]{2,1,0:T(8,128)} %pad_add_fusion.1), channel_id=1, source_target_pairs={{1,0},{2,1},{3,2},{4,3},{5,4},{6,5},{7,6},{8,7},{9,8},{10,9},{11,1... | collective-permute-start | bytes 3760136 | tf_op jit(solution)/shard_map/ppermute | solution.py:444
  29.1 1.0 copy-start.4
  29.1 20.5 %copy-start.6 = (f32[4,128,256]{2,1,0:T(8,128)S(1)}, f32[4,128,256]{2,1,0:T(8,128)}, u32[]{:S(2)}) copy-start(f32[4,128,256]{2,1,0:T(8,128)} %copy-done.5) | copy-start | bytes 1572868
  45.2 40.5 %collective-permute-start.4 = (s32[9,120,256]{2,1,0:T(8,128)S(1)}, s32[9,120,256]{2,1,0:T(8,128)S(1)}, u32[]{:S(2)}, u32[]{:S(2)}) collective-permute-start(s32[9,120,256]{2,1,0:T(8,128)S(1)} %get-tuple-element.16), channel_id=1, source_target_pairs={{0,1},{1,2},{2,3},{3,4},{4,5},{5,6},{6,7},{7,8},{8,9},{9,10},{10,1... | collective-permute-start | bytes 3317768 | tf_op jit(solution)/shard_map/ppermute | solution.py:444
  47.2 38.6 %collective-permute-start.5 = (s32[9,120,256]{2,1,0:T(8,128)S(1)}, s32[9,120,256]{2,1,0:T(8,128)S(1)}, u32[]{:S(2)}, u32[]{:S(2)}) collective-permute-start(s32[9,120,256]{2,1,0:T(8,128)S(1)} %get-tuple-element.17), channel_id=1, source_target_pairs={{1,0},{2,1},{3,2},{4,3},{5,4},{6,5},{7,6},{8,7},{9,8},{10,9},{11,1... | collective-permute-start | bytes 3317768 | tf_op jit(solution)/shard_map/ppermute | solution.py:444
  82.5 3.2 %copy-start.2 = (f32[4,128,256]{2,1,0:T(8,128)S(1)}, f32[4,128,256]{2,1,0:T(8,128)}, u32[]{:S(2)}) copy-start(f32[4,128,256]{2,1,0:T(8,128)} %refs_5_.1) | copy-start | bytes 1572868
  82.5 19.7 %collective-permute-start.8 = (f32[4,136,256]{2,1,0:T(8,128)S(1)}, f32[4,136,256]{2,1,0:T(8,128)S(1)}, u32[]{:S(2)}, u32[]{:S(2)}) collective-permute-start(f32[4,136,256]{2,1,0:T(8,128)S(1)} %get-tuple-element.21), channel_id=1, source_target_pairs={{0,16},{16,0},{1,17},{17,1},{2,18},{18,2},{3,19},{19,3},{4,20},{20... | collective-permute-start | bytes 1671176 | tf_op jit(solution)/shard_map/ppermute | solution.py:462
  102.4 17.8 %collective-permute-start.10 = (f32[4,136,256]{2,1,0:T(8,128)S(1)}, f32[4,136,256]{2,1,0:T(8,128)S(1)}, u32[]{:S(2)}, u32[]{:S(2)}) collective-permute-start(f32[4,136,256]{2,1,0:T(8,128)S(1)} %fusion.1.refs_3_), channel_id=1, source_target_pairs={{1,0},{2,1},{3,2},{4,3},{5,4},{6,5},{7,6},{8,7},{9,8},{10,9},{11,1... | collective-permute-start | bytes 1671176 | tf_op jit(solution)/shard_map/ppermute | solution.py:444
  104.3 15.9 %collective-permute-start.9 = (f32[4,136,256]{2,1,0:T(8,128)S(1)}, f32[4,136,256]{2,1,0:T(8,128)S(1)}, u32[]{:S(2)}, u32[]{:S(2)}) collective-permute-start(f32[4,136,256]{2,1,0:T(8,128)S(1)} %fusion.1.refs_3_), channel_id=1, source_target_pairs={{0,1},{1,2},{2,3},{3,4},{4,5},{5,6},{6,7},{7,8},{8,9},{9,10},{10,1... | collective-permute-start | bytes 1671176 | tf_op jit(solution)/shard_map/ppermute | solution.py:444

commit v6 on v5

--- a/solution.py
+++ b/solution.py
@@ -46,7 +46,7 @@
 
 
 def step_kernel(planes, rows, info, table, valid, loads, support, lo_d, mid, hi_d, edge_v, lo_i, hi_i, *rest):
-    lo_s, hi_s = rest[:2] if len(rest) > 12 else (None, None)
+    lo_s, hi_s, lo_l, hi_l = rest[:4] if len(rest) > 12 else (None,) * 4
     (u_out, e_out, idx_v, sup_v, m_v, k_v, s0_v, s1_v, u_v, in_sem, out_sem) = rest[-11:]
     tiles = rows // 8
     h = info[0]
@@ -148,18 +148,19 @@
             ref[at] = value
 
     def first_halo(source, side, at, ok):
-        def from_source(p, ref, r, row):
+        def from_source(p, refs, r, row):
             def cut(i, z):
-                return ref[i, pl.ds(pl.multiple_of(r, 8), 8), pl.ds(128 * z, 128)]
+                at = (i, pl.ds(pl.multiple_of(r, 8), 8), pl.ds(128 * z, 128))
+                return refs[0][at] if len(refs) == 1 else refs[0][at] + refs[1][at]
 
             first(at + p, row, ok, lambda case, z: cut(3 * case + p, z), lambda z: cut(6 + p, z))
 
         def plane(p):
             if lo_s is None:
-                over_rows(tiles, lambda r: from_source(p, source, r, r))
+                over_rows(tiles, lambda r: from_source(p, (source,), r, r))
             else:
-                over_rows(fresh // 8, lambda r: from_source(p, source, r, h * common + r))
-                over_rows(common // 8, lambda r: from_source(p, (lo_s, hi_s)[side], r, (1 - h) * fresh + r))
+                over_rows(fresh // 8, lambda r: from_source(p, (source, (lo_l, hi_l)[side]), r, h * common + r))
+                over_rows(common // 8, lambda r: from_source(p, ((lo_s, hi_s)[side],), r, (1 - h) * fresh + r))
 
         over_planes(3, plane)
 
@@ -440,8 +441,11 @@
 
         return pack(planes - 3, planes), pack(0, 3)
 
-    def exchange(up, down):
-        return lax.ppermute(up, "slab", rise), lax.ppermute(down, "slab", fall)
+    def exchange(up, down, keep=lambda i: True):
+        return (
+            lax.ppermute(up, "slab", [pair for pair in rise if keep(pair[1])]),
+            lax.ppermute(down, "slab", [pair for pair in fall if keep(pair[0])]),
+        )
 
     payload_a = packed((1 - mine) * gap, rows)
     payload_b = packed(mine * rows, rows - 2 * EXTRA)
@@ -451,7 +455,9 @@
     both, payload_b = lax.optimization_barrier((both, payload_b))
     lo_o, hi_o = both[:4], both[4:]
     common = [lax.dynamic_slice_in_dim(v, mine * (rows - 2 * EXTRA), 2 * EXTRA, axis=1) for v in ints_a]
-    ints_b = (*exchange(*payload_b), *common)
+    ints_b = (*exchange(*payload_b, lambda i: i % 4), *common)
+    ints_a, late = lax.optimization_barrier((ints_a, payload_b))
+    ints_b += exchange(*late, lambda i: i % 4 == 0)
     own = (lo_c, density, hi_c)
     opposite = (lo_o, partner, hi_o)
 

time: 126 us -> 121 us (0.960)
  waiting for transfers between devices: 45.7 us -> 41.4 us
  starting transfers between devices: 25.4 us -> 23.7 us
    ppermute x1, waiting for transfers between devices: 4.77 us -> 15 us  [local(): hi_c = lax.ppermute(density[:4], 'slab', fall)]
    ppermute x6 -> x8, waiting for transfers between devices: 25.7 us -> 15.7 us  [the longest x4 15.6 us: exchange(): lax.ppermute(down, 'slab', [pair for pair in fall if keep(pair[0])])]
    ppermute x1, waiting for transfers between devices: 14.3 us -> 10.6 us  [local(): both = lax.ppermute(jnp.concatenate([lo_c, hi_c]), 'case', swap)]
    ppermute x6 -> x8, starting transfers between devices: 16.7 us -> 16 us  [the longest x4 9.13 us: exchange(): lax.ppermute(up, 'slab', [pair for pair in rise if keep(pair[1])])]
  transfers between devices with their start and end apart: 11 -> 13, of which waited for: 5 -> 5; matrix products, arithmetic and copies ran while one was open for 8% -> 11% of each run, Pallas kernels for 27% -> 28%
where the time goes in v6:
time: 121 us; the launch traced here: 120 us
  waiting for transfers between devices  41.4 us (34%)
  Pallas kernels  39.2 us (32%)
  starting transfers between devices  23.7 us (20%)
  local copies, waits for them, and re-layouts  9.36 us (8%)
  other arithmetic  5.27 us (4%)
    pallas_call x2, Pallas kernels, step(): pl.pallas_call(kernel, out_shape=(jax.ShapeDtypeStruct((2, 3, planes, ful...  33.7 us
    ppermute x4, waiting for transfers between devices, exchange(): lax.ppermute(down, 'slab', [pair for pair in fall if keep(pair[0])])  15.6 us
    ppermute x1, waiting for transfers between devices, local(): hi_c = lax.ppermute(density[:4], 'slab', fall)  15 us
    ppermute x1, waiting for transfers between devices, local(): both = lax.ppermute(jnp.concatenate([lo_c, hi_c]), 'case', swap)  10.6 us
    ppermute x4, starting transfers between devices, exchange(): lax.ppermute(up, 'slab', [pair for pair in rise if keep(pair[1])])  9.13 us
    ppermute x4, starting transfers between devices, exchange(): lax.ppermute(down, 'slab', [pair for pair in fall if keep(pair[0])])  6.85 us
    pallas_call x1, Pallas kernels, smooth(): pl.pallas_call(kernel, out_shape=jax.ShapeDtypeStruct(dens.shape, f32), i...  5.55 us
    ppermute x1, starting transfers between devices, local(): lo_c = lax.ppermute(density[planes - 4:], 'slab', rise)  3.05 us
  transfers between devices with their start and end apart: 13, of which 5 were waited for; matrix products, arithmetic and copies ran while one was open for 11% of the time, Pallas kernels for 28%

profile of v6, /device:TPU:9, one launch (start us, length us, event | category | flops | bytes accessed | tf_op | source)
XLA Modules:
  0.0 119.9 jit_solution(1104125993616219893)
XLA Ops:
  0.6 1.3 %collective-permute-start.2 = (f32[4,128,256]{2,1,0:T(8,128)}, f32[4,128,256]{2,1,0:T(8,128)S(1)}, u32[]{:S(2)}, u32[]{:S(2)}) collective-permute-start(f32[4,128,256]{2,1,0:T(8,128)} %refs_5_.1), channel_id=1, source_target_pairs={{0,16},{16,0},{1,17},{17,1},{2,18},{18,2},{3,19},{19,3},{4,20},{20... | collective-permute-start | bytes 1572872 | tf_op jit(solution)/shard_map/ppermute | solution.py:431
  1.9 2.9 %collective-permute-start.1 = (f32[4,128,256]{2,1,0:T(8,128)}, f32[4,128,256]{2,1,0:T(8,128)S(1)}, u32[]{:S(2)}, u32[]{:S(2)}) collective-permute-start(f32[4,128,256]{2,1,0:T(8,128)} %refs_5_.1), channel_id=1, source_target_pairs={{1,0},{2,1},{3,2},{4,3},{5,4},{6,5},{7,6},{8,7},{9,8},{10,9},{11,1... | collective-permute-start | bytes 1572872 | tf_op jit(solution)/shard_map/ppermute | solution.py:433
  4.8 3.0 %collective-permute-start = (f32[4,128,256]{2,1,0:T(8,128)}, f32[4,128,256]{2,1,0:T(8,128)}, u32[]{:S(2)}, u32[]{:S(2)}) collective-permute-start(f32[4,128,256]{2,1,0:T(8,128)} %refs_5_.1), channel_id=1, source_target_pairs={{0,1},{1,2},{2,3},{3,4},{4,5},{5,6},{6,7},{7,8},{8,9},{9,10},{10,1... | collective-permute-start | bytes 1572872 | tf_op jit(solution)/shard_map/ppermute | solution.py:432
  7.8 1.2 constant_dynamic-slice_fusion.11
  9.0 1.5 %dynamic-slice_bitcast_fusion.1 = (s32[3,136,256]{2,1,0:T(8,128)S(1)}, s32[3,136,256]{2,1,0:T(8,128)S(1)}, s32[3,136,256]{2,1,0:T(8,128)S(1)}, s32[3,136,256]{2,1,0:T(8,128)S(1)}) fusion(s32[2,4,256,256]{3,2,1,0:T(8,128)} %refs_3_.3, s32[]{:T(128)S(6)} %select_n.30, s32[]{:T(128)S(6)} %add.42), kind=kLoop, calls=%fused_computation.10 | loop fusion | bytes 3342344 | tf_op jit(solution)/shard_map/squeeze | solution.py:440
  10.6 1.2 pad_add_fusion
  11.7 2.4 %collective-permute-start.6 = (s32[9,136,256]{2,1,0:T(8,128)}, s32[9,136,256]{2,1,0:T(8,128)}, u32[]{:S(2)}, u32[]{:S(2)}) collective-permute-start(s32[9,136,256]{2,1,0:T(8,128)} %pad_add_fusion), channel_id=1, source_target_pairs={{0,1},{1,2},{2,3},{3,4},{4,5},{5,6},{6,7},{7,8},{8,9},{9,10},{10,1... | collective-permute-start | bytes 3760136 | tf_op jit(solution)/shard_map/ppermute | solution.py:446
  14.1 1.2 pad_add_fusion.1
  15.3 0.0 copy-start.7
  15.3 0.0 copy-start.1
  15.3 2.0 %collective-permute-start.7 = (s32[9,136,256]{2,1,0:T(8,128)}, s32[9,136,256]{2,1,0:T(8,128)}, u32[]{:S(2)}, u32[]{:S(2)}) collective-permute-start(s32[9,136,256]{2,1,0:T(8,128)} %pad_add_fusion.1), channel_id=1, source_target_pairs={{1,0},{2,1},{3,2},{4,3},{5,4},{6,5},{7,6},{8,7},{9,8},{10,9},{11,1... | collective-permute-start | bytes 3760136 | tf_op jit(solution)/shard_map/ppermute | solution.py:447
  17.3 0.0 collective-permute-done.2.refs_6_
  17.4 0.0 copy-start.5
  17.4 15.0 %collective-permute-done.1.refs_7_ = f32[4,128,256]{2,1,0:T(8,128)S(1)} collective-permute-done((f32[4,128,256]{2,1,0:T(8,128)}, f32[4,128,256]{2,1,0:T(8,128)S(1)}, u32[]{:S(2)}, u32[]{:S(2)}) %collective-permute-start.1) | collective-permute-done | bytes 524320 | tf_op jit(solution)/shard_map/ppermute | solution.py:433
  32.4 0.0 copy-done.5
  32.4 0.0 copy-start.3
  32.4 0.8 copy-done.3
  33.2 0.0 collective-permute-done.refs_5_
  33.2 0.0 copy-start
  33.2 2.4 %pad_maximum_fusion = f32[8,128,256]{2,1,0:T(8,128)} fusion(f32[4,128,256]{2,1,0:T(8,128)} %copy-done.3, f32[4,128,256]{2,1,0:T(8,128)} %collective-permute-done.refs_5_), kind=kLoop, calls=%fused_computation.4 | loop fusion | flops 262144 | bytes 2097152 | tf_op jit(solution)/shard_map/concatenate | solution.py:454
  35.6 0.3 collective-permute-start.3
  35.9 0.0 copy-done.7
  35.9 0.1 copy.8.refs_1_
  36.0 0.1 pad_add_fusion.5.refs_0_
  36.0 0.1 pad_add_fusion.4.refs_0_
  36.1 0.1 add_convert_fusion.refs_2_.refs_1_
  36.2 0.8 constant_dynamic-slice_fusion.3
  37.0 0.0 copy-done.1
  37.0 0.1 constant_dynamic-slice_fusion.10
  37.0 0.0 copy-done
  37.0 0.1 dynamic-slice_bitcast_fusion.5
  37.2 0.0 copy-start.4
  37.2 0.0 copy-start.6
  37.2 0.2 pad_add_fusion.2
  37.4 0.8 copy-done.4
  38.2 0.8 constant_dynamic-slice_fusion.2
  39.0 10.6 %collective-permute-done.3 = f32[8,128,256]{2,1,0:T(8,128)} collective-permute-done((f32[8,128,256]{2,1,0:T(8,128)}, f32[8,128,256]{2,1,0:T(8,128)}, u32[]{:S(2)}, u32[]{:S(2)}) %collective-permute-start.3) | collective-permute-done | bytes 1048608 | tf_op jit(solution)/shard_map/ppermute | solution.py:454
  49.6 2.6 %collective-permute-start.4 = (s32[9,120,256]{2,1,0:T(8,128)S(1)}, s32[9,120,256]{2,1,0:T(8,128)S(1)}, u32[]{:S(2)}, u32[]{:S(2)}) collective-permute-start(s32[9,120,256]{2,1,0:T(8,128)S(1)} %get-tuple-element.22), channel_id=1, source_target_pairs={{0,1},{1,2},{2,3},{4,5},{5,6},{6,7},{8,9},{9,10},{10,11},{12,13},{... | collective-permute-start | bytes 3317768 | tf_op jit(solution)/shard_map/ppermute | solution.py:446
  52.2 1.9 %collective-permute-start.5 = (s32[9,120,256]{2,1,0:T(8,128)S(1)}, s32[9,120,256]{2,1,0:T(8,128)S(1)}, u32[]{:S(2)}, u32[]{:S(2)}) collective-permute-start(s32[9,120,256]{2,1,0:T(8,128)S(1)} %get-tuple-element.23), channel_id=1, source_target_pairs={{1,0},{2,1},{3,2},{5,4},{6,5},{7,6},{9,8},{10,9},{11,10},{13,12},{... | collective-permute-start | bytes 3317768 | tf_op jit(solution)/shard_map/ppermute | solution.py:447
  54.1 0.0 collective-permute-done.6.refs_9_
  54.1 0.0 collective-permute-done.7.refs_10_
  54.1 0.7 collective-permute-start.8
  54.9 0.7 collective-permute-start.9
  55.6 0.0 copy-done.6
  55.7 1.3 %fusion.2 = (f32[4,128,256]{2,1,0:T(8,128)S(1)}, f32[4,128,256]{2,1,0:T(8,128)S(1)}) fusion(f32[8,128,256]{2,1,0:T(8,128)} %collective-permute-done.3), kind=kLoop, calls=%fused_computation.34 | loop fusion | bytes 2097152 | tf_op jit(solution)/shard_map/slice | solution.py:456
  57.0 17.1 %relax.2 = (f32[2,3,4,256,256]{4,3,2,1,0:T(8,128)}, f32[4,136,256]{2,1,0:T(8,128)S(1)}) custom-call(s32[2]{0:T(128)S(1)} %pad_add_fusion.4.refs_0_, f32[8,3]{1,0:T(8,128)S(1)} %copy.8.refs_1_, f32[2]{0:T(128)S(1)} %add_convert_fusion.refs_2_.refs_1_, s32[2,4,256,256]{3,2,1,0:T(8,128)S(1)} %copy-done, s32[4,256,256]{2,1,0:T(8,128)S(1)} %copy-done.1, ...), custom_call_target="tpu_custom_call" | custom-call | flops 40000000 | bytes 40000000 | tf_op jit(solution)/shard_map/relax/pallas_call | solution.py:284
  74.1 0.0 copy-start.2
  74.1 0.3 collective-permute-start.10
  74.4 0.9 constant_dynamic-slice_fusion.6.refs_11_
  75.3 0.9 constant_dynamic-slice_fusion.5.refs_12_
  76.3 0.1 collective-permute-done.4.refs_9_
  76.4 4.4 %collective-permute-done.5.refs_10_ = s32[9,120,256]{2,1,0:T(8,128)S(1)} collective-permute-done((s32[9,120,256]{2,1,0:T(8,128)S(1)}, s32[9,120,256]{2,1,0:T(8,128)S(1)}, u32[]{:S(2)}, u32[]{:S(2)}) %collective-permute-start.5) | collective-permute-done | bytes 1105952 | tf_op jit(solution)/shard_map/ppermute | solution.py:447
  80.8 0.0 collective-permute-done.8.refs_13_
  80.8 0.0 collective-permute-done.9.refs_14_
  80.8 0.0 copy-done.2
  80.8 16.6 %relax.3 = (f32[2,3,4,256,256]{4,3,2,1,0:T(8,128)}, f32[4,136,256]{2,1,0:T(8,128)S(1)}) custom-call(s32[2]{0:T(128)S(1)} %pad_add_fusion.5.refs_0_, f32[8,3]{1,0:T(8,128)S(1)} %copy.8.refs_1_, f32[2]{0:T(128)S(1)} %add_convert_fusion.refs_2_.refs_1_, s32[2,4,256,256]{3,2,1,0:T(8,128)S(1)} %copy-done, ...), custom_call_target="tpu_custom_call", output_to_operand_aliasing={{0}: (15, {})} | custom-call | flops 40000000 | bytes 40000000 | tf_op jit(solution)/shard_map/relax/pallas_call | solution.py:284
  97.4 0.0 collective-permute-done.10
  97.4 0.1 fusion.1.refs_3_
  97.5 2.2 %collective-permute-start.12 = (f32[4,136,256]{2,1,0:T(8,128)S(1)}, f32[4,136,256]{2,1,0:T(8,128)S(1)}, u32[]{:S(2)}, u32[]{:S(2)}) collective-permute-start(f32[4,136,256]{2,1,0:T(8,128)S(1)} %fusion.1.refs_3_), channel_id=1, source_target_pairs={{1,0},{2,1},{3,2},{4,3},{5,4},{6,5},{7,6},{8,7},{9,8},{10,9},{11,1... | collective-permute-start | bytes 1671176 | tf_op jit(solution)/shard_map/ppermute | solution.py:447
  99.7 3.4 %collective-permute-start.11 = (f32[4,136,256]{2,1,0:T(8,128)S(1)}, f32[4,136,256]{2,1,0:T(8,128)S(1)}, u32[]{:S(2)}, u32[]{:S(2)}) collective-permute-start(f32[4,136,256]{2,1,0:T(8,128)S(1)} %fusion.1.refs_3_), channel_id=1, source_target_pairs={{0,1},{1,2},{2,3},{3,4},{4,5},{5,6},{6,7},{7,8},{8,9},{9,10},{10,1... | collective-permute-start | bytes 1671176 | tf_op jit(solution)/shard_map/ppermute | solution.py:446
  103.1 11.2 %collective-permute-done.12.refs_4_ = f32[4,136,256]{2,1,0:T(8,128)S(1)} collective-permute-done((f32[4,136,256]{2,1,0:T(8,128)S(1)}, f32[4,136,256]{2,1,0:T(8,128)S(1)}, u32[]{:S(2)}, u32[]{:S(2)}) %collective-permute-start.12) | collective-permute-done | bytes 557088 | tf_op jit(solution)/shard_map/ppermute | solution.py:447
  114.3 0.0 collective-permute-done.11.refs_2_
  114.4 5.6 %smooth.1 = f32[4,128,256]{2,1,0:T(8,128)} custom-call(s32[2]{0:T(128)S(1)} %pad_add_fusion.5.refs_0_, f32[2]{0:T(128)S(1)} %add_convert_fusion.refs_2_.refs_1_, f32[4,136,256]{2,1,0:T(8,128)S(1)} %collective-permute-done.11.refs_2_, f32[4,136,256]{2,1,0:T(8,128)S(1)} %fusion.1.refs_3_, f32[4,136,256]{2,1,0:T(8,128)S(1)} %collective-permute-done.12.refs_4_, ...), custom_call_target="tpu_custom_call" | custom-call | flops 5000000 | bytes 5000000 | tf_op jit(solution)/shard_map/smooth/pallas_call | solution.py:406
  (5 shorter events, 0.1 us)
Async XLA Ops:
  0.6 16.7 %collective-permute-start.2 = (f32[4,128,256]{2,1,0:T(8,128)}, f32[4,128,256]{2,1,0:T(8,128)S(1)}, u32[]{:S(2)}, u32[]{:S(2)}) collective-permute-start(f32[4,128,256]{2,1,0:T(8,128)} %refs_5_.1), channel_id=1, source_target_pairs={{0,16},{16,0},{1,17},{17,1},{2,18},{18,2},{3,19},{19,3},{4,20},{20... | collective-permute-start | bytes 1572872 | tf_op jit(solution)/shard_map/ppermute | solution.py:431
  1.9 30.5 %collective-permute-start.1 = (f32[4,128,256]{2,1,0:T(8,128)}, f32[4,128,256]{2,1,0:T(8,128)S(1)}, u32[]{:S(2)}, u32[]{:S(2)}) collective-permute-start(f32[4,128,256]{2,1,0:T(8,128)} %refs_5_.1), channel_id=1, source_target_pairs={{1,0},{2,1},{3,2},{4,3},{5,4},{6,5},{7,6},{8,7},{9,8},{10,9},{11,1... | collective-permute-start | bytes 1572872 | tf_op jit(solution)/shard_map/ppermute | solution.py:433
  4.8 28.4 %collective-permute-start = (f32[4,128,256]{2,1,0:T(8,128)}, f32[4,128,256]{2,1,0:T(8,128)}, u32[]{:S(2)}, u32[]{:S(2)}) collective-permute-start(f32[4,128,256]{2,1,0:T(8,128)} %refs_5_.1), channel_id=1, source_target_pairs={{0,1},{1,2},{2,3},{3,4},{4,5},{5,6},{6,7},{7,8},{8,9},{9,10},{10,1... | collective-permute-start | bytes 1572872 | tf_op jit(solution)/shard_map/ppermute | solution.py:432
  11.7 42.4 %collective-permute-start.6 = (s32[9,136,256]{2,1,0:T(8,128)}, s32[9,136,256]{2,1,0:T(8,128)}, u32[]{:S(2)}, u32[]{:S(2)}) collective-permute-start(s32[9,136,256]{2,1,0:T(8,128)} %pad_add_fusion), channel_id=1, source_target_pairs={{0,1},{1,2},{2,3},{3,4},{4,5},{5,6},{6,7},{7,8},{8,9},{9,10},{10,1... | collective-permute-start | bytes 3760136 | tf_op jit(solution)/shard_map/ppermute | solution.py:446
  15.3 20.6 %copy-start.7 = (f32[8,3]{0,1:T(4,128)S(1)}, f32[8,3]{0,1:T(4,128)}, u32[]{:S(2)}) copy-start(f32[8,3]{0,1:T(4,128)} %param.7) | copy-start | bytes 292
  15.3 21.7 %copy-start.1 = (s32[4,256,256]{2,1,0:T(8,128)S(1)}, s32[4,256,256]{2,1,0:T(8,128)}, u32[]{:S(2)}) copy-start(s32[4,256,256]{2,1,0:T(8,128)} %refs_4_.3) | copy-start | bytes 3145732
  15.3 38.8 %collective-permute-start.7 = (s32[9,136,256]{2,1,0:T(8,128)}, s32[9,136,256]{2,1,0:T(8,128)}, u32[]{:S(2)}, u32[]{:S(2)}) collective-permute-start(s32[9,136,256]{2,1,0:T(8,128)} %pad_add_fusion.1), channel_id=1, source_target_pairs={{1,0},{2,1},{3,2},{4,3},{5,4},{6,5},{7,6},{8,7},{9,8},{10,9},{11,1... | collective-permute-start | bytes 3760136 | tf_op jit(solution)/shard_map/ppermute | solution.py:447
  17.4 15.1 %copy-start.5 = (f32[4,128,256]{2,1,0:T(8,128)}, f32[4,128,256]{2,1,0:T(8,128)S(1)}, u32[]{:S(2)}) copy-start(f32[4,128,256]{2,1,0:T(8,128)S(1)} %collective-permute-done.2.refs_6_) | copy-start | bytes 1572868
  32.4 0.8 copy-start.3
  33.2 3.8 %copy-start = (s32[2,4,256,256]{3,2,1,0:T(8,128)S(1)}, s32[2,4,256,256]{3,2,1,0:T(8,128)}, u32[]{:S(2)}) copy-start(s32[2,4,256,256]{3,2,1,0:T(8,128)} %refs_3_.3) | copy-start | bytes 6291460
  35.6 14.0 %collective-permute-start.3 = (f32[8,128,256]{2,1,0:T(8,128)}, f32[8,128,256]{2,1,0:T(8,128)}, u32[]{:S(2)}, u32[]{:S(2)}) collective-permute-start(f32[8,128,256]{2,1,0:T(8,128)} %pad_maximum_fusion), channel_id=1, source_target_pairs={{0,16},{16,0},{1,17},{17,1},{2,18},{18,2},{3,19},{19,3},{4,20},{20... | collective-permute-start | bytes 3145736 | tf_op jit(solution)/shard_map/ppermute | solution.py:454
  37.2 1.0 copy-start.4
  37.2 18.5 %copy-start.6 = (f32[4,128,256]{2,1,0:T(8,128)S(1)}, f32[4,128,256]{2,1,0:T(8,128)}, u32[]{:S(2)}) copy-start(f32[4,128,256]{2,1,0:T(8,128)} %copy-done.5) | copy-start | bytes 1572868
  49.6 26.8 %collective-permute-start.4 = (s32[9,120,256]{2,1,0:T(8,128)S(1)}, s32[9,120,256]{2,1,0:T(8,128)S(1)}, u32[]{:S(2)}, u32[]{:S(2)}) collective-permute-start(s32[9,120,256]{2,1,0:T(8,128)S(1)} %get-tuple-element.22), channel_id=1, source_target_pairs={{0,1},{1,2},{2,3},{4,5},{5,6},{6,7},{8,9},{9,10},{10,11},{12,13},{... | collective-permute-start | bytes 3317768 | tf_op jit(solution)/shard_map/ppermute | solution.py:446
  52.2 28.6 %collective-permute-start.5 = (s32[9,120,256]{2,1,0:T(8,128)S(1)}, s32[9,120,256]{2,1,0:T(8,128)S(1)}, u32[]{:S(2)}, u32[]{:S(2)}) collective-permute-start(s32[9,120,256]{2,1,0:T(8,128)S(1)} %get-tuple-element.23), channel_id=1, source_target_pairs={{1,0},{2,1},{3,2},{5,4},{6,5},{7,6},{9,8},{10,9},{11,10},{13,12},{... | collective-permute-start | bytes 3317768 | tf_op jit(solution)/shard_map/ppermute | solution.py:447
  54.1 26.6 %collective-permute-start.8 = (s32[9,120,256]{2,1,0:T(8,128)S(1)}, s32[9,120,256]{2,1,0:T(8,128)S(1)}, u32[]{:S(2)}, u32[]{:S(2)}) collective-permute-start(s32[9,120,256]{2,1,0:T(8,128)S(1)} %get-tuple-element.22), channel_id=1, source_target_pairs={{3,4},{7,8},{11,12},{19,20},{23,24},{27,28}} | collective-permute-start | bytes 3317768 | tf_op jit(solution)/shard_map/ppermute | solution.py:446
  54.9 25.9 %collective-permute-start.9 = (s32[9,120,256]{2,1,0:T(8,128)S(1)}, s32[9,120,256]{2,1,0:T(8,128)S(1)}, u32[]{:S(2)}, u32[]{:S(2)}) collective-permute-start(s32[9,120,256]{2,1,0:T(8,128)S(1)} %get-tuple-element.23), channel_id=1, source_target_pairs={{4,3},{8,7},{12,11},{20,19},{24,23},{28,27}} | collective-permute-start | bytes 3317768 | tf_op jit(solution)/shard_map/ppermute | solution.py:447
  74.1 6.7 %copy-start.2 = (f32[4,128,256]{2,1,0:T(8,128)S(1)}, f32[4,128,256]{2,1,0:T(8,128)}, u32[]{:S(2)}) copy-start(f32[4,128,256]{2,1,0:T(8,128)} %refs_5_.1) | copy-start | bytes 1572868
  74.1 23.3 %collective-permute-start.10 = (f32[4,136,256]{2,1,0:T(8,128)S(1)}, f32[4,136,256]{2,1,0:T(8,128)S(1)}, u32[]{:S(2)}, u32[]{:S(2)}) collective-permute-start(f32[4,136,256]{2,1,0:T(8,128)S(1)} %get-tuple-element.29), channel_id=1, source_target_pairs={{0,16},{16,0},{1,17},{17,1},{2,18},{18,2},{3,19},{19,3},{4,20},{20... | collective-permute-start | bytes 1671176 | tf_op jit(solution)/shard_map/ppermute | solution.py:468
  97.5 16.8 %collective-permute-start.12 = (f32[4,136,256]{2,1,0:T(8,128)S(1)}, f32[4,136,256]{2,1,0:T(8,128)S(1)}, u32[]{:S(2)}, u32[]{:S(2)}) collective-permute-start(f32[4,136,256]{2,1,0:T(8,128)S(1)} %fusion.1.refs_3_), channel_id=1, source_target_pairs={{1,0},{2,1},{3,2},{4,3},{5,4},{6,5},{7,6},{8,7},{9,8},{10,9},{11,1... | collective-permute-start | bytes 1671176 | tf_op jit(solution)/shard_map/ppermute | solution.py:447
  99.7 14.7 %collective-permute-start.11 = (f32[4,136,256]{2,1,0:T(8,128)S(1)}, f32[4,136,256]{2,1,0:T(8,128)S(1)}, u32[]{:S(2)}, u32[]{:S(2)}) collective-permute-start(f32[4,136,256]{2,1,0:T(8,128)S(1)} %fusion.1.refs_3_), channel_id=1, source_target_pairs={{0,1},{1,2},{2,3},{3,4},{4,5},{5,6},{6,7},{7,8},{8,9},{9,10},{10,1... | collective-permute-start | bytes 1671176 | tf_op jit(solution)/shard_map/ppermute | solution.py:446
